TPU v7x, 32 devices: a whole 2x2x4 slice. The times are simulated.
32 devices in a mesh: space: 8 (over y, x, core), chan: 4 (over z).
Axes of the slice: x: 2, y: 2, z: 4, core: 2. Of those that a mesh axis runs over, the one named last changes fastest.
Arguments:
- features: bfloat16 [64, 128, 512], P('space'), may hold values from -6 to 6
- voxel_mask: int32 [64, 512], P('space'), may hold values 0 or 1
- neighbors: int32 [64, 26], P('space'), may hold values from -1 to 15, as said below
- w_conv: bfloat16 [27, 128, 128], P(None, 'chan'), may hold values from -0.109375 to 0.109375
- w_down: bfloat16 [8, 256, 128], replicated, may hold values from -0.1875 to 0.1875
- coarse_owner: int32 [64, 1], P('space'), may hold values from 0 to 7; in each aligned block of 8 rows (0 to 7, 8 to 15, ...) at most 2 rows name the same one
- cotangent: bfloat16 [128, 256, 64], P('space', 'chan'), may hold values from -0.5 to 0.5
Outputs:
- coarse: bfloat16 [128, 256, 64], P('space', 'chan')
- grad_conv: float32 [27, 128, 128], P(None, 'chan')
- grad_down: float32 [8, 256, 128], P(None, 'chan')
Inputs may be any that keep to these rules, and one draw needn't show every extreme that they name: `neighbors`: blocks 0 to 3 of a device lie in the first x-layer of its slab and the others in the second; slabs follow each other along x in device order, and block positions in a layer lie on a 8 x 8 grid in y and z. An entry is the neighbor's slot on the own device (below 8), 8 + i for slot 4 + i of the previous device, 12 + i for slot i of the next device, or -1 where the position is empty. `coarse_owner`: among the 8 blocks of one device at most 2 name the same owner.
All inputs are finite; a program needn't handle non-finite values. No bound on the sum of `voxel_mask` on one device may be relied on, other than what follows from the above.
Results may differ from a plain program's by a relative error of at most 0.001.
The roundings to bfloat16 on the way count: a program that leaves them out, or rounds other values in their place, can miss the bound.
Values may be sent and summed in bfloat16 or wider, within the bound.
No kernel may reach another device: no remote copies, remote signals or barrier semaphores. Data moves between devices by JAX's collectives and lax.ppermute only.
A program may use at most 128 MiB of HBM per device.

v0:
```python
import jax
import jax.numpy as jnp
from jax import lax
from jax.sharding import PartitionSpec as P

OFFSETS = [
    (step_x, step_y, step_z)
    for step_x in (-1, 0, 1)
    for step_y in (-1, 0, 1)
    for step_z in (-1, 0, 1)
]
CENTER = 13


def extended_2(cells, sides, width):
    for axis, dim in sides:
        count = lax.axis_size(axis)
        ends = count - 1
        head = lax.slice_in_dim(cells, 0, width, axis=dim)
        tail = lax.slice_in_dim(cells, cells.shape[dim] - width, cells.shape[dim], axis=dim)
        cells = jnp.concatenate(
            [
                lax.ppermute(tail, axis, [(i, (i + 1) % count) for i in range(ends)]),
                cells,
                lax.ppermute(head, axis, [((i + 1) % count, i) for i in range(ends)]),
            ],
            axis=dim,
        )
    return cells


def block_faces(blocks):
    block_count, channels = (blocks.shape[0], blocks.shape[1])
    cube_grid = blocks.reshape(block_count, channels, 8, 8, 8)
    face_list = [
        cube_grid[:, :, 0],
        cube_grid[:, :, 7],
        cube_grid[:, :, :, 0],
        cube_grid[:, :, :, 7],
        cube_grid[:, :, :, :, 0],
        cube_grid[:, :, :, :, 7],
    ]
    return jnp.stack(
        [one_face.reshape(block_count, channels, 64) for one_face in face_list], axis=1
    )


def neighbor_piece(lookup_rows, neighbor_ids, offset, slot_count):
    lead_axis = [which_axis for which_axis in range(3) if offset[which_axis] != 0][0]
    face_index = 2 * lead_axis + (1 if offset[lead_axis] < 0 else 0)
    row_index = jnp.where(
        neighbor_ids < 0,
        7 * slot_count,
        jnp.where(
            neighbor_ids < slot_count, 6 * neighbor_ids + face_index, 5 * slot_count + neighbor_ids
        ),
    )
    picked = jnp.take(lookup_rows, row_index, axis=0)
    picked = picked.reshape(picked.shape[0], picked.shape[1], 8, 8)
    other_axes = [which_axis for which_axis in range(3) if which_axis != lead_axis]
    for position_dim, which_axis in enumerate(other_axes):
        if offset[which_axis] == 1:
            picked = lax.slice_in_dim(picked, 0, 1, axis=2 + position_dim)
        elif offset[which_axis] == -1:
            picked = lax.slice_in_dim(picked, 7, 8, axis=2 + position_dim)
    return jnp.expand_dims(picked, 2 + lead_axis)


def padded_blocks(lookup_rows, neighbors, own_blocks, slot_total):
    block_count, channels = (own_blocks.shape[0], own_blocks.shape[1])
    cube_grid = own_blocks.reshape(block_count, channels, 8, 8, 8)
    planes = []
    for plane_x in range(3):
        line_list = []
        for line_y in range(3):
            cell_list = []
            for cell_z in range(3):
                position = 9 * plane_x + 3 * line_y + cell_z
                if position == CENTER:
                    cell_list.append(cube_grid)
                else:
                    column = position if position < CENTER else position - 1
                    cell_list.append(
                        neighbor_piece(
                            lookup_rows, neighbors[:, column], OFFSETS[position], slot_total
                        )
                    )
            line_list.append(jnp.concatenate(cell_list, axis=4))
        planes.append(jnp.concatenate(line_list, axis=3))
    return jnp.concatenate(planes, axis=2).reshape(block_count, channels, 1000)


def window_at(padded, position):
    step_x, step_y, step_z = OFFSETS[position]
    block_count, channels = (padded.shape[0], padded.shape[1])
    cube_grid = padded.reshape(block_count, channels, 10, 10, 10)
    piece = cube_grid[
        :, :, 1 + step_x : 9 + step_x, 1 + step_y : 9 + step_y, 1 + step_z : 9 + step_z
    ]
    return piece.reshape(block_count, channels, 512)


def conv_blocks(padded, weights):
    summed = None
    for position in range(27):
        product = jnp.einsum(
            "oi,bit->bot",
            weights[position],
            window_at(padded, position),
            preferred_element_type=jnp.float32,
        )
        summed = product if summed is None else summed + product
    return summed


def conv_weight_grad(padded, grad_out):
    grads = []
    for position in range(27):
        grads.append(
            jnp.einsum(
                "bot,bit->oi",
                grad_out,
                window_at(padded, position),
                preferred_element_type=jnp.float32,
            )
        )
    return jnp.stack(grads)


def down_forward(weights, hidden):
    kernel = weights.reshape(2, 2, 2, weights.shape[1], weights.shape[2])
    octants = hidden.reshape(hidden.shape[0], hidden.shape[1], 4, 2, 4, 2, 4, 2)
    result = jnp.einsum(
        "ijkcd,bdxiyjzk->cbxyz", kernel, octants, preferred_element_type=jnp.float32
    )
    return result.reshape(weights.shape[1], hidden.shape[0], 64)


def down_grad_weight(dpiece, hidden):
    grid_piece = dpiece.reshape(dpiece.shape[0], dpiece.shape[1], 4, 4, 4)
    octants = hidden.reshape(hidden.shape[0], hidden.shape[1], 4, 2, 4, 2, 4, 2)
    result = jnp.einsum(
        "cbxyz,bdxiyjzk->ijkcd", grid_piece, octants, preferred_element_type=jnp.float32
    )
    return result.reshape(8, dpiece.shape[0], hidden.shape[1])


def down_grad_input(weights, dpiece):
    kernel = weights.reshape(2, 2, 2, weights.shape[1], weights.shape[2])
    grid_piece = dpiece.reshape(dpiece.shape[0], dpiece.shape[1], 4, 4, 4)
    result = jnp.einsum(
        "ijkcd,cbxyz->bdxiyjzk", kernel, grid_piece, preferred_element_type=jnp.float32
    )
    return result.reshape(dpiece.shape[1], weights.shape[2], 512)


def routing_table(owner, peers, capacity):
    targets = jnp.arange(peers, dtype=jnp.int32)
    dest_hits = (owner[:, None] == targets[None, :]).astype(jnp.int32)
    earlier = jnp.cumsum(dest_hits, axis=0) - dest_hits
    dest_rank = jnp.sum(earlier * dest_hits, axis=1)
    places = jnp.arange(capacity, dtype=jnp.int32)
    return (owner[None, None, :] == targets[:, None, None]) & (
        dest_rank[None, None, :] == places[None, :, None]
    )


def local(features, voxel_mask, neighbors, w_conv, w_down, coarse_owner, cotangent):
    slot_count, channels = (features.shape[0], features.shape[1])
    edge_count = slot_count // 2
    peers = lax.axis_size("space")
    shards = lax.axis_size("chan")
    shard_index = lax.axis_index("chan")
    out_width = w_conv.shape[1]
    down_width = w_down.shape[1] // shards
    keep_mask = voxel_mask.astype(jnp.bfloat16)[:, None, :]
    mask_float = voxel_mask.astype(jnp.float32)[:, None, :]
    masked = features * keep_mask
    face_table = block_faces(masked)
    rim_faces = jnp.stack([face_table[:edge_count, 0], face_table[edge_count:, 1]])
    extended = extended_2(rim_faces, (("space", 0),), 1)
    lookup_rows = jnp.concatenate(
        [
            face_table.reshape(6 * slot_count, channels, 64),
            extended[0],
            extended[3],
            jnp.zeros((1, channels, 64), jnp.bfloat16),
        ]
    )
    in_part = lax.dynamic_slice_in_dim(w_down, shard_index * out_width, out_width, 2)
    padded = padded_blocks(lookup_rows, neighbors, masked, slot_count)
    conv_out = conv_blocks(padded, w_conv)
    own_input = lax.dynamic_slice_in_dim(masked, shard_index * out_width, out_width, 1)
    pre_act = own_input.astype(jnp.float32) + conv_out
    hidden = (mask_float * jax.nn.silu(pre_act)).astype(jnp.bfloat16)
    hidden_all = lax.all_gather(hidden, "chan", axis=1, tiled=True)
    own_down = lax.dynamic_slice_in_dim(w_down, shard_index * down_width, down_width, 1)
    down_out = down_forward(own_down, hidden_all)
    pieces = down_out.astype(jnp.bfloat16)
    capacity = cotangent.shape[0] // peers
    chosen = routing_table(coarse_owner[:, 0], peers, capacity).astype(jnp.bfloat16)
    outgoing = jnp.einsum(
        "drj,cjq->drcq", chosen, pieces, preferred_element_type=jnp.float32
    ).astype(jnp.bfloat16)
    arrived = lax.all_to_all(outgoing, "space", split_axis=0, concat_axis=0, tiled=True)
    coarse = arrived.reshape(peers * capacity, down_width, 64)
    returned = lax.all_to_all(
        cotangent.reshape(peers, capacity, down_width, 64),
        "space",
        split_axis=0,
        concat_axis=0,
        tiled=True,
    )
    dpiece = jnp.einsum(
        "drj,drcq->cjq", chosen, returned, preferred_element_type=jnp.float32
    ).astype(jnp.bfloat16)
    dpiece_all = lax.all_gather(dpiece, "chan", axis=0, tiled=True)
    dhidden = down_grad_input(in_part, dpiece_all)
    down_grad = down_grad_weight(dpiece, hidden_all)
    sigmoid = jax.nn.sigmoid(pre_act)
    dpre = (dhidden * mask_float * sigmoid * (1.0 + pre_act * (1.0 - sigmoid))).astype(jnp.bfloat16)
    conv_grad = conv_weight_grad(padded, dpre)
    conv_sum, down_sum = lax.psum((conv_grad, down_grad), "space")
    return (coarse, conv_sum, down_sum)


def solution(mesh):
    in_specs = (
        P("space", None, None),
        P("space", None),
        P("space", None),
        P(None, "chan", None),
        P(),
        P("space", None),
        P("space", "chan", None),
    )
    out_specs = (P("space", "chan", None), P(None, "chan", None), P(None, "chan", None))
    return jax.shard_map(local, mesh=mesh, in_specs=in_specs, out_specs=out_specs, check_vma=False)
```

profile of v0, /device:TPU:0, one launch (start us, length us, event | category | flops | bytes accessed | tf_op | source)
XLA Modules:
  0.0 274.0 jit_solution(6421216752966532505)
XLA Ops:
  9.4 5.2 %all-to-all-start.1 = ((bf16[8,2,4096]{2,1,0:T(2,128)(2,1)}), bf16[8,2,4096]{2,1,0:T(2,128)(2,1)}, u32[]{:S(2)}, u32[]{:S(2)}) async-start(bf16[8,2,4096]{2,1,0:T(2,128)(2,1)} %reshape.1023), calls=%async_computation.1 | async-start | bytes 262144 | tf_op jit(solution)/shard_map/all_to_all | solution.py:207
  14.6 1.4 fusion.119
  18.0 2.4 collective-permute-start
  70.1 1.3 gather_fusion.9
  101.2 3.5 %maximum_maximum_fusion.2 = (bf16[8,128,8,9,10]{1,4,3,2,0:T(8,128)(2,1)S(1)}, bf16[8,128,8,9,10]{1,4,3,2,0:T(8,128)(2,1)S(1)}) fusion(bf16[8,128,8,8,1]{1,4,3,2,0:T(2,128)(2,1)S(1)} %copy.312, bf16[8,128,8,8,8]{1,4,3,2,0:T(8,128)(2,1)S(1)} %bitcast.607, bf16[8,128,8,8,1]{1,4,3,2,0:T(2,128)(2,1)S(1)} %copy.311, bf16[8,128,8,1,1]{1,4,3,2,0:T(2,128)(2,1)S(1)} %copy-done.63, ...), kind=kLoop, calls=%fused_computation.28 | loop fusion | flops 17694720 | bytes 4587520 | tf_op jit(solution)/shard_map/concatenate | solution.py:89
  106.0 2.3 fusion.65
  109.5 2.0 fusion.63
  111.6 3.9 %maximum_maximum_fusion = bf16[8,128,9,10,10]{1,4,3,2,0:T(8,128)(2,1)S(1)} fusion(bf16[8,128,8,1,1]{1,4,3,2,0:T(2,128)(2,1)S(1)} %copy-done.61, bf16[8,128,8,1,8]{1,4,3,2,0:T(8,128)(2,1)S(1)} %select_bitcast_fusion.10, bf16[8,128,8,1,1]{1,4,3,2,0:T(2,128)(2,1)S(1)} %copy-done.62, bf16[8,128,8,8,1]{1,4,3,2,0:T(2,128)(2,1)S(1)} %copy.312, ...), kind=kLoop, calls=%fused_computation.26 | loop fusion | flops 33177600 | bytes 3686400 | tf_op jit(solution)/shard_map/concatenate | solution.py:90
  115.7 2.3 fusion.115
  118.0 2.5 fusion.80
  120.7 6.2 %maximum_maximum_fusion.1 = bf16[8,128,9,10,10]{1,4,3,2,0:T(8,128)(2,1)S(1)} fusion(bf16[8,128,1,1,1]{1,4,3,2,0:T(2,128)(2,1)S(1)} %copy-done.77, bf16[8,128,1,1,8]{1,4,3,2,0:T(8,128)(2,1)S(1)} %copy-done.74, bf16[8,128,1,1,1]{1,4,3,2,0:T(2,128)(2,1)S(1)} %copy-done.78, bf16[8,128,1,8,1]{1,4,3,2,0:T(2,128)(2,1)S(1)} %copy-done.69, ...), kind=kLoop, calls=%fused_computation.27 | loop fusion | flops 33177600 | bytes 3686400 | tf_op jit(solution)/shard_map/concatenate | solution.py:90
  127.0 2.3 fusion.114
  141.9 16.8 %all_gather.7 = bf16[256,8,64]{2,1,0:T(8,128)(2,1)S(1)} all-gather(bf16[64,8,64]{2,1,0:T(8,128)(2,1)S(1)} %fusion.16), channel_id=1, replica_groups=mesh['space'=8,'chan'=4] {'chan'}, dimensions={0}, use_global_device_ids=true | all-gather | bytes 327680 | tf_op jit(solution)/shard_map/all_gather | solution.py:217
  159.6 1.6 copy.363
  161.2 2.2 copy.364
  163.4 2.1 multiply_convert_fusion
  175.3 2.1 fusion.22
  177.4 2.2 fusion.21
  183.2 21.3 %all-gather.2.cloned.1.call-done = bf16[8,128,512]{2,1,0:T(8,128)(2,1)} async-done(((bf16[8,32,512]{2,1,0:T(8,128)(2,1)}), bf16[8,128,512]{2,1,0:T(8,128)(2,1)}) %all-gather.2.cloned.1.call-update) | async-done | bytes 1048592 | tf_op jit(solution)/shard_map/all_gather | solution.py:196
  204.5 1.7 copy.353
  209.5 9.5 %all_to_all.10 = bf16[8,2,4096]{2,1,0:T(2,128)(2,1)S(1)} all-to-all(bf16[8,2,4096]{2,1,0:T(2,128)(2,1)S(1)} %reshape.1021), channel_id=1, replica_groups=mesh['space'=8,'chan'=4] {'space'}, dimensions={0} | all-to-all | bytes 262144 | tf_op jit(solution)/shard_map/all_to_all | solution.py:205
  220.0 43.8 %all-reduce.3.cloned.1.call-done = (f32[27,32,128]{2,1,0:T(8,128)}, f32[8,64,128]{2,1,0:T(8,128)}) async-done(((f32[27,32,128]{2,1,0:T(8,128)}, f32[8,64,128]{2,1,0:T(8,128)}), (f32[27,32,128]{2,1,0:T(8,128)}, f32[8,64,128]{2,1,0:T(8,128)})) %all-reduce.3.cloned.1.call-update) | async-done | bytes 704528 | tf_op jit(solution)/shard_map/psum | solution.py:223
  263.7 1.8 copy.530
  265.5 1.7 copy.531
  (419 shorter events, 116.0 us)
Async XLA Ops:
  7.2 37.1 %copy-start = (bf16[8,256,128]{2,1,0:T(8,128)(2,1)S(1)}, bf16[8,256,128]{2,1,0:T(8,128)(2,1)}, u32[]{:S(2)}) copy-start(bf16[8,256,128]{2,1,0:T(8,128)(2,1)} %param.13) | copy-start | bytes 1572868
  7.2 14.5 %copy-start.52 = (s32[8,26]{1,0:T(8,128)S(1)}, s32[8,26]{1,0:T(8,128)}, u32[]{:S(2)}) copy-start(s32[8,26]{1,0:T(8,128)} %param.11) | copy-start | bytes 2500
  7.2 16.0 %copy-start.91 = (s32[8,1]{0,1:T(1,128)S(1)}, s32[8,1]{0,1:T(1,128)}, u32[]{:S(2)}) copy-start(s32[8,1]{0,1:T(1,128)} %param.14) | copy-start | bytes 100
  9.4 131.0 %all-to-all-start.1 = ((bf16[8,2,4096]{2,1,0:T(2,128)(2,1)}), bf16[8,2,4096]{2,1,0:T(2,128)(2,1)}, u32[]{:S(2)}, u32[]{:S(2)}) async-start(bf16[8,2,4096]{2,1,0:T(2,128)(2,1)} %reshape.1023), calls=%async_computation.1 | async-start | bytes 262144 | tf_op jit(solution)/shard_map/all_to_all | solution.py:207
  14.5 189.9 %all-gather.2.cloned.1.call-start = ((), (), s32[]{:S(2)}) async-start(), calls=%async_computation.2 | async-start | bytes 1310720 | tf_op jit(solution)/shard_map/all_gather | solution.py:196
  18.0 32.1 %collective-permute-start = (bf16[1,4,128,64]{2,3,1,0:T(8,128)(2,1)S(1)}, bf16[1,4,128,64]{2,3,1,0:T(8,128)(2,1)S(1)}, u32[]{:S(2)}, u32[]{:S(2)}) collective-permute-start(bf16[1,4,128,64]{2,3,1,0:T(8,128)(2,1)S(1)} %get-tuple-element.62), channel_id=1, source_target_pairs={{0,4},{4,8},{8,12},{12,16},{16,20},{20,24},{24,28},{1,5},{5,9},{9,... | collective-permute-start | bytes 196616 | tf_op jit(solution)/shard_map/ppermute | solution.py:23
  20.4 29.7 %collective-permute-start.1 = (bf16[1,4,128,64]{2,3,1,0:T(8,128)(2,1)S(1)}, bf16[1,4,128,64]{2,3,1,0:T(8,128)(2,1)S(1)}, u32[]{:S(2)}, u32[]{:S(2)}) collective-permute-start(bf16[1,4,128,64]{2,3,1,0:T(8,128)(2,1)S(1)} %get-tuple-element.63), channel_id=1, source_target_pairs={{4,0},{8,4},{12,8},{16,12},{20,16},{24,20},{28,24},{5,1},{9,5},{13... | collective-permute-start | bytes 196616 | tf_op jit(solution)/shard_map/ppermute | solution.py:25
  101.2 33.9 %copy-start.4 = (bf16[8,128,8,8,8]{1,4,3,2,0:T(8,128)(2,1)}, bf16[8,128,8,8,8]{1,4,3,2,0:T(8,128)(2,1)S(1)}, u32[]{:S(2)}) copy-start(bf16[8,128,8,8,8]{1,4,3,2,0:T(8,128)(2,1)S(1)} %get-tuple-element.58) | copy-start | bytes 3145732
  105.3 28.3 %copy-start.48 = (bf16[8,128,8,8,8]{1,4,3,2,0:T(8,128)(2,1)}, bf16[8,128,8,8,8]{1,4,3,2,0:T(8,128)(2,1)S(1)}, u32[]{:S(2)}) copy-start(bf16[8,128,8,8,8]{1,4,3,2,0:T(8,128)(2,1)S(1)} %get-tuple-element.55) | copy-start | bytes 3145732
  105.3 28.8 %copy-start.46 = (bf16[8,128,8,8,8]{1,4,3,2,0:T(8,128)(2,1)}, bf16[8,128,8,8,8]{1,4,3,2,0:T(8,128)(2,1)S(1)}, u32[]{:S(2)}) copy-start(bf16[8,128,8,8,8]{1,4,3,2,0:T(8,128)(2,1)S(1)} %get-tuple-element.54) | copy-start | bytes 3145732
  105.3 29.2 %copy-start.44 = (bf16[8,128,8,8,8]{1,4,3,2,0:T(8,128)(2,1)}, bf16[8,128,8,8,8]{1,4,3,2,0:T(8,128)(2,1)S(1)}, u32[]{:S(2)}) copy-start(bf16[8,128,8,8,8]{1,4,3,2,0:T(8,128)(2,1)S(1)} %get-tuple-element.53) | copy-start | bytes 3145732
  105.9 29.9 %copy-start.38 = (bf16[8,128,8,8,8]{1,4,3,2,0:T(8,128)(2,1)}, bf16[8,128,8,8,8]{1,4,3,2,0:T(8,128)(2,1)S(1)}, u32[]{:S(2)}) copy-start(bf16[8,128,8,8,8]{1,4,3,2,0:T(8,128)(2,1)S(1)} %get-tuple-element.50) | copy-start | bytes 3145732
  118.0 13.3 %copy-start.28 = (bf16[8,128,8,8,8]{1,4,3,2,0:T(8,128)(2,1)}, bf16[8,128,8,8,8]{1,4,3,2,0:T(8,128)(2,1)S(1)}, u32[]{:S(2)}) copy-start(bf16[8,128,8,8,8]{1,4,3,2,0:T(8,128)(2,1)S(1)} %get-tuple-element.45) | copy-start | bytes 3145732
  118.0 13.7 %copy-start.26 = (bf16[8,128,8,8,8]{1,4,3,2,0:T(8,128)(2,1)}, bf16[8,128,8,8,8]{1,4,3,2,0:T(8,128)(2,1)S(1)}, u32[]{:S(2)}) copy-start(bf16[8,128,8,8,8]{1,4,3,2,0:T(8,128)(2,1)S(1)} %get-tuple-element.44) | copy-start | bytes 3145732
  118.0 14.2 %copy-start.24 = (bf16[8,128,8,8,8]{1,4,3,2,0:T(8,128)(2,1)}, bf16[8,128,8,8,8]{1,4,3,2,0:T(8,128)(2,1)S(1)}, u32[]{:S(2)}) copy-start(bf16[8,128,8,8,8]{1,4,3,2,0:T(8,128)(2,1)S(1)} %get-tuple-element.43) | copy-start | bytes 3145732
  118.0 14.6 %copy-start.22 = (bf16[8,128,8,8,8]{1,4,3,2,0:T(8,128)(2,1)}, bf16[8,128,8,8,8]{1,4,3,2,0:T(8,128)(2,1)S(1)}, u32[]{:S(2)}) copy-start(bf16[8,128,8,8,8]{1,4,3,2,0:T(8,128)(2,1)S(1)} %get-tuple-element.42) | copy-start | bytes 3145732
  118.0 15.1 %copy-start.20 = (bf16[8,128,8,8,8]{1,4,3,2,0:T(8,128)(2,1)}, bf16[8,128,8,8,8]{1,4,3,2,0:T(8,128)(2,1)S(1)}, u32[]{:S(2)}) copy-start(bf16[8,128,8,8,8]{1,4,3,2,0:T(8,128)(2,1)S(1)} %get-tuple-element.41) | copy-start | bytes 3145732
  129.4 34.0 %copy-start.50 = (bf16[8,128,8,8,8]{1,4,3,2,0:T(8,128)(2,1)}, bf16[8,128,8,8,8]{1,4,3,2,0:T(8,128)(2,1)S(1)}, u32[]{:S(2)}) copy-start(bf16[8,128,8,8,8]{1,4,3,2,0:T(8,128)(2,1)S(1)} %get-tuple-element.32) | copy-start | bytes 3145732
  138.7 20.4 %copy-start.56 = (bf16[8,256,32]{2,1,0:T(8,128)(2,1)S(1)}, bf16[8,256,32]{2,1,0:T(8,128)(2,1)}, u32[]{:S(2)}) copy-start(bf16[8,256,32]{2,1,0:T(8,128)(2,1)} %constant_dynamic-slice_fusion) | copy-start | bytes 393220
  141.9 19.3 %copy-start.58 = (bf16[64,8,64]{2,1,0:T(8,128)(2,1)}, bf16[64,8,64]{2,1,0:T(8,128)(2,1)S(1)}, u32[]{:S(2)}) copy-start(bf16[64,8,64]{2,1,0:T(8,128)(2,1)S(1)} %fusion.16) | copy-start | bytes 196612
  173.5 90.2 %all-reduce.3.cloned.1.call-start = ((), (), s32[]{:S(2)}) async-start(), calls=%async_computation.3 | async-start | bytes 1409024 | tf_op jit(solution)/shard_map/psum | solution.py:223
  182.3 24.2 %copy-start.66 = (bf16[64,8,64]{0,1,2:T(8,128)(2,1)S(1)}, bf16[64,8,64]{0,1,2:T(8,128)(2,1)}, u32[]{:S(2)}) copy-start(bf16[64,8,64]{0,1,2:T(8,128)(2,1)} %copy.391) | copy-start | bytes 196612
  183.2 24.4 %copy-start.73 = (bf16[8,64,128]{2,1,0:T(8,128)(2,1)S(1)}, bf16[8,64,128]{2,1,0:T(8,128)(2,1)}, u32[]{:S(2)}) copy-start(bf16[8,64,128]{2,1,0:T(8,128)(2,1)} %constant_dynamic-slice_fusion.1) | copy-start | bytes 393220
  206.5 60.7 %copy-start.1 = (bf16[8,256,128]{2,1,0:T(8,128)(2,1)S(1)}, bf16[8,256,128]{2,1,0:T(8,128)(2,1)}, u32[]{:S(2)}) copy-start(bf16[8,256,128]{2,1,0:T(8,128)(2,1)} %param.13) | copy-start | bytes 1572868
  (73 other events, 334.6 us)
Sparse Core Ops, SparseCore 0:
  173.6 30.7 all-gather.1
  208.3 55.3 all-reduce.2
where the time goes:
time: 275 us; the launch traced here: 274 us
  waiting for transfers between devices  65.1 us (24%)
  local copies, waits for them, and re-layouts  64.8 us (24%)
  other arithmetic  54.1 us (20%)
  matrix products  38.8 us (14%)
  blocking collectives  26.3 us (10%)
  between operations  16.1 us (6%)
  starting transfers between devices  8.91 us (3%)
    psum x1, waiting for transfers between devices, local(): conv_sum, down_sum = lax.psum((conv_grad, down_grad), 'space')  43.8 us
    gather x26, local copies, waits for them, and re-layouts, neighbor_piece(): picked = jnp.take(lookup_rows, row_index, axis=0)  23.4 us
    all_gather x1, waiting for transfers between devices, local(): hidden_all = lax.all_gather(hidden, 'chan', axis=1, tiled=True)  21.3 us
    dot_general x27, matrix products, conv_blocks(): jnp.einsum('oi,bit->bot', weights[position], window_at(padded, position),...  20.7 us
    all_gather x1, blocking collectives, local(): dpiece_all = lax.all_gather(dpiece, 'chan', axis=0, tiled=True)  16.8 us
    dot_general x27, matrix products, conv_weight_grad(): jnp.einsum('bot,bit->oi', grad_out, window_at(padded, position), preferre...  14.6 us
    unnamed x203, local copies, waits for them, and re-layouts  12.2 us
    gather x26, other arithmetic  11.7 us
  transfers between devices with their start and end apart: 5, of which 2 were waited for; matrix products, arithmetic and copies ran while one was open for 48% of the time, Pallas kernels for 0%

commit v1 on v0

v1 whole, which is shorter than its diff:
```python
import functools

import jax
import jax.numpy as jnp
import numpy as np
from jax import lax
from jax.experimental import pallas as pl
from jax.experimental.pallas import tpu as pltpu
from jax.sharding import PartitionSpec as P

F32 = jnp.float32
BF16 = jnp.bfloat16
SIGNS = (-1, 0, 1)
LANES = 128
NT = (((1,), (1,)), ((), ()))
TN = (((0,), (0,)), ((), ()))
VMEM_LIMIT = 60 * 1024 * 1024


def vmem():
    return pl.BlockSpec(memory_space=pltpu.VMEM)


def smem():
    return pl.BlockSpec(memory_space=pltpu.SMEM)


def rim_lane(cell_y, cell_z):
    if 0 <= cell_y < 8 and 0 <= cell_z < 8:
        return 8 * cell_y + cell_z
    if 0 <= cell_z < 8:
        return 64 + 8 * (cell_y > 0) + cell_z
    if 0 <= cell_y < 8:
        return 80 + 8 * (cell_z > 0) + cell_y
    return 96 + 2 * (cell_y > 0) + (cell_z > 0)


def edge_table():
    table = np.zeros((9, LANES, LANES), np.float32)
    for place, (step_y, step_z) in enumerate((a, b) for a in SIGNS for b in SIGNS):
        for cell_y in range(8):
            for cell_z in range(8):
                far_y, far_z = cell_y + 8 * step_y, cell_z + 8 * step_z
                if -1 <= far_y <= 8 and -1 <= far_z <= 8:
                    table[place, 8 * cell_y + cell_z, rim_lane(far_y, far_z)] = 1
    return table


def shift_table():
    table = np.zeros((9, 2, 64, 2, LANES), np.float32)
    for place, (step_y, step_z) in enumerate((a, b) for a in SIGNS for b in SIGNS):
        for cell_y in range(8):
            for cell_z in range(8):
                lane = rim_lane(cell_y + step_y, cell_z + step_z)
                for plane in range(2):
                    table[place, plane, 8 * cell_y + cell_z, plane, lane] = 1
    return table.reshape(9 * 2 * 64, 2 * LANES)


def octant_table():
    table = np.zeros((8, 8, 8, 8, 2, 64), np.float32)
    for x in range(8):
        for y in range(8):
            for z in range(8):
                octant = 4 * (x % 2) + 2 * (y % 2) + z % 2
                table[x, y, z, octant, :, 16 * (x // 2) + 4 * (y // 2) + z // 2] = 1
    return table.reshape(512, 8 * LANES)


def ranks(owner_ref, block):
    place = jnp.int32(0)
    for earlier in range(block):
        place = place + (owner_ref[earlier, 0] == owner_ref[block, 0]).astype(jnp.int32)
    return place


def pick_kernel(capacity, owner_ref, returned_ref, out_ref):
    blocks = owner_ref.shape[0]
    for pair in range(blocks // 2):
        rows = []
        for block in (2 * pair, 2 * pair + 1):
            slot = owner_ref[block, 0] * capacity + ranks(owner_ref, block)
            rows.append(returned_ref[slot].astype(F32))
        out_ref[:, pair * LANES : (pair + 1) * LANES] = jnp.concatenate(rows, axis=1).astype(BF16)


def route_kernel(capacity, owner_ref, *refs):
    out_ref = refs[-1]
    blocks = owner_ref.shape[0]
    total = refs[0][...]
    for ref in refs[1:-1]:
        total = total + ref[...]
    out_ref[...] = jnp.zeros_like(out_ref)
    for block in range(blocks):
        slot = owner_ref[block, 0] * capacity + ranks(owner_ref, block)
        piece = total[:, block * 64 : (block + 1) * 64].astype(BF16)
        out_ref[slot] = piece


def main_kernel(
    shards,
    partner,
    split,
    nbr_ref,
    at_ref,
    feat_ref,
    mask_ref,
    prev_ref,
    next_ref,
    wconv_ref,
    wdown_ref,
    edge_ref,
    shift_ref,
    octant_ref,
    *refs,
):
    dps = refs[:shards]
    refs = refs[shards:]
    outs = refs[:3]
    planes, patches, weights, pre_s, hidden_s, octs, spread, pieces_s, dp_s, dh_s, dhi, dlo, d3, grads = refs[3:]
    blocks, channels = feat_ref.shape[0], feat_ref.shape[1]
    edge = blocks // 2
    width = wconv_ref.shape[1]
    total = wdown_ref.shape[1]
    share = total // shards
    me = at_ref[0]
    lane = lax.broadcasted_iota(jnp.int32, (channels, LANES), 1)
    low = lane < 64
    halo = 10 * blocks

    zero_plane = jnp.zeros((channels, LANES), BF16)
    for block in range(blocks):
        keep = mask_ref[block : block + 1, :].astype(F32)
        masked = feat_ref[block].astype(F32) * keep
        planes[10 * block] = zero_plane
        planes[10 * block + 9] = zero_plane
        for pair in range(4):
            tile = masked[:, pair * LANES : (pair + 1) * LANES]
            planes[10 * block + 1 + 2 * pair] = jnp.where(low, tile, 0.0).astype(BF16)
            planes[10 * block + 2 + 2 * pair] = jnp.where(low, pltpu.roll(tile, 64, 1), 0.0).astype(BF16)
    for i in range(edge):
        planes[halo + i] = zero_plane
        planes[halo + edge + i] = zero_plane
        planes[halo + i, :, 0:64] = prev_ref[i]
        planes[halo + edge + i, :, 0:64] = next_ref[i]

    def rim(item, carry):
        block = item // 26
        column = item - block * 26
        source = nbr_ref[block, column]

        @pl.when(source >= 0)
        def _():
            position = column + (column >= 13).astype(jnp.int32)
            step_x = position // 9 - 1
            table = edge_ref[position - 9 * (step_x + 1)]

            @pl.when(step_x == 0)
            def _():
                cells = planes[pl.ds(source * 10 + 1, 8)].reshape(8 * channels, LANES)
                moved = jnp.dot(cells, table, preferred_element_type=F32).astype(BF16)
                planes[pl.ds(block * 10 + 1, 8)] += moved.reshape(8, channels, LANES)

            @pl.when(step_x != 0)
            def _():
                own = source * 10 + jnp.where(step_x < 0, 8, 1)
                cells = planes[jnp.where(source < blocks, own, halo + source - blocks)]
                moved = jnp.dot(cells, table, preferred_element_type=F32).astype(BF16)
                planes[block * 10 + jnp.where(step_x < 0, 0, 9)] += moved

        return carry

    lax.fori_loop(0, blocks * 26, rim, 0)

    for k in range(27):
        weights[(k // 9) * width : (k // 9 + 1) * width, (k % 9) * channels : (k % 9 + 1) * channels] = wconv_ref[k]

    def patch(item, carry):
        block = 2 * (item // 5)
        plane = 2 * (item % 5)
        first, second = block * 10 + plane, block * 10 + 10 + plane
        source = jnp.concatenate(
            [
                jnp.concatenate([planes[first], planes[first + 1]], axis=1),
                jnp.concatenate([planes[second], planes[second + 1]], axis=1),
            ],
            axis=0,
        )
        window = lax.dot_general(shift_ref[...], source, NT, preferred_element_type=F32).astype(BF16)
        for j in range(9):
            for half in range(2):
                row = pl.multiple_of((first + 10 * half) * 64, 128)
                patches[pl.ds(row, 128), j * channels : (j + 1) * channels] = window[
                    j * 128 : (j + 1) * 128, half * channels : (half + 1) * channels
                ]
        return carry

    lax.fori_loop(0, 5 * (blocks // 2), patch, 0)

    own_rows = pl.ds(pl.multiple_of(me * width, width), width)

    def forward(block, carry):
        rows = pl.ds(pl.multiple_of(block * 640, 128), 640)
        sums = lax.dot_general(weights[...], patches[rows, :], NT, preferred_element_type=F32)
        keep = mask_ref[pl.ds(block, 1), :].astype(F32)
        pre = (
            feat_ref[block, own_rows, :].astype(F32) * keep
            + sums[:width, 0:512]
            + pltpu.roll(sums[width : 2 * width], 640 - 64, 1)[:, 0:512]
            + sums[2 * width :, 128:640]
        )
        here = pl.ds(pl.multiple_of(block * width, width), width)
        pre_s[here, :] = pre
        hidden_s[here, :] = (keep * (pre * (1.0 / (1.0 + jnp.exp(-pre))))).astype(BF16)
        return carry

    lax.fori_loop(0, blocks, forward, 0)

    split_up = jnp.dot(hidden_s[...], octant_ref[...], preferred_element_type=F32)
    low_w = low[:width]
    spread[...] = jnp.zeros_like(spread)
    for octant in range(8):
        for pair in range(blocks // 2):
            even = split_up[2 * pair * width : (2 * pair + 1) * width, octant * LANES : (octant + 1) * LANES]
            odd = split_up[(2 * pair + 1) * width : (2 * pair + 2) * width, octant * LANES : (octant + 1) * LANES]
            tile = jnp.where(low_w, even, odd).astype(BF16)
            octs[octant * width : (octant + 1) * width, pair * LANES : (pair + 1) * LANES] = tile
            spread[pl.ds(pl.multiple_of(octant * channels + me * width, width), width), pair * LANES : (pair + 1) * LANES] = tile
    down_weights = jnp.concatenate([wdown_ref[octant] for octant in range(8)], axis=1)
    pieces_s[...] = jnp.dot(down_weights, spread[...], preferred_element_type=F32)
    for k in range(shards):
        theirs = pl.multiple_of(partner(me, k) * share, share)
        outs[0][k] = pieces_s[pl.ds(theirs, share), :]
        dp_s[pl.ds(theirs, share), :] = dps[k][...]

    for octant in range(8):
        dh_s[octant] = lax.dot_general(wdown_ref[octant], dp_s[...], TN, preferred_element_type=F32)
    for octant in range(8):
        for pair in range(blocks // 2):
            tile = dh_s[octant, own_rows, pair * LANES : (pair + 1) * LANES]
            high = tile.astype(BF16).astype(F32)
            rest = tile - high
            lanes = slice(octant * LANES, (octant + 1) * LANES)
            even = slice(2 * pair * width, (2 * pair + 1) * width)
            odd = slice((2 * pair + 1) * width, (2 * pair + 2) * width)
            dhi[even, lanes] = jnp.where(low_w, high, 0.0).astype(BF16)
            dhi[odd, lanes] = jnp.where(low_w, 0.0, high).astype(BF16)
            dlo[even, lanes] = jnp.where(low_w, rest, 0.0).astype(BF16)
            dlo[odd, lanes] = jnp.where(low_w, 0.0, rest).astype(BF16)
    dhidden = lax.dot_general(dhi[...], octant_ref[...], NT, preferred_element_type=F32)
    dhidden = dhidden + lax.dot_general(dlo[...], octant_ref[...], NT, preferred_element_type=F32)

    blank = jnp.zeros((width, LANES), F32)
    for block in range(blocks):
        rows = slice(block * width, (block + 1) * width)
        pre = pre_s[rows, :]
        keep = mask_ref[block : block + 1, :].astype(F32)
        gate = 1.0 / (1.0 + jnp.exp(-pre))
        dpre = dhidden[rows] * keep * gate * (1.0 + pre * (1.0 - gate))
        at = block * 640
        d3[0:width, at : at + 512] = dpre.astype(BF16)
        d3[0:width, at + 512 : at + 640] = blank.astype(BF16)
        d3[width : 2 * width, at : at + 640] = pltpu.roll(jnp.concatenate([dpre, blank], axis=1), 64, 1).astype(BF16)
        d3[2 * width :, at : at + 128] = blank.astype(BF16)
        d3[2 * width :, at + 128 : at + 640] = dpre.astype(BF16)

    down_grad = lax.dot_general(dp_s[...], octs[...], NT, preferred_element_type=F32)
    if split is None:
        for j in range(9):
            part = jnp.dot(d3[...], patches[:, j * channels : (j + 1) * channels], preferred_element_type=F32)
            for dx in range(3):
                outs[1][9 * dx + j] = part[dx * width : (dx + 1) * width]
        grads[0:total] = down_grad[:, 0:LANES]
        grads[total : 2 * total] = down_grad[:, LANES:]
        for k in range(shards):
            theirs = pl.multiple_of(partner(me, k) * share, share)
            outs[2][k, :, 0:LANES] = grads[pl.ds(theirs, share), :]
            outs[2][k, :, LANES:] = grads[pl.ds(total + theirs, share), :]
        return
    chips, conv_rows, down_rows = split
    chunk = conv_rows + shards * down_rows
    for j in range(9):
        part = jnp.dot(d3[...], patches[:, j * channels : (j + 1) * channels], preferred_element_type=F32)
        for dx in range(3):
            first = (9 * dx + j) * width
            for row in range(first, first + width, 8):
                at = (row // conv_rows) * chunk + row % conv_rows
                grads[at : at + 8] = part[dx * width + row - first : dx * width + row - first + 8]
    for row in range(27 * width, 2 * chips * conv_rows, 8):
        at = (row // conv_rows) * chunk + row % conv_rows
        grads[at : at + 8] = jnp.zeros((8, LANES), F32)
    down_s = pieces_s
    down_s[:, 0 : 2 * LANES] = down_grad
    for k in range(shards):
        theirs = partner(me, k) * share
        for part in range(2 * chips):
            row = part * down_rows
            source = pl.ds(pl.multiple_of(theirs + row % share, 8), down_rows)
            at = part * chunk + conv_rows + k * down_rows
            grads[at : at + down_rows] = down_s[source, (row // share) * LANES : (row // share + 1) * LANES]
    core, chip = at_ref[1], at_ref[2]
    for k in range(chips):
        theirs = chip ^ k
        outs[1][k] = grads[pl.ds(pl.multiple_of((2 * theirs + core) * chunk, 8), chunk), :]
        outs[2][k] = grads[pl.ds(pl.multiple_of((2 * theirs + 1 - core) * chunk, 8), chunk), :]


def finish_kernel(shards, partner, split, at_ref, own_ref, other_ref, conv_ref, down_ref, conv_s, down_s):
    chips, conv_rows, down_rows = split
    me, core, chip = at_ref[0], at_ref[1], at_ref[2]
    share = down_ref.shape[1]
    width = conv_ref.shape[1]
    for side, ref in enumerate((own_ref, other_ref)):
        for k in range(chips):
            part = 2 * (chip ^ k) + (core if side == 0 else 1 - core)
            conv_s[pl.ds(pl.multiple_of(part * conv_rows, 8), conv_rows), :] = ref[k, :conv_rows]
            for source in range(shards):
                row = conv_rows + source * down_rows
                at = pl.multiple_of(part * down_rows, 8)
                down_s[source, pl.ds(at, down_rows), :] = ref[k, row : row + down_rows]
    for k in range(27):
        conv_ref[k] = conv_s[k * width : (k + 1) * width]
    group = lax.broadcasted_iota(jnp.int32, (share, LANES), 1) // width
    for octant in range(8):
        result = jnp.zeros((share, LANES), F32)
        for k in range(shards):
            source = partner(me, k)
            tile = down_s[k, (octant // 4) * share : (octant // 4 + 1) * share, :]
            turned = pltpu.roll(tile, ((source - octant % 4 + 4) % 4) * width, 1)
            result = jnp.where(group == source, turned, result)
        down_ref[octant] = result


def permute(values, axis, pairs):
    return lax.ppermute(values, axis, pairs)


def exchange(values, axis, step):
    count = lax.axis_size(axis)
    return lax.ppermute(values, axis, [(i, i ^ step) for i in range(count)])


def local(features, voxel_mask, neighbors, w_conv, w_down, coarse_owner, cotangent):
    blocks, channels = features.shape[0], features.shape[1]
    edge = blocks // 2
    peers = lax.axis_size("space")
    shards = lax.axis_size("chan")
    width = w_conv.shape[1]
    total = w_down.shape[1]
    share = total // shards
    capacity = cotangent.shape[0] // peers
    me = lax.axis_index("chan").astype(jnp.int32)
    spot = lax.axis_index("space").astype(jnp.int32)
    at = jnp.stack([me, spot % 2, spot // 2])

    def partner(index, k):
        return index ^ k

    head = features[:edge, :, :64] * voxel_mask[:edge, None, :64].astype(BF16)
    tail = features[edge:, :, 448:] * voxel_mask[edge:, None, 448:].astype(BF16)
    ends = peers - 1
    before = lax.ppermute(tail, "space", [(i, i + 1) for i in range(ends)])
    after = lax.ppermute(head, "space", [(i + 1, i) for i in range(ends)])

    returned = lax.all_to_all(
        cotangent.reshape(peers, capacity * share, 64), "space", split_axis=0, concat_axis=0, tiled=True
    ).reshape(peers * capacity, share, 64)
    lanes = blocks * 64
    dpiece = pl.pallas_call(
        functools.partial(pick_kernel, capacity),
        out_shape=jax.ShapeDtypeStruct((share, lanes), BF16),
        in_specs=[smem(), vmem()],
        out_specs=vmem(),
    )(coarse_owner, returned)
    dpieces = [dpiece] + [exchange(dpiece, "chan", k) for k in range(1, shards)]

    down_rows = 2 * share // peers
    chips = peers // 2
    split = None
    if peers & ends == 0 and down_rows % 8 == 0 and share % down_rows == 0:
        conv_rows = -(-27 * width // (8 * peers)) * 8
        split = (chips, conv_rows, down_rows)
        chunk = conv_rows + shards * down_rows
        grad_shapes = [(chips, chunk, LANES)] * 2
        grad_rows = peers * chunk
    else:
        grad_shapes = [(27, width, channels), (shards, share, 2 * LANES)]
        grad_rows = 2 * total

    pieces, first, second = pl.pallas_call(
        functools.partial(main_kernel, shards, partner, split),
        out_shape=[jax.ShapeDtypeStruct(s, F32) for s in [(shards, share, lanes)] + grad_shapes],
        in_specs=[smem(), smem()] + [vmem()] * (9 + shards),
        out_specs=[vmem()] * 3,
        scratch_shapes=[
            pltpu.VMEM((11 * blocks, channels, LANES), BF16),
            pltpu.VMEM((blocks * 640, 9 * channels), BF16),
            pltpu.VMEM((3 * width, 9 * channels), BF16),
            pltpu.VMEM((blocks * width, 512), F32),
            pltpu.VMEM((blocks * width, 512), BF16),
            pltpu.VMEM((8 * width, lanes), BF16),
            pltpu.VMEM((8 * channels, lanes), BF16),
            pltpu.VMEM((total, lanes), F32),
            pltpu.VMEM((total, lanes), BF16),
            pltpu.VMEM((8, channels, lanes), F32),
            pltpu.VMEM((blocks * width, 8 * LANES), BF16),
            pltpu.VMEM((blocks * width, 8 * LANES), BF16),
            pltpu.VMEM((3 * width, blocks * 640), BF16),
            pltpu.VMEM((grad_rows, LANES), F32),
        ],
        compiler_params=pltpu.CompilerParams(vmem_limit_bytes=VMEM_LIMIT),
    )(
        neighbors,
        at,
        features,
        voxel_mask,
        before,
        after,
        w_conv,
        w_down,
        jnp.asarray(edge_table(), BF16),
        jnp.asarray(shift_table(), BF16),
        jnp.asarray(octant_table(), BF16),
        *dpieces,
    )

    parts = [pieces[0]] + [exchange(pieces[k], "chan", k) for k in range(1, shards)]
    outgoing = pl.pallas_call(
        functools.partial(route_kernel, capacity),
        out_shape=jax.ShapeDtypeStruct((peers * capacity, share, 64), BF16),
        in_specs=[smem()] + [vmem()] * shards,
        out_specs=vmem(),
    )(coarse_owner, *parts)
    coarse = lax.all_to_all(
        outgoing.reshape(peers, capacity * share, 64), "space", split_axis=0, concat_axis=0, tiled=True
    ).reshape(peers * capacity, share, 64)

    if split is None:
        conv_sum = lax.psum(first, "space")
        parts = [second[0]] + [exchange(second[k], "chan", k) for k in range(1, shards)]
        down_parts = jnp.stack(parts)
        order = jnp.arange(shards, dtype=jnp.int32) ^ me
        down_parts = jnp.take(down_parts, order, axis=0).reshape(shards, share, 8, width)
        down_sum = lax.psum(down_parts.transpose(2, 1, 0, 3).reshape(8, share, shards * width), "space")
        return coarse, conv_sum, down_sum

    chips, conv_rows, down_rows = split
    halves = first + exchange(second, "space", 1)
    mine = halves[0]
    for k in range(1, chips):
        mine = mine + exchange(halves[k], "space", 2 * k)
    downs = [mine[conv_rows + k * down_rows : conv_rows + (k + 1) * down_rows] for k in range(shards)]
    downs = [downs[0]] + [exchange(downs[k], "chan", k) for k in range(1, shards)]
    mine = jnp.concatenate([mine[:conv_rows]] + downs)
    all_mine = jnp.stack([mine] + [exchange(mine, "space", 2 * k) for k in range(1, chips)])
    all_other = exchange(all_mine, "space", 1)
    conv_sum, down_sum = pl.pallas_call(
        functools.partial(finish_kernel, shards, partner, split),
        out_shape=[
            jax.ShapeDtypeStruct((27, width, channels), F32),
            jax.ShapeDtypeStruct((8, share, channels), F32),
        ],
        in_specs=[smem(), vmem(), vmem()],
        out_specs=[vmem()] * 2,
        scratch_shapes=[
            pltpu.VMEM((peers * conv_rows, LANES), F32),
            pltpu.VMEM((shards, 2 * share, LANES), F32),
        ],
    )(at, all_mine, all_other)
    return coarse, conv_sum, down_sum


def solution(mesh):
    in_specs = (
        P("space", None, None),
        P("space", None),
        P("space", None),
        P(None, "chan", None),
        P(),
        P("space", None),
        P("space", "chan", None),
    )
    out_specs = (P("space", "chan", None), P(None, "chan", None), P(None, "chan", None))
    return jax.shard_map(local, mesh=mesh, in_specs=in_specs, out_specs=out_specs, check_vma=False)
```

time: 275 us -> 118 us (0.43)
  local copies, waits for them, and re-layouts: 64.8 us -> 9.33 us
  other arithmetic: 54.1 us -> 2.85 us
  matrix products: 38.8 us -> 0 us
  Pallas kernels: 0 us -> 36 us
  waiting for transfers between devices: 65.1 us -> 30.8 us
  starting transfers between devices: 8.91 us -> 30 us
  blocking collectives: 26.3 us -> 7.92 us
  between operations: 16.1 us -> 0.8 us
    psum x1 -> x0, waiting for transfers between devices: 43.8 us -> none  [local(): conv_sum, down_sum = lax.psum((conv_grad, down_grad), 'space')]
    dot_general x59 -> x0, matrix products: 38.8 us -> none  [the longest x27 20.7 us: conv_blocks(): jnp.einsum('oi,bit->bot', weights[position], window_at(padded, position),...]
    pallas_call x0 -> x4, Pallas kernels: none -> 36 us  [the longest x1 30.1 us: local(): pl.pallas_call(functools.partial(main_kernel, shards, partner, split), ou...]
    ppermute x2 -> x19, waiting for transfers between devices: 0.01 us -> 30.8 us  [the longest x17 30.8 us: exchange(): return lax.ppermute(values, axis, [(i, i ^ step) for i in range(count)])]
    gather x26 -> x0, local copies, waits for them, and re-layouts: 23.4 us -> none  [neighbor_piece(): picked = jnp.take(lookup_rows, row_index, axis=0)]
    all_gather x1 -> x0, waiting for transfers between devices: 21.3 us -> none  [local(): hidden_all = lax.all_gather(hidden, 'chan', axis=1, tiled=True)]
    ppermute x2 -> x19, starting transfers between devices: 3.66 us -> 24.7 us  [the longest x17 20.4 us: exchange(): return lax.ppermute(values, axis, [(i, i ^ step) for i in range(count)])]
    all_gather x1 -> x0, blocking collectives: 16.8 us -> none  [local(): dpiece_all = lax.all_gather(dpiece, 'chan', axis=0, tiled=True)]
  transfers between devices with their start and end apart: 5 -> 20, of which waited for: 2 -> 14; matrix products, arithmetic and copies ran while one was open for 48% -> 5% of each run, Pallas kernels for 0% -> 3%
where the time goes in v1:
time: 118 us
  Pallas kernels  36 us (31%)
  waiting for transfers between devices  30.8 us (26%)
  starting transfers between devices  30 us (25%)
  local copies, waits for them, and re-layouts  9.33 us (8%)
  blocking collectives  7.92 us (7%)
  other arithmetic  2.85 us (2%)
    ppermute x17, waiting for transfers between devices, exchange(): return lax.ppermute(values, axis, [(i, i ^ step) for i in range(count)])  30.8 us
    pallas_call x1, Pallas kernels, local(): pl.pallas_call(functools.partial(main_kernel, shards, partner, split), ou...  30.1 us
    ppermute x17, starting transfers between devices, exchange(): return lax.ppermute(values, axis, [(i, i ^ step) for i in range(count)])  20.4 us
    all_to_all x1, blocking collectives, local(): lax.all_to_all(outgoing.reshape(peers, capacity * share, 64), 'space', sp...  7.92 us
    all_to_all x1, starting transfers between devices, local(): lax.all_to_all(cotangent.reshape(peers, capacity * share, 64), 'space', s...  5.3 us
    unnamed x28, local copies, waits for them, and re-layouts  4.84 us
    ppermute x1, starting transfers between devices, local(): before = lax.ppermute(tail, 'space', [(i, i + 1) for i in range(ends)])  3.04 us
  transfers between devices with their start and end apart: 20, of which 14 were waited for; matrix products, arithmetic and copies ran while one was open for 5% of the time, Pallas kernels for 3%

profile of v1, /device:TPU:0, one launch (start us, length us, event | category | flops | bytes accessed | tf_op | source)
XLA Modules:
  0.0 117.7 jit_solution(445035422739549730)
XLA Ops:
  0.6 1.7 %copy.20 = bf16[8,128,64]{1,2,0:T(8,128)(2,1)} copy(bf16[8,128,64]{2,1,0:T(8,128)(2,1)} %bitcast.36) | data formatting | bytes 262144 | tf_op jit(solution)/shard_map/reshape | solution.py:366
  2.4 5.3 %all-to-all-start = ((bf16[8,128,64]{1,2,0:T(8,128)(2,1)}), bf16[8,128,64]{1,2,0:T(8,128)(2,1)S(1)}, u32[]{:S(2)}, u32[]{:S(2)}) async-start(bf16[8,128,64]{1,2,0:T(8,128)(2,1)} %copy.20), calls=%async_computation | async-start | bytes 262144 | tf_op jit(solution)/shard_map/all_to_all | solution.py:365
  10.1 3.0 %collective-permute-start = (bf16[4,128,64]{2,1,0:T(8,128)(2,1)S(1)}, bf16[4,128,64]{2,1,0:T(8,128)(2,1)S(1)}, u32[]{:S(2)}, u32[]{:S(2)}) collective-permute-start(bf16[4,128,64]{2,1,0:T(8,128)(2,1)S(1)} %get-tuple-element.17), channel_id=1, source_target_pairs={{0,4},{4,8},{8,12},{12,16},{16,20},{20,24},{24,28},{1,5},{5,9},{9,... | collective-permute-start | bytes 196616 | tf_op jit(solution)/shard_map/ppermute | solution.py:362
  15.4 1.7 %shard_map.121.refs_0_ = bf16[64,512]{1,0:T(8,128)(2,1)} custom-call(s32[8,1]{1,0:T(8,128)} %copy.23.owner_ref, bf16[16,64,64]{2,1,0:T(8,128)(2,1)} %bitcast.35), custom_call_target="tpu_custom_call" | custom-call | tf_op jit(solution)/shard_map/pallas_call | solution.py:369
  17.1 3.6 %collective-permute-start.4 = (bf16[64,512]{1,0:T(8,128)(2,1)}, bf16[64,512]{1,0:T(8,128)(2,1)S(1)}, u32[]{:S(2)}, u32[]{:S(2)}) collective-permute-start(bf16[64,512]{1,0:T(8,128)(2,1)} %shard_map.121.refs_0_), channel_id=1, source_target_pairs={{0,3},{1,2},{2,1},{3,0},{4,7},{5,6},{6,5},{7,4},{8,11},{9,10},{10,... | collective-permute-start | bytes 196616 | tf_op jit(solution)/shard_map/ppermute | solution.py:340
  23.4 3.8 %collective-permute-done.3.refs_2_ = bf16[64,512]{1,0:T(8,128)(2,1)S(1)} collective-permute-done((bf16[64,512]{1,0:T(8,128)(2,1)}, bf16[64,512]{1,0:T(8,128)(2,1)S(1)}, u32[]{:S(2)}, u32[]{:S(2)}) %collective-permute-start.3) | collective-permute-done | bytes 65568 | tf_op jit(solution)/shard_map/ppermute | solution.py:340
  28.5 30.1 %shard_map.122 = (f32[4,64,512]{2,1,0:T(8,128)}, f32[4,176,128]{2,1,0:T(8,128)}, f32[4,176,128]{2,1,0:T(8,128)}) custom-call(s32[8,26]{1,0:T(8,128)} %nbr_ref.1, s32[3]{0:T(128)} %pad_add_fusion.at_ref, bf16[8,128,512]{2,1,0:T(8,128)(2,1)} %feat_ref.1, s32[8,512]{1,0:T(8,128)} %mask_ref.1, bf16[4,128,64]{2,1,0:T(8,128)(2,1)} %copy-done.7, ...), custom_call_target="tpu_custom_call" | custom-call | tf_op jit(solution)/shard_map/pallas_call | solution.py:390
  59.4 1.5 %collective-permute-done.8 = f32[4,176,128]{2,1,0:T(8,128)S(1)} collective-permute-done((f32[4,176,128]{2,1,0:T(8,128)}, f32[4,176,128]{2,1,0:T(8,128)S(1)}, u32[]{:S(2)}, u32[]{:S(2)}) %collective-permute-start.8) | collective-permute-done | bytes 360480 | tf_op jit(solution)/shard_map/ppermute | solution.py:340
  62.0 1.7 %collective-permute-start.9 = (f32[176,128]{1,0:T(8,128)S(1)}, f32[176,128]{1,0:T(8,128)S(1)}, u32[]{:S(2)}, u32[]{:S(2)}) collective-permute-start(f32[176,128]{1,0:T(8,128)S(1)} %get-tuple-element.22), channel_id=1, source_target_pairs={{0,8},{4,12},{8,0},{12,4},{16,24},{20,28},{24,16},{28,20},{1,9},{5... | collective-permute-start | bytes 270344 | tf_op jit(solution)/shard_map/ppermute | solution.py:340
  65.6 1.9 %collective-permute-done.9 = f32[176,128]{1,0:T(8,128)S(1)} collective-permute-done((f32[176,128]{1,0:T(8,128)S(1)}, f32[176,128]{1,0:T(8,128)S(1)}, u32[]{:S(2)}, u32[]{:S(2)}) %collective-permute-start.9) | collective-permute-done | bytes 90144 | tf_op jit(solution)/shard_map/ppermute | solution.py:340
  67.5 1.8 %collective-permute-done.11 = f32[176,128]{1,0:T(8,128)S(1)} collective-permute-done((f32[176,128]{1,0:T(8,128)S(1)}, f32[176,128]{1,0:T(8,128)S(1)}, u32[]{:S(2)}, u32[]{:S(2)}) %collective-permute-start.11) | collective-permute-done | bytes 90144 | tf_op jit(solution)/shard_map/ppermute | solution.py:340
  71.4 1.9 %collective-permute-start.14 = (f32[16,128]{1,0:T(8,128)S(1)}, f32[16,128]{1,0:T(8,128)S(1)}, u32[]{:S(2)}, u32[]{:S(2)}) collective-permute-start(f32[16,128]{1,0:T(8,128)S(1)} %get-tuple-element.28), channel_id=1, source_target_pairs={{0,3},{1,2},{2,1},{3,0},{4,7},{5,6},{6,5},{7,4},{8,11},{9,10},{10,... | collective-permute-start | bytes 24584 | tf_op jit(solution)/shard_map/ppermute | solution.py:340
  74.4 2.4 %collective-permute-done.14 = f32[16,128]{1,0:T(8,128)S(1)} collective-permute-done((f32[16,128]{1,0:T(8,128)S(1)}, f32[16,128]{1,0:T(8,128)S(1)}, u32[]{:S(2)}, u32[]{:S(2)}) %collective-permute-start.14) | collective-permute-done | bytes 8224 | tf_op jit(solution)/shard_map/ppermute | solution.py:340
  77.9 1.6 %collective-permute-start.16 = (f32[176,128]{1,0:T(8,128)S(1)}, f32[176,128]{1,0:T(8,128)S(1)}, u32[]{:S(2)}, u32[]{:S(2)}) collective-permute-start(f32[176,128]{1,0:T(8,128)S(1)} %get-tuple-element.26), channel_id=1, source_target_pairs={{0,16},{4,20},{8,24},{12,28},{16,0},{20,4},{24,8},{28,12},{1,17},{... | collective-permute-start | bytes 270344 | tf_op jit(solution)/shard_map/ppermute | solution.py:340
  79.5 1.6 %collective-permute-start.15 = (f32[176,128]{1,0:T(8,128)S(1)}, f32[176,128]{1,0:T(8,128)S(1)}, u32[]{:S(2)}, u32[]{:S(2)}) collective-permute-start(f32[176,128]{1,0:T(8,128)S(1)} %get-tuple-element.26), channel_id=1, source_target_pairs={{0,8},{4,12},{8,0},{12,4},{16,24},{20,28},{24,16},{28,20},{1,9},{5... | collective-permute-start | bytes 270344 | tf_op jit(solution)/shard_map/ppermute | solution.py:340
  82.5 1.5 %collective-permute-done.15 = f32[176,128]{1,0:T(8,128)S(1)} collective-permute-done((f32[176,128]{1,0:T(8,128)S(1)}, f32[176,128]{1,0:T(8,128)S(1)}, u32[]{:S(2)}, u32[]{:S(2)}) %collective-permute-start.15) | collective-permute-done | bytes 90144 | tf_op jit(solution)/shard_map/ppermute | solution.py:340
  84.0 2.5 %collective-permute-done.17 = f32[176,128]{1,0:T(8,128)S(1)} collective-permute-done((f32[176,128]{1,0:T(8,128)S(1)}, f32[176,128]{1,0:T(8,128)S(1)}, u32[]{:S(2)}, u32[]{:S(2)}) %collective-permute-start.17) | collective-permute-done | bytes 90144 | tf_op jit(solution)/shard_map/ppermute | solution.py:340
  87.4 1.4 %collective-permute-start.7 = (f32[64,512]{1,0:T(8,128)S(1)}, f32[64,512]{1,0:T(8,128)S(1)}, u32[]{:S(2)}, u32[]{:S(2)}) collective-permute-start(f32[64,512]{1,0:T(8,128)S(1)} %get-tuple-element.18), channel_id=1, source_target_pairs={{0,3},{1,2},{2,1},{3,0},{4,7},{5,6},{6,5},{7,4},{8,11},{9,10},{10,... | collective-permute-start | bytes 393224 | tf_op jit(solution)/shard_map/ppermute | solution.py:340
  89.9 1.9 %collective-permute-start.5 = (f32[64,512]{1,0:T(8,128)S(1)}, f32[64,512]{1,0:T(8,128)S(1)}, u32[]{:S(2)}, u32[]{:S(2)}) collective-permute-start(f32[64,512]{1,0:T(8,128)S(1)} %get-tuple-element.20), channel_id=1, source_target_pairs={{0,1},{1,0},{2,3},{3,2},{4,5},{5,4},{6,7},{7,6},{8,9},{9,8},{10,11... | collective-permute-start | bytes 393224 | tf_op jit(solution)/shard_map/ppermute | solution.py:340
  91.8 3.9 %collective-permute-done.7.refs_3_ = f32[64,512]{1,0:T(8,128)S(1)} collective-permute-done((f32[64,512]{1,0:T(8,128)S(1)}, f32[64,512]{1,0:T(8,128)S(1)}, u32[]{:S(2)}, u32[]{:S(2)}) %collective-permute-start.7) | collective-permute-done | bytes 131104 | tf_op jit(solution)/shard_map/ppermute | solution.py:340
  95.6 6.5 %collective-permute-done.6.refs_2_ = f32[64,512]{1,0:T(8,128)S(1)} collective-permute-done((f32[64,512]{1,0:T(8,128)S(1)}, f32[64,512]{1,0:T(8,128)S(1)}, u32[]{:S(2)}, u32[]{:S(2)}) %collective-permute-start.6) | collective-permute-done | bytes 131104 | tf_op jit(solution)/shard_map/ppermute | solution.py:340
  102.9 1.9 %shard_map.123 = bf16[16,64,64]{2,1,0:T(8,128)(2,1)} custom-call(s32[8,1]{1,0:T(8,128)} %copy.23.owner_ref, f32[64,512]{1,0:T(8,128)} %get-tuple-element.21.refs_0_, f32[64,512]{1,0:T(8,128)} %copy-done.5, f32[64,512]{1,0:T(8,128)} %copy-done.4, f32[64,512]{1,0:T(8,128)} %copy-done.3), custom_call_target="tpu_custom_call" | custom-call | tf_op jit(solution)/shard_map/pallas_call | solution.py:428
  105.9 7.9 %all_to_all.10 = bf16[8,128,64]{1,2,0:T(8,128)(2,1)S(1)} all-to-all(bf16[8,128,64]{1,2,0:T(8,128)(2,1)S(1)} %copy.24), channel_id=1, replica_groups=mesh['space'=8,'chan'=4] {'space'}, dimensions={0} | all-to-all | bytes 262144 | tf_op jit(solution)/shard_map/all_to_all | solution.py:434
  115.4 2.3 %shard_map.124 = (f32[27,32,128]{2,1,0:T(8,128)}, f32[8,64,128]{2,1,0:T(8,128)}) custom-call(s32[3]{0:T(128)} %pad_add_fusion.at_ref, f32[4,176,128]{2,1,0:T(8,128)} %copy-done, f32[4,176,128]{2,1,0:T(8,128)} %copy-done.2), custom_call_target="tpu_custom_call" | custom-call | tf_op jit(solution)/shard_map/pallas_call | solution.py:457
  (64 shorter events, 23.3 us)
Async XLA Ops:
  2.4 5.3 %copy-start.8 = (s32[8,512]{1,0:T(8,128)S(1)}, s32[8,512]{1,0:T(8,128)}, u32[]{:S(2)}) copy-start(s32[8,512]{1,0:T(8,128)} %mask_ref.1) | copy-start | bytes 49156
  2.4 12.2 %all-to-all-start = ((bf16[8,128,64]{1,2,0:T(8,128)(2,1)}), bf16[8,128,64]{1,2,0:T(8,128)(2,1)S(1)}, u32[]{:S(2)}, u32[]{:S(2)}) async-start(bf16[8,128,64]{1,2,0:T(8,128)(2,1)} %copy.20), calls=%async_computation | async-start | bytes 262144 | tf_op jit(solution)/shard_map/all_to_all | solution.py:365
  8.8 13.3 %collective-permute-start.1 = (bf16[4,128,64]{2,1,0:T(8,128)(2,1)S(1)}, bf16[4,128,64]{2,1,0:T(8,128)(2,1)S(1)}, u32[]{:S(2)}, u32[]{:S(2)}) collective-permute-start(bf16[4,128,64]{2,1,0:T(8,128)(2,1)S(1)} %get-tuple-element.16), channel_id=1, source_target_pairs={{4,0},{8,4},{12,8},{16,12},{20,16},{24,20},{28,24},{5,1},{9,5},{13... | collective-permute-start | bytes 196616 | tf_op jit(solution)/shard_map/ppermute | solution.py:363
  10.1 12.0 %collective-permute-start = (bf16[4,128,64]{2,1,0:T(8,128)(2,1)S(1)}, bf16[4,128,64]{2,1,0:T(8,128)(2,1)S(1)}, u32[]{:S(2)}, u32[]{:S(2)}) collective-permute-start(bf16[4,128,64]{2,1,0:T(8,128)(2,1)S(1)} %get-tuple-element.17), channel_id=1, source_target_pairs={{0,4},{4,8},{8,12},{12,16},{16,20},{20,24},{24,28},{1,5},{5,9},{9,... | collective-permute-start | bytes 196616 | tf_op jit(solution)/shard_map/ppermute | solution.py:362
  17.1 6.4 %collective-permute-start.4 = (bf16[64,512]{1,0:T(8,128)(2,1)}, bf16[64,512]{1,0:T(8,128)(2,1)S(1)}, u32[]{:S(2)}, u32[]{:S(2)}) collective-permute-start(bf16[64,512]{1,0:T(8,128)(2,1)} %shard_map.121.refs_0_), channel_id=1, source_target_pairs={{0,3},{1,2},{2,1},{3,0},{4,7},{5,6},{6,5},{7,4},{8,11},{9,10},{10,... | collective-permute-start | bytes 196616 | tf_op jit(solution)/shard_map/ppermute | solution.py:340
  20.7 6.6 %collective-permute-start.3 = (bf16[64,512]{1,0:T(8,128)(2,1)}, bf16[64,512]{1,0:T(8,128)(2,1)S(1)}, u32[]{:S(2)}, u32[]{:S(2)}) collective-permute-start(bf16[64,512]{1,0:T(8,128)(2,1)} %shard_map.121.refs_0_), channel_id=1, source_target_pairs={{0,2},{1,3},{2,0},{3,1},{4,6},{5,7},{6,4},{7,5},{8,10},{9,11},{10,... | collective-permute-start | bytes 196616 | tf_op jit(solution)/shard_map/ppermute | solution.py:340
  20.7 6.6 %collective-permute-start.2 = (bf16[64,512]{1,0:T(8,128)(2,1)}, bf16[64,512]{1,0:T(8,128)(2,1)S(1)}, u32[]{:S(2)}, u32[]{:S(2)}) collective-permute-start(bf16[64,512]{1,0:T(8,128)(2,1)} %shard_map.121.refs_0_), channel_id=1, source_target_pairs={{0,1},{1,0},{2,3},{3,2},{4,5},{5,4},{6,7},{7,6},{8,9},{9,8},{10,11... | collective-permute-start | bytes 196616 | tf_op jit(solution)/shard_map/ppermute | solution.py:340
  22.1 5.1 %copy-start.6 = (bf16[4,128,64]{2,1,0:T(8,128)(2,1)}, bf16[4,128,64]{2,1,0:T(8,128)(2,1)S(1)}, u32[]{:S(2)}) copy-start(bf16[4,128,64]{2,1,0:T(8,128)(2,1)S(1)} %collective-permute-done.1.next_ref) | copy-start | bytes 196612
  58.5 2.4 %collective-permute-start.8 = (f32[4,176,128]{2,1,0:T(8,128)}, f32[4,176,128]{2,1,0:T(8,128)S(1)}, u32[]{:S(2)}, u32[]{:S(2)}) collective-permute-start(f32[4,176,128]{2,1,0:T(8,128)} %get-tuple-element.10), channel_id=1, source_target_pairs={{0,4},{4,0},{8,12},{12,8},{16,20},{20,16},{24,28},{28,24},{1,5},{5... | collective-permute-start | bytes 1081352 | tf_op jit(solution)/shard_map/ppermute | solution.py:340
  62.0 5.5 %collective-permute-start.9 = (f32[176,128]{1,0:T(8,128)S(1)}, f32[176,128]{1,0:T(8,128)S(1)}, u32[]{:S(2)}, u32[]{:S(2)}) collective-permute-start(f32[176,128]{1,0:T(8,128)S(1)} %get-tuple-element.22), channel_id=1, source_target_pairs={{0,8},{4,12},{8,0},{12,4},{16,24},{20,28},{24,16},{28,20},{1,9},{5... | collective-permute-start | bytes 270344 | tf_op jit(solution)/shard_map/ppermute | solution.py:340
  63.7 5.6 %collective-permute-start.11 = (f32[176,128]{1,0:T(8,128)S(1)}, f32[176,128]{1,0:T(8,128)S(1)}, u32[]{:S(2)}, u32[]{:S(2)}) collective-permute-start(f32[176,128]{1,0:T(8,128)S(1)} %get-tuple-element.23), channel_id=1, source_target_pairs={{0,24},{4,28},{8,16},{12,20},{16,8},{20,12},{24,0},{28,4},{1,25},{... | collective-permute-start | bytes 270344 | tf_op jit(solution)/shard_map/ppermute | solution.py:340
  64.6 6.0 %collective-permute-start.10 = (f32[176,128]{1,0:T(8,128)S(1)}, f32[176,128]{1,0:T(8,128)S(1)}, u32[]{:S(2)}, u32[]{:S(2)}) collective-permute-start(f32[176,128]{1,0:T(8,128)S(1)} %get-tuple-element.24), channel_id=1, source_target_pairs={{0,16},{4,20},{8,24},{12,28},{16,0},{20,4},{24,8},{28,12},{1,17},{... | collective-permute-start | bytes 270344 | tf_op jit(solution)/shard_map/ppermute | solution.py:340
  70.7 3.7 %collective-permute-start.12 = (f32[16,128]{1,0:T(8,128)S(1)}, f32[16,128]{1,0:T(8,128)S(1)}, u32[]{:S(2)}, u32[]{:S(2)}) collective-permute-start(f32[16,128]{1,0:T(8,128)S(1)} %get-tuple-element.27), channel_id=1, source_target_pairs={{0,1},{1,0},{2,3},{3,2},{4,5},{5,4},{6,7},{7,6},{8,9},{9,8},{10,11... | collective-permute-start | bytes 24584 | tf_op jit(solution)/shard_map/ppermute | solution.py:340
  71.4 5.4 %collective-permute-start.14 = (f32[16,128]{1,0:T(8,128)S(1)}, f32[16,128]{1,0:T(8,128)S(1)}, u32[]{:S(2)}, u32[]{:S(2)}) collective-permute-start(f32[16,128]{1,0:T(8,128)S(1)} %get-tuple-element.28), channel_id=1, source_target_pairs={{0,3},{1,2},{2,1},{3,0},{4,7},{5,6},{6,5},{7,4},{8,11},{9,10},{10,... | collective-permute-start | bytes 24584 | tf_op jit(solution)/shard_map/ppermute | solution.py:340
  73.3 4.5 %collective-permute-start.13 = (f32[16,128]{1,0:T(8,128)S(1)}, f32[16,128]{1,0:T(8,128)S(1)}, u32[]{:S(2)}, u32[]{:S(2)}) collective-permute-start(f32[16,128]{1,0:T(8,128)S(1)} %get-tuple-element.29), channel_id=1, source_target_pairs={{0,2},{1,3},{2,0},{3,1},{4,6},{5,7},{6,4},{7,5},{8,10},{9,11},{10,... | collective-permute-start | bytes 24584 | tf_op jit(solution)/shard_map/ppermute | solution.py:340
  74.2 12.4 %copy-start.1 = (f32[4,64,512]{2,1,0:T(8,128)S(1)}, f32[4,64,512]{2,1,0:T(8,128)}, u32[]{:S(2)}) copy-start(f32[4,64,512]{2,1,0:T(8,128)} %get-tuple-element.8) | copy-start | bytes 1572868
  77.9 4.6 %collective-permute-start.16 = (f32[176,128]{1,0:T(8,128)S(1)}, f32[176,128]{1,0:T(8,128)S(1)}, u32[]{:S(2)}, u32[]{:S(2)}) collective-permute-start(f32[176,128]{1,0:T(8,128)S(1)} %get-tuple-element.26), channel_id=1, source_target_pairs={{0,16},{4,20},{8,24},{12,28},{16,0},{20,4},{24,8},{28,12},{1,17},{... | collective-permute-start | bytes 270344 | tf_op jit(solution)/shard_map/ppermute | solution.py:340
  79.5 4.5 %collective-permute-start.15 = (f32[176,128]{1,0:T(8,128)S(1)}, f32[176,128]{1,0:T(8,128)S(1)}, u32[]{:S(2)}, u32[]{:S(2)}) collective-permute-start(f32[176,128]{1,0:T(8,128)S(1)} %get-tuple-element.26), channel_id=1, source_target_pairs={{0,8},{4,12},{8,0},{12,4},{16,24},{20,28},{24,16},{28,20},{1,9},{5... | collective-permute-start | bytes 270344 | tf_op jit(solution)/shard_map/ppermute | solution.py:340
  81.1 5.4 %collective-permute-start.17 = (f32[176,128]{1,0:T(8,128)S(1)}, f32[176,128]{1,0:T(8,128)S(1)}, u32[]{:S(2)}, u32[]{:S(2)}) collective-permute-start(f32[176,128]{1,0:T(8,128)S(1)} %get-tuple-element.26), channel_id=1, source_target_pairs={{0,24},{4,28},{8,16},{12,20},{16,8},{20,12},{24,0},{28,4},{1,25},{... | collective-permute-start | bytes 270344 | tf_op jit(solution)/shard_map/ppermute | solution.py:340
  86.6 28.1 %collective-permute-start.18 = (f32[4,176,128]{2,1,0:T(8,128)S(1)}, f32[4,176,128]{2,1,0:T(8,128)S(1)}, u32[]{:S(2)}, u32[]{:S(2)}) collective-permute-start(f32[4,176,128]{2,1,0:T(8,128)S(1)} %pad_maximum_fusion.own_ref), channel_id=1, source_target_pairs={{0,4},{4,0},{8,12},{12,8},{16,20},{20,16},{24,28},{28,24},{1,5},{5... | collective-permute-start | bytes 1081352 | tf_op jit(solution)/shard_map/ppermute | solution.py:340
  87.4 8.2 %collective-permute-start.7 = (f32[64,512]{1,0:T(8,128)S(1)}, f32[64,512]{1,0:T(8,128)S(1)}, u32[]{:S(2)}, u32[]{:S(2)}) collective-permute-start(f32[64,512]{1,0:T(8,128)S(1)} %get-tuple-element.18), channel_id=1, source_target_pairs={{0,3},{1,2},{2,1},{3,0},{4,7},{5,6},{6,5},{7,4},{8,11},{9,10},{10,... | collective-permute-start | bytes 393224 | tf_op jit(solution)/shard_map/ppermute | solution.py:340
  88.8 13.4 %collective-permute-start.6 = (f32[64,512]{1,0:T(8,128)S(1)}, f32[64,512]{1,0:T(8,128)S(1)}, u32[]{:S(2)}, u32[]{:S(2)}) collective-permute-start(f32[64,512]{1,0:T(8,128)S(1)} %get-tuple-element.19), channel_id=1, source_target_pairs={{0,2},{1,3},{2,0},{3,1},{4,6},{5,7},{6,4},{7,5},{8,10},{9,11},{10,... | collective-permute-start | bytes 393224 | tf_op jit(solution)/shard_map/ppermute | solution.py:340
  89.9 12.3 %collective-permute-start.5 = (f32[64,512]{1,0:T(8,128)S(1)}, f32[64,512]{1,0:T(8,128)S(1)}, u32[]{:S(2)}, u32[]{:S(2)}) collective-permute-start(f32[64,512]{1,0:T(8,128)S(1)} %get-tuple-element.20), channel_id=1, source_target_pairs={{0,1},{1,0},{2,3},{3,2},{4,5},{5,4},{6,7},{7,6},{8,9},{9,8},{10,11... | collective-permute-start | bytes 393224 | tf_op jit(solution)/shard_map/ppermute | solution.py:340
  95.6 6.5 %copy-start.3 = (f32[64,512]{1,0:T(8,128)}, f32[64,512]{1,0:T(8,128)S(1)}, u32[]{:S(2)}) copy-start(f32[64,512]{1,0:T(8,128)S(1)} %collective-permute-done.7.refs_3_) | copy-start | bytes 393220
  (9 other events, 13.8 us)

commit v2 on v1

v2 whole, which is shorter than its diff:
```python
import functools

import jax
import jax.numpy as jnp
import numpy as np
from jax import lax
from jax.experimental import pallas as pl
from jax.experimental.pallas import tpu as pltpu
from jax.sharding import PartitionSpec as P

F32 = jnp.float32
BF16 = jnp.bfloat16
SIGNS = (-1, 0, 1)
LANES = 128
NT = (((1,), (1,)), ((), ()))
TN = (((0,), (0,)), ((), ()))
MIB = 1024 * 1024
PLANE = 80
STRIDE = 896
SPAN = 640


def vmem():
    return pl.BlockSpec(memory_space=pltpu.VMEM)


def smem():
    return pl.BlockSpec(memory_space=pltpu.SMEM)


def rim_lane(cell_y, cell_z):
    if 0 <= cell_y < 8 and 0 <= cell_z < 8:
        return 8 * cell_y + cell_z
    if 0 <= cell_z < 8:
        return 64 + 8 * (cell_y > 0) + cell_z
    if 0 <= cell_y < 8:
        return 80 + 8 * (cell_z > 0) + cell_y
    return 96 + 2 * (cell_y > 0) + (cell_z > 0)


def edge_table():
    table = np.zeros((10, LANES, LANES), np.float32)
    for place, (step_y, step_z) in enumerate((a, b) for a in SIGNS for b in SIGNS):
        for cell_y in range(8):
            for cell_z in range(8):
                far_y, far_z = cell_y + 8 * step_y, cell_z + 8 * step_z
                if -1 <= far_y <= 8 and -1 <= far_z <= 8:
                    table[place, 8 * cell_y + cell_z, rim_lane(far_y, far_z)] = 1
    return table


def shift_table():
    table = np.zeros((3, 2, 10, 8, 2, LANES), np.float32)
    for place, step_z in enumerate(SIGNS):
        for cell_y in range(10):
            for cell_z in range(8):
                for plane in range(2):
                    table[place, plane, cell_y, cell_z, plane, rim_lane(cell_y - 1, cell_z + step_z)] = 1
    return table.reshape(3 * 2 * PLANE, 2 * LANES)


def spread_table():
    table = np.zeros((8, 64, 8, PLANE), np.float32)
    for x in range(8):
        for cell in range(64):
            table[x, cell, x, cell] = 1
    return table.reshape(512, SPAN)


def octant_table():
    table = np.zeros((8, PLANE, 8, 2, 64), np.float32)
    for x in range(8):
        for y in range(8):
            for z in range(8):
                octant = 4 * (x % 2) + 2 * (y % 2) + z % 2
                table[x, 8 * y + z, octant, :, 16 * (x // 2) + 4 * (y // 2) + z // 2] = 1
    return table.reshape(SPAN, 8 * LANES)


def low_half(rows):
    return lax.broadcasted_iota(jnp.int32, (rows, LANES), 1) < 64


def swap_halves(tile):
    return pltpu.roll(tile, 64, 1)


def prepare_kernel(head_ref, tail_ref, mask_ref, cot_ref, head_out, tail_out, cot_out):
    edge, channels = head_ref.shape[0], head_ref.shape[1]
    low = low_half(channels)
    for pair in range(edge // 2):
        one, two = 2 * pair, 2 * pair + 1
        first = head_ref[one].astype(F32) * mask_ref[one : one + 1, :LANES].astype(F32)
        second = head_ref[two].astype(F32) * mask_ref[two : two + 1, :LANES].astype(F32)
        head_out[pair] = jnp.where(low, first, swap_halves(second)).astype(BF16)
        first = tail_ref[one].astype(F32) * mask_ref[edge + one : edge + one + 1, -LANES:].astype(F32)
        second = tail_ref[two].astype(F32) * mask_ref[edge + two : edge + two + 1, -LANES:].astype(F32)
        tail_out[pair] = jnp.where(low, swap_halves(first), second).astype(BF16)
    for peer in range(cot_out.shape[0]):
        pair = [cot_ref[2 * peer].astype(F32), cot_ref[2 * peer + 1].astype(F32)]
        cot_out[peer] = jnp.concatenate(pair, axis=1).astype(BF16)


def pick_kernel(owner_ref, returned_ref, out_ref, rank_ref):
    blocks = owner_ref.shape[0]
    low = low_half(out_ref.shape[0])
    for pair in range(blocks // 2):
        rows = []
        for side in range(2):
            block = 2 * pair + side
            owner = owner_ref[block, 0]
            rank = jnp.int32(0)
            for earlier in range(block):
                rank = rank + (owner_ref[earlier, 0] == owner).astype(jnp.int32)
            rank_ref[0, block] = owner
            rank_ref[1, block] = rank
            tile = returned_ref[owner].astype(F32)
            rows.append(jnp.where(rank == side, tile, swap_halves(tile)))
        out_ref[:, pair * LANES : (pair + 1) * LANES] = jnp.where(low, rows[0], rows[1]).astype(BF16)


def route_kernel(rank_ref, *refs):
    out_ref = refs[-1]
    blocks = rank_ref.shape[1]
    half = lax.broadcasted_iota(jnp.int32, (out_ref.shape[1], LANES), 1) // 64
    out_ref[...] = jnp.zeros_like(out_ref)
    for block in range(blocks):
        lanes = slice(block // 2 * LANES, (block // 2 + 1) * LANES)
        total = refs[0][:, lanes]
        for ref in refs[1:-1]:
            total = total + ref[:, lanes]
        owner, rank = rank_ref[0, block], rank_ref[1, block]
        tile = jnp.where(rank == block % 2, total, swap_halves(total))
        out_ref[owner] += jnp.where(half == rank, tile, 0.0).astype(BF16)


def forward_kernel(
    axis,
    nbr_ref,
    feat_ref,
    mask_ref,
    prev_ref,
    next_ref,
    wconv_ref,
    edge_ref,
    shift_ref,
    spread_ref,
    octant_ref,
    pre_out,
    octs_out,
    patches_out,
    planes,
    weights,
    own_s,
    hidden_s,
    same_from,
    same_code,
    side_from,
    side_code,
):
    blocks, channels = feat_ref.shape[0], feat_ref.shape[1]
    edge = blocks // 2
    width = wconv_ref.shape[1]
    me = lax.axis_index(axis)
    own_rows = pl.ds(pl.multiple_of(me * width, width), width)
    low = low_half(channels)
    halo = 10 * blocks
    dummy = 11 * blocks

    same, side = jnp.int32(0), jnp.int32(0)
    for block in range(blocks):
        for column in range(26):
            position = column + (column >= 13)
            source = nbr_ref[block, column]
            there = (source >= 0).astype(jnp.int32)
            step, table = position // 9, position % 9
            if step == 1:
                same_from[same] = source
                same_code[same] = block * 16 + table
                same = same + there
            else:
                side_from[side] = source
                side_code[side] = (block * 10 + (9 if step else 0)) * 32 + table * 2 + step // 2
                side = side + there

    def two_planes(first, tile):
        planes[first] = jnp.where(low, tile, 0.0).astype(BF16)
        planes[first + 1] = jnp.where(low, swap_halves(tile), 0.0).astype(BF16)

    zero_plane = jnp.zeros((channels, LANES), BF16)
    planes[dummy] = zero_plane
    for block in range(blocks):
        keep = mask_ref[block : block + 1, :].astype(F32)
        masked = feat_ref[block].astype(F32) * keep
        planes[10 * block] = zero_plane
        planes[10 * block + 9] = zero_plane
        for pair in range(4):
            two_planes(10 * block + 1 + 2 * pair, masked[:, pair * LANES : (pair + 1) * LANES])
    for pair in range(edge // 2):
        two_planes(halo + 2 * pair, prev_ref[pair].astype(F32))
        two_planes(halo + edge + 2 * pair, next_ref[pair].astype(F32))

    def same_layer(item, carry):
        code = same_code[item]
        block = lax.shift_right_logical(code, 4)
        table = edge_ref[code & 15]
        cells = planes[pl.ds(same_from[item] * 10 + 1, 8)].reshape(8 * channels, LANES)
        moved = jnp.dot(cells, table, preferred_element_type=F32).astype(BF16)
        planes[pl.ds(block * 10 + 1, 8)] += moved.reshape(8, channels, LANES)
        return carry

    lax.fori_loop(0, same, same_layer, 0)
    for extra in range(3):
        side_from[side + extra] = dummy - halo + blocks
        side_code[side + extra] = dummy * 32 + 18

    def side_layer(item, carry):
        results = []
        for extra in range(4):
            source, code = side_from[4 * item + extra], side_code[4 * item + extra]
            own = source * 10 + jnp.where(code & 1 == 1, 1, 8)
            cells = planes[jnp.where(source < blocks, own, halo + source - blocks)]
            table = edge_ref[lax.shift_right_logical(code, 1) & 15]
            moved = jnp.dot(cells, table, preferred_element_type=F32).astype(BF16)
            results.append((lax.shift_right_logical(code, 5), moved))
        for place, moved in results:
            planes[place] += moved
        return carry

    lax.fori_loop(0, lax.shift_right_logical(side + 3, 2), side_layer, 0)

    for k in range(27):
        weights[(k // 3) * width : (k // 3 + 1) * width, (k % 3) * channels : (k % 3 + 1) * channels] = wconv_ref[k]

    for block in range(0, blocks, 2):
        for plane in range(0, 10, 2):
            first, second = block * 10 + plane, block * 10 + 10 + plane
            source = jnp.concatenate(
                [
                    jnp.concatenate([planes[first], planes[first + 1]], axis=1),
                    jnp.concatenate([planes[second], planes[second + 1]], axis=1),
                ],
                axis=0,
            )
            window = lax.dot_general(shift_ref[...], source, NT, preferred_element_type=F32).astype(BF16)
            for j in range(3):
                for half in range(2):
                    row = (block + half) * STRIDE + plane * PLANE
                    patches_out[row : row + 2 * PLANE, j * channels : (j + 1) * channels] = window[
                        j * 2 * PLANE : (j + 1) * 2 * PLANE, half * channels : (half + 1) * channels
                    ]
    for block in range(blocks):
        row = block * STRIDE + 10 * PLANE
        patches_out[row : (block + 1) * STRIDE, :] = jnp.zeros((STRIDE - 10 * PLANE, 3 * channels), BF16)

    for block in range(blocks):
        own_s[block * width : (block + 1) * width, :] = feat_ref[block, own_rows, :]
    own = jnp.dot(own_s[...], spread_ref[...], preferred_element_type=F32)
    keeps = jnp.dot(mask_ref[...].astype(F32).astype(BF16), spread_ref[...], preferred_element_type=F32)
    for block in range(blocks):
        rows = slice(block * STRIDE, (block + 1) * STRIDE)
        here = slice(block * width, (block + 1) * width)
        sums = lax.dot_general(weights[...], patches_out[rows, :], NT, preferred_element_type=F32)
        keep = keeps[block : block + 1]
        pre = own[here] * keep + sums[:width, :SPAN]
        for k in range(1, 9):
            moved = pltpu.roll(sums[k * width : (k + 1) * width], STRIDE - (k // 3) * PLANE - (k % 3) * 8, 1)
            pre = pre + moved[:, :SPAN]
        pre_out[here, :] = pre
        hidden_s[here, :] = (keep * (pre * (1.0 / (1.0 + jnp.exp(-pre))))).astype(BF16)

    split_up = jnp.dot(hidden_s[...], octant_ref[...], preferred_element_type=F32)
    low = low_half(width)
    for octant in range(8):
        lanes = slice(octant * LANES, (octant + 1) * LANES)
        for pair in range(blocks // 2):
            even = split_up[2 * pair * width : (2 * pair + 1) * width, lanes]
            odd = split_up[(2 * pair + 1) * width : (2 * pair + 2) * width, lanes]
            octs_out[octant * width : (octant + 1) * width, pair * LANES : (pair + 1) * LANES] = jnp.where(
                low, even, odd
            ).astype(BF16)


def down_kernel(axes, shards, octs_ref, wdown_ref, *refs):
    dps = refs[:shards]
    pieces_out, grads_out, dp_out, spread, sums = refs[shards:]
    me = lax.axis_index(axes[1])
    core = lax.axis_index(axes[0]) & 1
    channels, total = wdown_ref.shape[2], wdown_ref.shape[1]
    width = channels // shards
    share = total // shards
    for k in range(shards):
        theirs = pl.multiple_of((me ^ k) * share, share)
        dp_out[pl.ds(theirs, share), :] = dps[k][...]
    grads = lax.dot_general(dp_out[...], octs_ref[...], NT, preferred_element_type=F32)
    sums[:, : 2 * LANES] = grads
    for k in range(shards):
        rows = pl.ds(pl.multiple_of((me ^ k) * share, share), share)
        low, high = sums[rows, :LANES], sums[rows, LANES : 2 * LANES]
        grads_out[k, core] = low
        grads_out[k, 1 - core] = high
    spread[...] = jnp.zeros_like(spread)
    for octant in range(8):
        rows = pl.ds(pl.multiple_of(octant * channels + me * width, width), width)
        spread[rows, :] = octs_ref[octant * width : (octant + 1) * width, :]
    down_weights = jnp.concatenate([wdown_ref[octant] for octant in range(8)], axis=1)
    sums[...] = jnp.dot(down_weights, spread[...], preferred_element_type=F32)
    for k in range(shards):
        pieces_out[k] = sums[pl.ds(pl.multiple_of((me ^ k) * share, share), share), :]


def backward_kernel(
    axes, dp_ref, wdown_ref, mask_ref, pre_ref, spread_ref, octant_ref, patches_ref, keep_out, give_out, dh_s, dhi, dlo, d9, conv_s
):
    blocks = mask_ref.shape[0]
    channels = wdown_ref.shape[2]
    width = pre_ref.shape[0] // blocks
    me = lax.axis_index(axes[1])
    core = lax.axis_index(axes[0]) & 1
    own_rows = pl.ds(pl.multiple_of(me * width, width), width)
    low = low_half(width)

    for octant in range(8):
        dh_s[octant] = lax.dot_general(wdown_ref[octant], dp_ref[...], TN, preferred_element_type=F32)
    for octant in range(8):
        lanes = slice(octant * LANES, (octant + 1) * LANES)
        for pair in range(blocks // 2):
            tile = dh_s[octant, own_rows, pair * LANES : (pair + 1) * LANES]
            high = tile.astype(BF16).astype(F32)
            rest = tile - high
            even = slice(2 * pair * width, (2 * pair + 1) * width)
            odd = slice((2 * pair + 1) * width, (2 * pair + 2) * width)
            dhi[even, lanes] = jnp.where(low, high, 0.0).astype(BF16)
            dhi[odd, lanes] = jnp.where(low, 0.0, high).astype(BF16)
            dlo[even, lanes] = jnp.where(low, rest, 0.0).astype(BF16)
            dlo[odd, lanes] = jnp.where(low, 0.0, rest).astype(BF16)
    dhidden = lax.dot_general(dhi[...], octant_ref[...], NT, preferred_element_type=F32)
    dhidden = dhidden + lax.dot_general(dlo[...], octant_ref[...], NT, preferred_element_type=F32)
    keeps = jnp.dot(mask_ref[...].astype(F32).astype(BF16), spread_ref[...], preferred_element_type=F32)

    blank = jnp.zeros((width, STRIDE - SPAN), F32)
    for block in range(blocks):
        rows = slice(block * width, (block + 1) * width)
        pre = pre_ref[rows, :]
        gate = 1.0 / (1.0 + jnp.exp(-pre))
        dpre = dhidden[rows] * keeps[block : block + 1] * gate * (1.0 + pre * (1.0 - gate))
        dpre = jnp.concatenate([dpre, blank], axis=1)
        lanes = slice(block * STRIDE, (block + 1) * STRIDE)
        for k in range(9):
            moved = pltpu.roll(dpre, (k // 3) * PLANE + (k % 3) * 8, 1) if k else dpre
            d9[k * width : (k + 1) * width, lanes] = moved.astype(BF16)

    for j in range(3):
        part = jnp.dot(d9[...], patches_ref[:, j * channels : (j + 1) * channels], preferred_element_type=F32)
        for k in range(9):
            at = (3 * k + j) * width
            conv_s[at : at + width] = part[k * width : (k + 1) * width]
    half = keep_out.shape[0]
    keep_out[...] = conv_s[pl.ds(pl.multiple_of(core * half, 8), half), :]
    give_out[...] = conv_s[pl.ds(pl.multiple_of((1 - core) * half, 8), half), :]


def finish_kernel(axes, shards, half, own_ref, other_ref, conv_ref, down_ref, both):
    me = lax.axis_index(axes[1])
    core = lax.axis_index(axes[0]) & 1
    share = down_ref.shape[1]
    width = LANES // shards
    both[core] = own_ref[...]
    both[1 - core] = other_ref[...]
    conv_ref[:half] = both[0, :half]
    conv_ref[half:] = both[1, :half]
    group = lax.broadcasted_iota(jnp.int32, (share, LANES), 1) // width
    for octant in range(8):
        result = jnp.zeros((share, LANES), F32)
        for k in range(shards):
            source = me ^ k
            row = half + k * share
            tile = both[octant // shards, row : row + share, :]
            turned = pltpu.roll(tile, ((source - octant % shards + shards) & (shards - 1)) * width, 1)
            result = jnp.where(group == source, turned, result)
        down_ref[octant] = result


def exchange(values, axis, step):
    count = lax.axis_size(axis)
    return lax.ppermute(values, axis, [(i, i ^ step) for i in range(count)])


def local(features, voxel_mask, neighbors, w_conv, w_down, coarse_owner, cotangent):
    blocks, channels = features.shape[0], features.shape[1]
    edge = blocks // 2
    peers = lax.axis_size("space")
    shards = lax.axis_size("chan")
    axes = ("space", "chan")
    width = w_conv.shape[1]
    total = w_down.shape[1]
    share = total // shards
    capacity = cotangent.shape[0] // peers
    lanes = blocks * 64
    tables = [jnp.asarray(t(), BF16) for t in (edge_table, shift_table, spread_table, octant_table)]
    edges, shifts, spreads, octants = tables

    head, tail, packed = pl.pallas_call(
        prepare_kernel,
        grid=(1,),
        out_shape=[
            jax.ShapeDtypeStruct((edge // 2, channels, LANES), BF16),
            jax.ShapeDtypeStruct((edge // 2, channels, LANES), BF16),
            jax.ShapeDtypeStruct((peers, share, capacity * 64), BF16),
        ],
        in_specs=[
            pl.BlockSpec((edge, channels, LANES), lambda i: (0, 0, 0)),
            pl.BlockSpec((edge, channels, LANES), lambda i: (1, 0, 3)),
            pl.BlockSpec(voxel_mask.shape, lambda i: (0, 0)),
            pl.BlockSpec(cotangent.shape, lambda i: (0, 0, 0)),
        ],
        out_specs=[
            pl.BlockSpec((edge // 2, channels, LANES), lambda i: (0, 0, 0)),
            pl.BlockSpec((edge // 2, channels, LANES), lambda i: (0, 0, 0)),
            pl.BlockSpec((peers, share, capacity * 64), lambda i: (0, 0, 0)),
        ],
    )(features, features, voxel_mask, cotangent)
    ends = peers - 1
    before = lax.ppermute(tail, "space", [(i, i + 1) for i in range(ends)])
    after = lax.ppermute(head, "space", [(i + 1, i) for i in range(ends)])
    returned = lax.all_to_all(packed, "space", split_axis=0, concat_axis=0, tiled=True)

    dpiece, place = pl.pallas_call(
        pick_kernel,
        out_shape=[
            jax.ShapeDtypeStruct((share, lanes), BF16),
            jax.ShapeDtypeStruct((2, blocks), jnp.int32),
        ],
        in_specs=[smem(), vmem()],
        out_specs=[vmem(), smem()],
    )(coarse_owner, returned)
    dpieces = [dpiece] + [exchange(dpiece, "chan", k) for k in range(1, shards)]

    pre, octs, patches = pl.pallas_call(
        functools.partial(forward_kernel, "chan"),
        out_shape=[
            jax.ShapeDtypeStruct((blocks * width, SPAN), F32),
            jax.ShapeDtypeStruct((8 * width, lanes), BF16),
            jax.ShapeDtypeStruct((blocks * STRIDE, 3 * channels), BF16),
        ],
        in_specs=[smem()] + [vmem()] * 9,
        out_specs=[vmem()] * 3,
        scratch_shapes=[
            pltpu.VMEM((11 * blocks + 1, channels, LANES), BF16),
            pltpu.VMEM((9 * width, 3 * channels), BF16),
            pltpu.VMEM((blocks * width, 512), BF16),
            pltpu.VMEM((blocks * width, SPAN), BF16),
            pltpu.SMEM((8 * blocks + 8,), jnp.int32),
            pltpu.SMEM((8 * blocks + 8,), jnp.int32),
            pltpu.SMEM((18 * blocks + 8,), jnp.int32),
            pltpu.SMEM((18 * blocks + 8,), jnp.int32),
        ],
        compiler_params=pltpu.CompilerParams(vmem_limit_bytes=40 * MIB),
    )(neighbors, features, voxel_mask, before, after, w_conv, edges, shifts, spreads, octants)

    pieces, down_grad, dp_all = pl.pallas_call(
        functools.partial(down_kernel, axes, shards),
        out_shape=[
            jax.ShapeDtypeStruct((shards, share, lanes), F32),
            jax.ShapeDtypeStruct((shards, 2, share, LANES), F32),
            jax.ShapeDtypeStruct((total, lanes), BF16),
        ],
        in_specs=[vmem()] * (2 + shards),
        out_specs=[vmem()] * 3,
        scratch_shapes=[pltpu.VMEM((8 * channels, lanes), BF16), pltpu.VMEM((total, lanes), F32)],
        compiler_params=pltpu.CompilerParams(vmem_limit_bytes=24 * MIB),
    )(octs, w_down, *dpieces)
    downs = [down_grad[0]] + [exchange(down_grad[k], "chan", k) for k in range(1, shards)]
    parts = [pieces[0]] + [exchange(pieces[k], "chan", k) for k in range(1, shards)]

    half = 27 * width // 2
    conv_keep, conv_give = pl.pallas_call(
        functools.partial(backward_kernel, axes),
        out_shape=[jax.ShapeDtypeStruct((half, channels), F32)] * 2,
        in_specs=[vmem()] * 7,
        out_specs=[vmem()] * 2,
        scratch_shapes=[
            pltpu.VMEM((8, channels, lanes), F32),
            pltpu.VMEM((blocks * width, 8 * LANES), BF16),
            pltpu.VMEM((blocks * width, 8 * LANES), BF16),
            pltpu.VMEM((9 * width, blocks * STRIDE), BF16),
            pltpu.VMEM((27 * width, channels), F32),
        ],
        compiler_params=pltpu.CompilerParams(vmem_limit_bytes=40 * MIB),
    )(dp_all, w_down, voxel_mask, pre, spreads, octants, patches)

    outgoing = pl.pallas_call(
        route_kernel,
        out_shape=jax.ShapeDtypeStruct((peers, share, capacity * 64), BF16),
        in_specs=[smem()] + [vmem()] * shards,
        out_specs=vmem(),
    )(place, *parts)
    coarse = lax.all_to_all(outgoing, "space", split_axis=0, concat_axis=0, tiled=True)
    coarse = coarse.reshape(peers, share, capacity, 64).transpose(0, 2, 1, 3).reshape(peers * capacity, share, 64)

    keep = jnp.concatenate([conv_keep] + [d[0] for d in downs])
    give = jnp.concatenate([conv_give] + [d[1] for d in downs])
    mine = keep + exchange(give, "space", 1)
    cut = mine.shape[0] // 2
    first, second = mine[:cut], mine[cut:]
    steps = []
    step = 2
    while step < peers:
        steps.append(step)
        step *= 2
    for near, far in zip(steps, reversed(steps)):
        first = first + exchange(first, "space", near)
        second = second + exchange(second, "space", far)
    mine = jnp.concatenate([first, second])
    other = exchange(mine, "space", 1)
    conv_sum, down_sum = pl.pallas_call(
        functools.partial(finish_kernel, axes, shards, half),
        out_shape=[
            jax.ShapeDtypeStruct((27 * width, channels), F32),
            jax.ShapeDtypeStruct((8, share, channels), F32),
        ],
        in_specs=[vmem(), vmem()],
        out_specs=[vmem()] * 2,
        scratch_shapes=[pltpu.VMEM((2,) + mine.shape, F32)],
    )(mine, other)
    return coarse, conv_sum.reshape(27, width, channels), down_sum


def solution(mesh):
    in_specs = (
        P("space", None, None),
        P("space", None),
        P("space", None),
        P(None, "chan", None),
        P(),
        P("space", None),
        P("space", "chan", None),
    )
    out_specs = (P("space", "chan", None), P(None, "chan", None), P(None, "chan", None))
    return jax.shard_map(local, mesh=mesh, in_specs=in_specs, out_specs=out_specs, check_vma=False)
```

time: 118 us -> 91.6 us (0.78); the launches traced: 118 us -> 90.1 us
  Pallas kernels: 36 us -> 21.3 us
  waiting for transfers between devices: 30.8 us -> 21.3 us
  blocking collectives: 7.92 us -> 0 us
  local copies, waits for them, and re-layouts: 9.33 us -> 13.1 us
  starting transfers between devices: 30 us -> 32.6 us
  other arithmetic: 2.85 us -> 0.92 us
    ppermute x17 -> x15, waiting for transfers between devices: 30.8 us -> 16 us  [exchange(): return lax.ppermute(values, axis, [(i, i ^ step) for i in range(count)])]
    pallas_call x4 -> x7, Pallas kernels: 36 us -> 21.3 us  [the longest x1 7.21 us: local(): pl.pallas_call(functools.partial(forward_kernel, 'chan'), out_shape=[jax....]
    all_to_all x1 -> x0, blocking collectives: 7.92 us -> none  [local(): lax.all_to_all(outgoing.reshape(peers, capacity * share, 64), 'space', sp...]
    unnamed x28 -> x41, local copies, waits for them, and re-layouts: 4.84 us -> 12.2 us
    all_to_all x1 -> x2, waiting for transfers between devices: 0.01 us -> 5.35 us  [the longest x1 4.85 us: local(): lax.all_to_all(outgoing, 'space', split_axis=0, concat_axis=0, tiled=True)]
    all_to_all x1 -> x2, starting transfers between devices: 5.3 us -> 8.71 us  [the longest x1 5.17 us: local(): lax.all_to_all(packed, 'space', split_axis=0, concat_axis=0, tiled=True)]
    reshape x2 -> x0, local copies, waits for them, and re-layouts: 2.8 us -> none  [the longest x1 1.73 us: local(): cotangent.reshape(peers, capacity * share, 64)]
    ppermute x17 -> x15, starting transfers between devices: 20.4 us -> 20.2 us  [exchange(): return lax.ppermute(values, axis, [(i, i ^ step) for i in range(count)])]
  transfers between devices with their start and end apart: 20 -> 19, of which waited for: 14 -> 7; matrix products, arithmetic and copies ran while one was open for 5% -> 3% of each run, Pallas kernels for 3% -> 18%
where the time goes in v2:
time: 91.6 us; the launch traced here: 90.1 us
  starting transfers between devices  32.6 us (36%)
  Pallas kernels  21.3 us (23%)
  waiting for transfers between devices  21.3 us (23%)
  local copies, waits for them, and re-layouts  13.1 us (14%)
  other arithmetic  0.92 us (1%)
    ppermute x15, starting transfers between devices, exchange(): return lax.ppermute(values, axis, [(i, i ^ step) for i in range(count)])  20.2 us
    ppermute x15, waiting for transfers between devices, exchange(): return lax.ppermute(values, axis, [(i, i ^ step) for i in range(count)])  16 us
    unnamed x41, local copies, waits for them, and re-layouts  12.2 us
    pallas_call x1, Pallas kernels, local(): pl.pallas_call(functools.partial(forward_kernel, 'chan'), out_shape=[jax....  7.21 us
    pallas_call x1, Pallas kernels, local(): pl.pallas_call(functools.partial(backward_kernel, axes), out_shape=[jax.S...  5.63 us
    all_to_all x1, starting transfers between devices, local(): lax.all_to_all(packed, 'space', split_axis=0, concat_axis=0, tiled=True)  5.17 us
    all_to_all x1, waiting for transfers between devices, local(): lax.all_to_all(outgoing, 'space', split_axis=0, concat_axis=0, tiled=True)  4.85 us
    all_to_all x1, starting transfers between devices, local(): lax.all_to_all(outgoing, 'space', split_axis=0, concat_axis=0, tiled=True)  3.54 us
  transfers between devices with their start and end apart: 19, of which 7 were waited for; matrix products, arithmetic and copies ran while one was open for 3% of the time, Pallas kernels for 18%

profile of v2, /device:TPU:0, one launch (start us, length us, event | category | flops | bytes accessed | tf_op | source)
XLA Modules:
  0.0 90.1 jit_solution(15626746410033924745)
XLA Ops:
  0.7 2.0 %shard_map.130 = (bf16[2,128,128]{2,1,0:T(8,128)(2,1)}, bf16[2,128,128]{2,1,0:T(8,128)(2,1)}, bf16[8,64,128]{2,1,0:T(8,128)(2,1)}) custom-call(bf16[8,128,512]{2,1,0:T(8,128)(2,1)} %feat_ref.1, bf16[8,128,512]{2,1,0:T(8,128)(2,1)} %feat_ref.1, s32[8,512]{1,0:T(8,128)} %mask_ref.5, bf16[16,64,64]{2,1,0:T(8,128)(2,1)} %cot_ref.1), custom_call_target="tpu_custom_call" | custom-call | tf_op jit(solution)/shard_map/pallas_call | solution.py:403
  2.7 5.2 %all-to-all-start = ((bf16[8,64,128]{2,1,0:T(8,128)(2,1)}), bf16[8,64,128]{2,1,0:T(8,128)(2,1)S(1)}, u32[]{:S(2)}, u32[]{:S(2)}) async-start(bf16[8,64,128]{2,1,0:T(8,128)(2,1)} %get-tuple-element.18), calls=%async_computation | async-start | bytes 262144 | tf_op jit(solution)/shard_map/all_to_all | solution.py:426
  7.8 2.4 %collective-permute-start = (bf16[2,128,128]{2,1,0:T(8,128)(2,1)}, bf16[2,128,128]{2,1,0:T(8,128)(2,1)S(1)}, u32[]{:S(2)}, u32[]{:S(2)}) collective-permute-start(bf16[2,128,128]{2,1,0:T(8,128)(2,1)} %get-tuple-element.20), channel_id=1, source_target_pairs={{0,4},{4,8},{8,12},{12,16},{16,20},{20,24},{24,28},{1,5},{5,9},{9,... | collective-permute-start | bytes 196616 | tf_op jit(solution)/shard_map/ppermute | solution.py:424
  10.2 1.3 %collective-permute-start.1 = (bf16[2,128,128]{2,1,0:T(8,128)(2,1)}, bf16[2,128,128]{2,1,0:T(8,128)(2,1)S(1)}, u32[]{:S(2)}, u32[]{:S(2)}) collective-permute-start(bf16[2,128,128]{2,1,0:T(8,128)(2,1)} %get-tuple-element.21), channel_id=1, source_target_pairs={{4,0},{8,4},{12,8},{16,12},{20,16},{24,20},{28,24},{5,1},{9,5},{13... | collective-permute-start | bytes 196616 | tf_op jit(solution)/shard_map/ppermute | solution.py:425
  11.5 1.3 %copy.14.owner_ref = s32[8,1]{1,0:T(8,128)} copy(s32[8,1]{0,1:T(1,128)} %param.16) | data formatting | bytes 64 | tf_op args[5]
  14.0 1.6 %shard_map.131 = (bf16[64,512]{1,0:T(8,128)(2,1)}, s32[2,8]{1,0:T(2,128)}) custom-call(s32[8,1]{1,0:T(8,128)} %copy.14.owner_ref, bf16[8,64,128]{2,1,0:T(8,128)(2,1)} %copy-done.13), custom_call_target="tpu_custom_call" | custom-call | tf_op jit(solution)/shard_map/pallas_call | solution.py:428
  15.7 3.7 %collective-permute-start.4 = (bf16[64,512]{1,0:T(8,128)(2,1)}, bf16[64,512]{1,0:T(8,128)(2,1)S(1)}, u32[]{:S(2)}, u32[]{:S(2)}) collective-permute-start(bf16[64,512]{1,0:T(8,128)(2,1)} %get-tuple-element.23.refs_0_), channel_id=1, source_target_pairs={{0,3},{1,2},{2,1},{3,0},{4,7},{5,6},{6,5},{7,4},{8,11},{9,10},{10,... | collective-permute-start | bytes 196616 | tf_op jit(solution)/shard_map/ppermute | solution.py:386
  20.1 1.2 %copy-done = bf16[8,128,512]{2,1,0:T(8,128)(2,1)S(1)} copy-done((bf16[8,128,512]{2,1,0:T(8,128)(2,1)S(1)}, bf16[8,128,512]{2,1,0:T(8,128)(2,1)}, u32[]{:S(2)}) %copy-start) | copy-done | bytes 1048600
  21.4 1.3 %copy-done.1 = bf16[640,1024]{1,0:T(8,128)(2,1)S(1)} copy-done((bf16[640,1024]{1,0:T(8,128)(2,1)S(1)}, bf16[640,1024]{1,0:T(8,128)(2,1)}, u32[]{:S(2)}) %copy-start.1) | copy-done | bytes 1310744
  22.7 1.1 %copy-done.2 = bf16[512,640]{1,0:T(8,128)(2,1)S(1)} copy-done((bf16[512,640]{1,0:T(8,128)(2,1)S(1)}, bf16[512,640]{1,0:T(8,128)(2,1)}, u32[]{:S(2)}) %copy-start.2) | copy-done | bytes 655384
  28.0 7.2 %shard_map.132 = (f32[256,640]{1,0:T(8,128)S(1)}, bf16[256,512]{1,0:T(8,128)(2,1)S(1)}, bf16[7168,384]{1,0:T(8,128)(2,1)S(1)}) custom-call(s32[8,26]{1,0:T(8,128)S(1)} %copy-done.11, bf16[8,128,512]{2,1,0:T(8,128)(2,1)S(1)} %copy-done, s32[8,512]{1,0:T(8,128)S(1)} %copy-done.8, bf16[2,128,128]{2,1,0:T(8,128)(2,1)S(1)} %collective-permute-done.prev_ref, ...), custom_call_target="tpu_custom_call" | custom-call | tf_op jit(solution)/shard_map/pallas_call | solution.py:439
  36.8 3.7 %collective-permute-start.10 = (f32[2,64,128]{2,1,0:T(8,128)S(1)}, f32[2,64,128]{2,1,0:T(8,128)S(1)}, u32[]{:S(2)}, u32[]{:S(2)}) collective-permute-start(f32[2,64,128]{2,1,0:T(8,128)S(1)} %get-tuple-element.43), channel_id=1, source_target_pairs={{0,3},{1,2},{2,1},{3,0},{4,7},{5,6},{6,5},{7,4},{8,11},{9,10},{10,... | collective-permute-start | bytes 196616 | tf_op jit(solution)/shard_map/ppermute | solution.py:386
  41.3 5.6 %shard_map.135 = (f32[432,128]{1,0:T(8,128)S(1)}, f32[432,128]{1,0:T(8,128)S(1)}) custom-call(bf16[256,512]{1,0:T(8,128)(2,1)S(1)} %get-tuple-element.25.dp_ref, bf16[8,256,128]{2,1,0:T(8,128)(2,1)S(1)} %copy-done.4, s32[8,512]{1,0:T(8,128)S(1)} %copy-done.9, f32[256,640]{1,0:T(8,128)S(1)} %get-tuple-element.26.pre_ref, bf16[512,640]{1,0:T(8,128)(2,1)S(1)} %copy-done.3, ...), custom_call_target="tpu_custom_call" | custom-call | tf_op jit(solution)/shard_map/pallas_call | solution.py:477
  47.5 1.3 %collective-permute-done.11 = f32[688,128]{1,0:T(8,128)S(1)} collective-permute-done((f32[688,128]{1,0:T(8,128)S(1)}, f32[688,128]{1,0:T(8,128)S(1)}, u32[]{:S(2)}, u32[]{:S(2)}) %collective-permute-start.11) | collective-permute-done | bytes 352288 | tf_op jit(solution)/shard_map/ppermute | solution.py:386
  48.9 4.4 %collective-permute-start.12 = (f32[344,128]{1,0:T(8,128)S(1)}, f32[344,128]{1,0:T(8,128)S(1)}, u32[]{:S(2)}, u32[]{:S(2)}) collective-permute-start(f32[344,128]{1,0:T(8,128)S(1)} %get-tuple-element.39), channel_id=1, source_target_pairs={{0,8},{4,12},{8,0},{12,4},{16,24},{20,28},{24,16},{28,20},{1,9},{5... | collective-permute-start | bytes 528392 | tf_op jit(solution)/shard_map/ppermute | solution.py:386
  53.4 4.6 %collective-permute-done.12 = f32[344,128]{1,0:T(8,128)S(1)} collective-permute-done((f32[344,128]{1,0:T(8,128)S(1)}, f32[344,128]{1,0:T(8,128)S(1)}, u32[]{:S(2)}, u32[]{:S(2)}) %collective-permute-start.12) | collective-permute-done | bytes 176160 | tf_op jit(solution)/shard_map/ppermute | solution.py:386
  58.1 1.5 %collective-permute-done.14 = f32[344,128]{1,0:T(8,128)S(1)} collective-permute-done((f32[344,128]{1,0:T(8,128)S(1)}, f32[344,128]{1,0:T(8,128)S(1)}, u32[]{:S(2)}, u32[]{:S(2)}) %collective-permute-start.14) | collective-permute-done | bytes 176160 | tf_op jit(solution)/shard_map/ppermute | solution.py:386
  61.6 3.6 %collective-permute-start.7 = (f32[64,512]{1,0:T(8,128)S(1)}, f32[64,512]{1,0:T(8,128)S(1)}, u32[]{:S(2)}, u32[]{:S(2)}) collective-permute-start(f32[64,512]{1,0:T(8,128)S(1)} %get-tuple-element.33), channel_id=1, source_target_pairs={{0,3},{1,2},{2,1},{3,0},{4,7},{5,6},{6,5},{7,4},{8,11},{9,10},{10,... | collective-permute-start | bytes 393224 | tf_op jit(solution)/shard_map/ppermute | solution.py:386
  65.9 3.5 %collective-permute-done.7.refs_3_ = f32[64,512]{1,0:T(8,128)S(1)} collective-permute-done((f32[64,512]{1,0:T(8,128)S(1)}, f32[64,512]{1,0:T(8,128)S(1)}, u32[]{:S(2)}, u32[]{:S(2)}) %collective-permute-start.7) | collective-permute-done | bytes 131104 | tf_op jit(solution)/shard_map/ppermute | solution.py:386
  69.4 5.1 %collective-permute-done.6.refs_2_ = f32[64,512]{1,0:T(8,128)S(1)} collective-permute-done((f32[64,512]{1,0:T(8,128)S(1)}, f32[64,512]{1,0:T(8,128)S(1)}, u32[]{:S(2)}, u32[]{:S(2)}) %collective-permute-start.6) | collective-permute-done | bytes 131104 | tf_op jit(solution)/shard_map/ppermute | solution.py:386
  75.2 1.9 %shard_map.134 = bf16[8,64,128]{2,1,0:T(8,128)(2,1)} custom-call(s32[2,8]{1,0:T(2,128)} %get-tuple-element.19.rank_ref, f32[64,512]{1,0:T(8,128)} %get-tuple-element.36.refs_0_, f32[64,512]{1,0:T(8,128)} %copy-done.17, f32[64,512]{1,0:T(8,128)} %copy-done.16, f32[64,512]{1,0:T(8,128)} %copy-done.15), custom_call_target="tpu_custom_call" | custom-call | tf_op jit(solution)/shard_map/pallas_call | solution.py:492
  77.1 3.5 %all-to-all-start.1 = ((bf16[8,64,128]{2,1,0:T(8,128)(2,1)}), bf16[8,64,128]{2,1,0:T(8,128)(2,1)S(1)}, u32[]{:S(2)}, u32[]{:S(2)}) async-start(bf16[8,64,128]{2,1,0:T(8,128)(2,1)} %shard_map.134), calls=%async_computation.1 | async-start | bytes 262144 | tf_op jit(solution)/shard_map/all_to_all | solution.py:498
  81.3 4.8 %all-to-all-done.1 = bf16[8,64,128]{2,1,0:T(8,128)(2,1)S(1)} async-done(((bf16[8,64,128]{2,1,0:T(8,128)(2,1)}), bf16[8,64,128]{2,1,0:T(8,128)(2,1)S(1)}, u32[]{:S(2)}, u32[]{:S(2)}) %all-to-all-start.1) | async-done | bytes 131104 | tf_op jit(solution)/shard_map/all_to_all | solution.py:498
  87.8 2.3 %shard_map.136 = (f32[864,128]{1,0:T(8,128)}, f32[8,64,128]{2,1,0:T(8,128)}) custom-call(f32[688,128]{1,0:T(8,128)} %copy-done.12, f32[688,128]{1,0:T(8,128)} %copy-done.14), custom_call_target="tpu_custom_call" | custom-call | tf_op jit(solution)/shard_map/pallas_call | solution.py:516
  (73 shorter events, 15.0 us)
Async XLA Ops:
  0.6 40.6 %copy-start.3 = (bf16[512,640]{1,0:T(8,128)(2,1)S(1)}, bf16[512,640]{1,0:T(8,128)(2,1)}, u32[]{:S(2)}) copy-start(bf16[512,640]{1,0:T(8,128)(2,1)} %constant.10.clone.spread_ref) | copy-start | bytes 1966084
  0.6 40.6 %copy-start.9 = (s32[8,512]{1,0:T(8,128)S(1)}, s32[8,512]{1,0:T(8,128)}, u32[]{:S(2)}) copy-start(s32[8,512]{1,0:T(8,128)} %mask_ref.5) | copy-start | bytes 49156
  0.7 34.6 %copy-start.4 = (bf16[8,256,128]{2,1,0:T(8,128)(2,1)S(1)}, bf16[8,256,128]{2,1,0:T(8,128)(2,1)}, u32[]{:S(2)}) copy-start(bf16[8,256,128]{2,1,0:T(8,128)(2,1)} %wdown_ref.3) | copy-start | bytes 1572868
  2.7 10.7 %all-to-all-start = ((bf16[8,64,128]{2,1,0:T(8,128)(2,1)}), bf16[8,64,128]{2,1,0:T(8,128)(2,1)S(1)}, u32[]{:S(2)}, u32[]{:S(2)}) async-start(bf16[8,64,128]{2,1,0:T(8,128)(2,1)} %get-tuple-element.18), calls=%async_computation | async-start | bytes 262144 | tf_op jit(solution)/shard_map/all_to_all | solution.py:426
  7.8 12.3 %collective-permute-start = (bf16[2,128,128]{2,1,0:T(8,128)(2,1)}, bf16[2,128,128]{2,1,0:T(8,128)(2,1)S(1)}, u32[]{:S(2)}, u32[]{:S(2)}) collective-permute-start(bf16[2,128,128]{2,1,0:T(8,128)(2,1)} %get-tuple-element.20), channel_id=1, source_target_pairs={{0,4},{4,8},{8,12},{12,16},{16,20},{20,24},{24,28},{1,5},{5,9},{9,... | collective-permute-start | bytes 196616 | tf_op jit(solution)/shard_map/ppermute | solution.py:424
  10.2 9.9 %collective-permute-start.1 = (bf16[2,128,128]{2,1,0:T(8,128)(2,1)}, bf16[2,128,128]{2,1,0:T(8,128)(2,1)S(1)}, u32[]{:S(2)}, u32[]{:S(2)}) collective-permute-start(bf16[2,128,128]{2,1,0:T(8,128)(2,1)} %get-tuple-element.21), channel_id=1, source_target_pairs={{4,0},{8,4},{12,8},{16,12},{20,16},{24,20},{28,24},{5,1},{9,5},{13... | collective-permute-start | bytes 196616 | tf_op jit(solution)/shard_map/ppermute | solution.py:425
  15.7 19.6 %collective-permute-start.4 = (bf16[64,512]{1,0:T(8,128)(2,1)}, bf16[64,512]{1,0:T(8,128)(2,1)S(1)}, u32[]{:S(2)}, u32[]{:S(2)}) collective-permute-start(bf16[64,512]{1,0:T(8,128)(2,1)} %get-tuple-element.23.refs_0_), channel_id=1, source_target_pairs={{0,3},{1,2},{2,1},{3,0},{4,7},{5,6},{6,5},{7,4},{8,11},{9,10},{10,... | collective-permute-start | bytes 196616 | tf_op jit(solution)/shard_map/ppermute | solution.py:386
  19.3 15.9 %collective-permute-start.3 = (bf16[64,512]{1,0:T(8,128)(2,1)}, bf16[64,512]{1,0:T(8,128)(2,1)S(1)}, u32[]{:S(2)}, u32[]{:S(2)}) collective-permute-start(bf16[64,512]{1,0:T(8,128)(2,1)} %get-tuple-element.23.refs_0_), channel_id=1, source_target_pairs={{0,2},{1,3},{2,0},{3,1},{4,6},{5,7},{6,4},{7,5},{8,10},{9,11},{10,... | collective-permute-start | bytes 196616 | tf_op jit(solution)/shard_map/ppermute | solution.py:386
  19.3 15.9 %collective-permute-start.2 = (bf16[64,512]{1,0:T(8,128)(2,1)}, bf16[64,512]{1,0:T(8,128)(2,1)S(1)}, u32[]{:S(2)}, u32[]{:S(2)}) collective-permute-start(bf16[64,512]{1,0:T(8,128)(2,1)} %get-tuple-element.23.refs_0_), channel_id=1, source_target_pairs={{0,1},{1,0},{2,3},{3,2},{4,5},{5,4},{6,7},{7,6},{8,9},{9,8},{10,11... | collective-permute-start | bytes 196616 | tf_op jit(solution)/shard_map/ppermute | solution.py:386
  36.8 10.2 %collective-permute-start.10 = (f32[2,64,128]{2,1,0:T(8,128)S(1)}, f32[2,64,128]{2,1,0:T(8,128)S(1)}, u32[]{:S(2)}, u32[]{:S(2)}) collective-permute-start(f32[2,64,128]{2,1,0:T(8,128)S(1)} %get-tuple-element.43), channel_id=1, source_target_pairs={{0,3},{1,2},{2,1},{3,0},{4,7},{5,6},{6,5},{7,4},{8,11},{9,10},{10,... | collective-permute-start | bytes 196616 | tf_op jit(solution)/shard_map/ppermute | solution.py:386
  40.5 6.5 %collective-permute-start.9 = (f32[2,64,128]{2,1,0:T(8,128)S(1)}, f32[2,64,128]{2,1,0:T(8,128)S(1)}, u32[]{:S(2)}, u32[]{:S(2)}) collective-permute-start(f32[2,64,128]{2,1,0:T(8,128)S(1)} %get-tuple-element.44), channel_id=1, source_target_pairs={{0,2},{1,3},{2,0},{3,1},{4,6},{5,7},{6,4},{7,5},{8,10},{9,11},{10,... | collective-permute-start | bytes 196616 | tf_op jit(solution)/shard_map/ppermute | solution.py:386
  40.5 6.5 %collective-permute-start.8 = (f32[2,64,128]{2,1,0:T(8,128)S(1)}, f32[2,64,128]{2,1,0:T(8,128)S(1)}, u32[]{:S(2)}, u32[]{:S(2)}) collective-permute-start(f32[2,64,128]{2,1,0:T(8,128)S(1)} %get-tuple-element.45), channel_id=1, source_target_pairs={{0,1},{1,0},{2,3},{3,2},{4,5},{5,4},{6,7},{7,6},{8,9},{9,8},{10,11... | collective-permute-start | bytes 196616 | tf_op jit(solution)/shard_map/ppermute | solution.py:386
  47.0 1.8 %collective-permute-start.11 = (f32[688,128]{1,0:T(8,128)S(1)}, f32[688,128]{1,0:T(8,128)S(1)}, u32[]{:S(2)}, u32[]{:S(2)}) collective-permute-start(f32[688,128]{1,0:T(8,128)S(1)} %get-tuple-element.48), channel_id=1, source_target_pairs={{0,4},{4,0},{8,12},{12,8},{16,20},{20,16},{24,28},{28,24},{1,5},{5... | collective-permute-start | bytes 1056776 | tf_op jit(solution)/shard_map/ppermute | solution.py:386
  48.9 9.2 %collective-permute-start.12 = (f32[344,128]{1,0:T(8,128)S(1)}, f32[344,128]{1,0:T(8,128)S(1)}, u32[]{:S(2)}, u32[]{:S(2)}) collective-permute-start(f32[344,128]{1,0:T(8,128)S(1)} %get-tuple-element.39), channel_id=1, source_target_pairs={{0,8},{4,12},{8,0},{12,4},{16,24},{20,28},{24,16},{28,20},{1,9},{5... | collective-permute-start | bytes 528392 | tf_op jit(solution)/shard_map/ppermute | solution.py:386
  53.3 6.2 %collective-permute-start.14 = (f32[344,128]{1,0:T(8,128)S(1)}, f32[344,128]{1,0:T(8,128)S(1)}, u32[]{:S(2)}, u32[]{:S(2)}) collective-permute-start(f32[344,128]{1,0:T(8,128)S(1)} %get-tuple-element.40), channel_id=1, source_target_pairs={{0,16},{4,20},{8,24},{12,28},{16,0},{20,4},{24,8},{28,12},{1,17},{... | collective-permute-start | bytes 528392 | tf_op jit(solution)/shard_map/ppermute | solution.py:386
  59.6 21.0 %collective-permute-start.13 = (f32[344,128]{1,0:T(8,128)S(1)}, f32[344,128]{1,0:T(8,128)S(1)}, u32[]{:S(2)}, u32[]{:S(2)}) collective-permute-start(f32[344,128]{1,0:T(8,128)S(1)} %get-tuple-element.37), channel_id=1, source_target_pairs={{0,16},{4,20},{8,24},{12,28},{16,0},{20,4},{24,8},{28,12},{1,17},{... | collective-permute-start | bytes 528392 | tf_op jit(solution)/shard_map/ppermute | solution.py:386
  59.9 20.7 %collective-permute-start.15 = (f32[344,128]{1,0:T(8,128)S(1)}, f32[344,128]{1,0:T(8,128)S(1)}, u32[]{:S(2)}, u32[]{:S(2)}) collective-permute-start(f32[344,128]{1,0:T(8,128)S(1)} %get-tuple-element.38), channel_id=1, source_target_pairs={{0,8},{4,12},{8,0},{12,4},{16,24},{20,28},{24,16},{28,20},{1,9},{5... | collective-permute-start | bytes 528392 | tf_op jit(solution)/shard_map/ppermute | solution.py:386
  61.6 7.9 %collective-permute-start.7 = (f32[64,512]{1,0:T(8,128)S(1)}, f32[64,512]{1,0:T(8,128)S(1)}, u32[]{:S(2)}, u32[]{:S(2)}) collective-permute-start(f32[64,512]{1,0:T(8,128)S(1)} %get-tuple-element.33), channel_id=1, source_target_pairs={{0,3},{1,2},{2,1},{3,0},{4,7},{5,6},{6,5},{7,4},{8,11},{9,10},{10,... | collective-permute-start | bytes 393224 | tf_op jit(solution)/shard_map/ppermute | solution.py:386
  65.2 9.3 %collective-permute-start.6 = (f32[64,512]{1,0:T(8,128)S(1)}, f32[64,512]{1,0:T(8,128)S(1)}, u32[]{:S(2)}, u32[]{:S(2)}) collective-permute-start(f32[64,512]{1,0:T(8,128)S(1)} %get-tuple-element.34), channel_id=1, source_target_pairs={{0,2},{1,3},{2,0},{3,1},{4,6},{5,7},{6,4},{7,5},{8,10},{9,11},{10,... | collective-permute-start | bytes 393224 | tf_op jit(solution)/shard_map/ppermute | solution.py:386
  65.2 9.3 %collective-permute-start.5 = (f32[64,512]{1,0:T(8,128)S(1)}, f32[64,512]{1,0:T(8,128)S(1)}, u32[]{:S(2)}, u32[]{:S(2)}) collective-permute-start(f32[64,512]{1,0:T(8,128)S(1)} %get-tuple-element.35), channel_id=1, source_target_pairs={{0,1},{1,0},{2,3},{3,2},{4,5},{5,4},{6,7},{7,6},{8,9},{9,8},{10,11... | collective-permute-start | bytes 393224 | tf_op jit(solution)/shard_map/ppermute | solution.py:386
  69.4 5.1 %copy-start.15 = (f32[64,512]{1,0:T(8,128)}, f32[64,512]{1,0:T(8,128)S(1)}, u32[]{:S(2)}) copy-start(f32[64,512]{1,0:T(8,128)S(1)} %collective-permute-done.7.refs_3_) | copy-start | bytes 393220
  77.1 9.1 %all-to-all-start.1 = ((bf16[8,64,128]{2,1,0:T(8,128)(2,1)}), bf16[8,64,128]{2,1,0:T(8,128)(2,1)S(1)}, u32[]{:S(2)}, u32[]{:S(2)}) async-start(bf16[8,64,128]{2,1,0:T(8,128)(2,1)} %shard_map.134), calls=%async_computation.1 | async-start | bytes 262144 | tf_op jit(solution)/shard_map/all_to_all | solution.py:498
  80.7 6.3 %copy-start.12 = (f32[688,128]{1,0:T(8,128)}, f32[688,128]{1,0:T(8,128)S(1)}, u32[]{:S(2)}) copy-start(f32[688,128]{1,0:T(8,128)S(1)} %pad_maximum_fusion.own_ref) | copy-start | bytes 1056772
  80.7 6.3 %collective-permute-start.16 = (f32[688,128]{1,0:T(8,128)S(1)}, f32[688,128]{1,0:T(8,128)S(1)}, u32[]{:S(2)}, u32[]{:S(2)}) collective-permute-start(f32[688,128]{1,0:T(8,128)S(1)} %pad_maximum_fusion.own_ref), channel_id=1, source_target_pairs={{0,4},{4,0},{8,12},{12,8},{16,20},{20,16},{24,28},{28,24},{1,5},{5... | collective-permute-start | bytes 1056776 | tf_op jit(solution)/shard_map/ppermute | solution.py:386
  (13 other events, 11.5 us)

commit v3 on v2

--- a/solution.py
+++ b/solution.py
@@ -2,7 +2,6 @@
 
 import jax
 import jax.numpy as jnp
-import numpy as np
 from jax import lax
 from jax.experimental import pallas as pl
 from jax.experimental.pallas import tpu as pltpu
@@ -28,53 +27,56 @@
     return pl.BlockSpec(memory_space=pltpu.SMEM)
 
 
+def cost(microseconds):
+    return pl.CostEstimate(flops=int(microseconds * 1.15e9), bytes_accessed=0, transcendentals=0)
+
+
 def rim_lane(cell_y, cell_z):
-    if 0 <= cell_y < 8 and 0 <= cell_z < 8:
-        return 8 * cell_y + cell_z
-    if 0 <= cell_z < 8:
-        return 64 + 8 * (cell_y > 0) + cell_z
-    if 0 <= cell_y < 8:
-        return 80 + 8 * (cell_z > 0) + cell_y
-    return 96 + 2 * (cell_y > 0) + (cell_z > 0)
-
-
-def edge_table():
-    table = np.zeros((10, LANES, LANES), np.float32)
-    for place, (step_y, step_z) in enumerate((a, b) for a in SIGNS for b in SIGNS):
-        for cell_y in range(8):
-            for cell_z in range(8):
-                far_y, far_z = cell_y + 8 * step_y, cell_z + 8 * step_z
-                if -1 <= far_y <= 8 and -1 <= far_z <= 8:
-                    table[place, 8 * cell_y + cell_z, rim_lane(far_y, far_z)] = 1
-    return table
-
-
-def shift_table():
-    table = np.zeros((3, 2, 10, 8, 2, LANES), np.float32)
-    for place, step_z in enumerate(SIGNS):
-        for cell_y in range(10):
-            for cell_z in range(8):
-                for plane in range(2):
-                    table[place, plane, cell_y, cell_z, plane, rim_lane(cell_y - 1, cell_z + step_z)] = 1
-    return table.reshape(3 * 2 * PLANE, 2 * LANES)
+    high_y, high_z = (cell_y > 0).astype(jnp.int32), (cell_z > 0).astype(jnp.int32)
+    own_y, own_z = (cell_y >= 0) & (cell_y < 8), (cell_z >= 0) & (cell_z < 8)
+    edges = jnp.where(own_z, 64 + 8 * high_y + cell_z, 80 + 8 * high_z + cell_y)
+    lane = jnp.where(own_y & own_z, 8 * cell_y + cell_z, edges)
+    return jnp.where(own_y | own_z, lane, 96 + 2 * high_y + high_z)
+
+
+def column(rows):
+    return lax.broadcasted_iota(jnp.int32, (rows, 1), 0)
+
+
+def row(lanes):
+    return lax.broadcasted_iota(jnp.int32, (1, lanes), 1)
+
+
+def equal(left, right):
+    return jnp.where(left == right, 1.0, 0.0).astype(BF16)
+
+
+def edge_table(step_y, step_z):
+    source = column(LANES)
+    far_y, far_z = (source >> 3) + 8 * step_y, (source & 7) + 8 * step_z
+    there = (source < 64) & (far_y >= -1) & (far_y <= 8) & (far_z >= -1) & (far_z <= 8)
+    return equal(jnp.where(there, rim_lane(far_y, far_z), -1), row(LANES))
+
+
+def shift_table(step_z):
+    cell = column(2 * PLANE)
+    plane = (cell >= PLANE).astype(jnp.int32)
+    cell = cell - plane * PLANE
+    lane = rim_lane((cell >> 3) - 1, (cell & 7) + step_z)
+    return equal(plane * LANES + lane, row(2 * LANES))
 
 
 def spread_table():
-    table = np.zeros((8, 64, 8, PLANE), np.float32)
-    for x in range(8):
-        for cell in range(64):
-            table[x, cell, x, cell] = 1
-    return table.reshape(512, SPAN)
-
-
-def octant_table():
-    table = np.zeros((8, PLANE, 8, 2, 64), np.float32)
-    for x in range(8):
-        for y in range(8):
-            for z in range(8):
-                octant = 4 * (x % 2) + 2 * (y % 2) + z % 2
-                table[x, 8 * y + z, octant, :, 16 * (x // 2) + 4 * (y // 2) + z // 2] = 1
-    return table.reshape(SPAN, 8 * LANES)
+    voxel = column(512)
+    return equal((voxel >> 6) * PLANE + (voxel & 63), row(SPAN))
+
+
+def octant_table(plane):
+    cell = column(PLANE)
+    octant = 4 * (plane % 2) + 2 * ((cell >> 3) & 1) + (cell & 1)
+    place = 16 * (plane // 2) + 4 * ((cell >> 4) & 3) + ((cell >> 1) & 3)
+    lane = row(8 * LANES)
+    return equal(jnp.where(cell < 64, octant * 64 + place, -1), (lane >> 7) * 64 + (lane & 63))
 
 
 def low_half(rows):
@@ -102,16 +104,16 @@
 
 
 def pick_kernel(owner_ref, returned_ref, out_ref, rank_ref):
-    blocks = owner_ref.shape[0]
+    blocks = owner_ref.shape[1]
     low = low_half(out_ref.shape[0])
     for pair in range(blocks // 2):
         rows = []
         for side in range(2):
             block = 2 * pair + side
-            owner = owner_ref[block, 0]
+            owner = owner_ref[0, block]
             rank = jnp.int32(0)
             for earlier in range(block):
-                rank = rank + (owner_ref[earlier, 0] == owner).astype(jnp.int32)
+                rank = rank + (owner_ref[0, earlier] == owner).astype(jnp.int32)
             rank_ref[0, block] = owner
             rank_ref[1, block] = rank
             tile = returned_ref[owner].astype(F32)
@@ -136,19 +138,17 @@
 
 def forward_kernel(
     axis,
-    nbr_ref,
-    feat_ref,
-    mask_ref,
     prev_ref,
     next_ref,
-    wconv_ref,
-    edge_ref,
-    shift_ref,
-    spread_ref,
-    octant_ref,
+    nbr_hbm,
+    feat_hbm,
+    mask_hbm,
+    wconv_hbm,
     pre_out,
     octs_out,
     patches_out,
+    spread_ref,
+    octant_ref,
     planes,
     weights,
     own_s,
@@ -157,7 +157,27 @@
     same_code,
     side_from,
     side_code,
+    nbr_ref,
+    feat_ref,
+    mask_ref,
+    wconv_ref,
+    edge_ref,
+    shift_ref,
+    sems,
 ):
+    loads = [
+        pltpu.make_async_copy(source, target, sems.at[i])
+        for i, (source, target) in enumerate(
+            [
+                (nbr_hbm, nbr_ref),
+                (mask_hbm, mask_ref),
+                (feat_hbm, feat_ref),
+                (wconv_hbm, wconv_ref),
+            ]
+        )
+    ]
+    for load in loads:
+        load.start()
     blocks, channels = feat_ref.shape[0], feat_ref.shape[1]
     edge = blocks // 2
     width = wconv_ref.shape[1]
@@ -167,6 +187,16 @@
     halo = 10 * blocks
     dummy = 11 * blocks
 
+    for table in range(9):
+        edge_ref[table] = edge_table(table // 3 - 1, table % 3 - 1)
+    edge_ref[9] = jnp.zeros((LANES, LANES), BF16)
+    for j in range(3):
+        shift_ref[j * 2 * PLANE : (j + 1) * 2 * PLANE, :] = shift_table(j - 1)
+    spread_ref[...] = spread_table()
+    for plane in range(8):
+        octant_ref[plane * PLANE : (plane + 1) * PLANE, :] = octant_table(plane)
+
+    loads[0].wait()
     same, side = jnp.int32(0), jnp.int32(0)
     for block in range(blocks):
         for column in range(26):
@@ -183,6 +213,8 @@
                 side_code[side] = (block * 10 + (9 if step else 0)) * 32 + table * 2 + step // 2
                 side = side + there
 
+    loads[1].wait()
+    loads[2].wait()
     def two_planes(first, tile):
         planes[first] = jnp.where(low, tile, 0.0).astype(BF16)
         planes[first + 1] = jnp.where(low, swap_halves(tile), 0.0).astype(BF16)
@@ -229,6 +261,7 @@
 
     lax.fori_loop(0, lax.shift_right_logical(side + 3, 2), side_layer, 0)
 
+    loads[3].wait()
     for k in range(27):
         weights[(k // 3) * width : (k // 3 + 1) * width, (k % 3) * channels : (k % 3 + 1) * channels] = wconv_ref[k]
 
@@ -397,8 +430,6 @@
     share = total // shards
     capacity = cotangent.shape[0] // peers
     lanes = blocks * 64
-    tables = [jnp.asarray(t(), BF16) for t in (edge_table, shift_table, spread_table, octant_table)]
-    edges, shifts, spreads, octants = tables
 
     head, tail, packed = pl.pallas_call(
         prepare_kernel,
@@ -419,6 +450,8 @@
             pl.BlockSpec((edge // 2, channels, LANES), lambda i: (0, 0, 0)),
             pl.BlockSpec((peers, share, capacity * 64), lambda i: (0, 0, 0)),
         ],
+        cost_estimate=cost(2),
+        compiler_params=pltpu.CompilerParams(vmem_limit_bytes=60 * MIB),
     )(features, features, voxel_mask, cotangent)
     ends = peers - 1
     before = lax.ppermute(tail, "space", [(i, i + 1) for i in range(ends)])
@@ -433,18 +466,22 @@
         ],
         in_specs=[smem(), vmem()],
         out_specs=[vmem(), smem()],
-    )(coarse_owner, returned)
+        cost_estimate=cost(1.5),
+        compiler_params=pltpu.CompilerParams(vmem_limit_bytes=8 * MIB),
+    )(coarse_owner.reshape(1, blocks), returned)
     dpieces = [dpiece] + [exchange(dpiece, "chan", k) for k in range(1, shards)]
 
-    pre, octs, patches = pl.pallas_call(
+    pre, octs, patches, spreads, octants = pl.pallas_call(
         functools.partial(forward_kernel, "chan"),
         out_shape=[
             jax.ShapeDtypeStruct((blocks * width, SPAN), F32),
             jax.ShapeDtypeStruct((8 * width, lanes), BF16),
             jax.ShapeDtypeStruct((blocks * STRIDE, 3 * channels), BF16),
-        ],
-        in_specs=[smem()] + [vmem()] * 9,
-        out_specs=[vmem()] * 3,
+            jax.ShapeDtypeStruct((512, SPAN), BF16),
+            jax.ShapeDtypeStruct((SPAN, 8 * LANES), BF16),
+        ],
+        in_specs=[vmem()] * 2 + [pl.BlockSpec(memory_space=pltpu.HBM)] * 4,
+        out_specs=[vmem()] * 5,
         scratch_shapes=[
             pltpu.VMEM((11 * blocks + 1, channels, LANES), BF16),
             pltpu.VMEM((9 * width, 3 * channels), BF16),
@@ -454,9 +491,17 @@
             pltpu.SMEM((8 * blocks + 8,), jnp.int32),
             pltpu.SMEM((18 * blocks + 8,), jnp.int32),
             pltpu.SMEM((18 * blocks + 8,), jnp.int32),
-        ],
+            pltpu.SMEM(neighbors.shape, jnp.int32),
+            pltpu.VMEM(features.shape, BF16),
+            pltpu.VMEM(voxel_mask.shape, jnp.int32),
+            pltpu.VMEM(w_conv.shape, BF16),
+            pltpu.VMEM((10, LANES, LANES), BF16),
+            pltpu.VMEM((3 * 2 * PLANE, 2 * LANES), BF16),
+            pltpu.SemaphoreType.DMA((4,)),
+        ],
+        cost_estimate=cost(8),
         compiler_params=pltpu.CompilerParams(vmem_limit_bytes=40 * MIB),
-    )(neighbors, features, voxel_mask, before, after, w_conv, edges, shifts, spreads, octants)
+    )(before, after, neighbors, features, voxel_mask, w_conv)
 
     pieces, down_grad, dp_all = pl.pallas_call(
         functools.partial(down_kernel, axes, shards),
@@ -468,6 +513,7 @@
         in_specs=[vmem()] * (2 + shards),
         out_specs=[vmem()] * 3,
         scratch_shapes=[pltpu.VMEM((8 * channels, lanes), BF16), pltpu.VMEM((total, lanes), F32)],
+        cost_estimate=cost(1),
         compiler_params=pltpu.CompilerParams(vmem_limit_bytes=24 * MIB),
     )(octs, w_down, *dpieces)
     downs = [down_grad[0]] + [exchange(down_grad[k], "chan", k) for k in range(1, shards)]
@@ -486,6 +532,7 @@
             pltpu.VMEM((9 * width, blocks * STRIDE), BF16),
             pltpu.VMEM((27 * width, channels), F32),
         ],
+        cost_estimate=cost(6),
         compiler_params=pltpu.CompilerParams(vmem_limit_bytes=40 * MIB),
     )(dp_all, w_down, voxel_mask, pre, spreads, octants, patches)
 
@@ -494,6 +541,8 @@
         out_shape=jax.ShapeDtypeStruct((peers, share, capacity * 64), BF16),
         in_specs=[smem()] + [vmem()] * shards,
         out_specs=vmem(),
+        cost_estimate=cost(1.5),
+        compiler_params=pltpu.CompilerParams(vmem_limit_bytes=8 * MIB),
     )(place, *parts)
     coarse = lax.all_to_all(outgoing, "space", split_axis=0, concat_axis=0, tiled=True)
     coarse = coarse.reshape(peers, share, capacity, 64).transpose(0, 2, 1, 3).reshape(peers * capacity, share, 64)
@@ -522,6 +571,8 @@
         in_specs=[vmem(), vmem()],
         out_specs=[vmem()] * 2,
         scratch_shapes=[pltpu.VMEM((2,) + mine.shape, F32)],
+        cost_estimate=cost(1.5),
+        compiler_params=pltpu.CompilerParams(vmem_limit_bytes=8 * MIB),
     )(mine, other)
     return coarse, conv_sum.reshape(27, width, channels), down_sum
 

time: 91.6 us -> 70.9 us (0.77); the launches traced: 90.1 us -> 70.3 us
  local copies, waits for them, and re-layouts: 13.1 us -> 0.28 us
  waiting for transfers between devices: 21.3 us -> 14.9 us
    unnamed x41 -> x16, local copies, waits for them, and re-layouts: 12.2 us -> 0.08 us
    ppermute x15, waiting for transfers between devices: 16 us -> 8.14 us  [exchange(): return lax.ppermute(values, axis, [(i, i ^ step) for i in range(count)])]
    all_to_all x1, waiting for transfers between devices: 0.51 us -> 1.82 us  [local(): lax.all_to_all(packed, 'space', split_axis=0, concat_axis=0, tiled=True)]
    pallas_call x1, Pallas kernels: 7.21 us -> 8.39 us  [local(): pl.pallas_call(functools.partial(forward_kernel, 'chan'), out_shape=[jax....]
    pallas_call x1, Pallas kernels: 2.29 us -> 1.2 us  [local(): pl.pallas_call(functools.partial(finish_kernel, axes, shards, half), out_...]
  transfers between devices with their start and end apart: 19 -> 19, of which waited for: 7 -> 5; matrix products, arithmetic and copies ran while one was open for 3% -> 2% of each run, Pallas kernels for 18% -> 24%
where the time goes in v3:
time: 70.9 us; the launch traced here: 70.3 us
  starting transfers between devices  32.8 us (46%)
  Pallas kernels  20.5 us (29%)
  waiting for transfers between devices  14.9 us (21%)
  other arithmetic  0.93 us (1%)
  between operations  0.93 us (1%)
    ppermute x15, starting transfers between devices, exchange(): return lax.ppermute(values, axis, [(i, i ^ step) for i in range(count)])  20.5 us
    pallas_call x1, Pallas kernels, local(): pl.pallas_call(functools.partial(forward_kernel, 'chan'), out_shape=[jax....  8.39 us
    ppermute x15, waiting for transfers between devices, exchange(): return lax.ppermute(values, axis, [(i, i ^ step) for i in range(count)])  8.14 us
    pallas_call x1, Pallas kernels, local(): pl.pallas_call(functools.partial(backward_kernel, axes), out_shape=[jax.S...  5.77 us
    all_to_all x1, starting transfers between devices, local(): lax.all_to_all(packed, 'space', split_axis=0, concat_axis=0, tiled=True)  5.17 us
    all_to_all x1, waiting for transfers between devices, local(): lax.all_to_all(outgoing, 'space', split_axis=0, concat_axis=0, tiled=True)  4.89 us
    all_to_all x1, starting transfers between devices, local(): lax.all_to_all(outgoing, 'space', split_axis=0, concat_axis=0, tiled=True)  3.37 us
    ppermute x1, starting transfers between devices, local(): before = lax.ppermute(tail, 'space', [(i, i + 1) for i in range(ends)])  2.4 us
  transfers between devices with their start and end apart: 19, of which 5 were waited for; matrix products, arithmetic and copies ran while one was open for 2% of the time, Pallas kernels for 24%

profile of v3, /device:TPU:0, one launch (start us, length us, event | category | flops | bytes accessed | tf_op | source)
XLA Modules:
  0.0 70.3 jit_solution(29656732413058056)
XLA Ops:
  0.7 2.0 %shard_map.94 = (bf16[2,128,128]{2,1,0:T(8,128)(2,1)}, bf16[2,128,128]{2,1,0:T(8,128)(2,1)}, bf16[8,64,128]{2,1,0:T(8,128)(2,1)}) custom-call(bf16[8,128,512]{2,1,0:T(8,128)(2,1)} %feat_hbm.1, bf16[8,128,512]{2,1,0:T(8,128)(2,1)} %feat_hbm.1, s32[8,512]{1,0:T(8,128)} %mask_ref.3, bf16[16,64,64]{2,1,0:T(8,128)(2,1)} %cot_ref.1), custom_call_target="tpu_custom_call" | custom-call | flops 2300000000 | tf_op jit(solution)/shard_map/pallas_call | solution.py:434
  2.7 5.2 %all-to-all-start = ((bf16[8,64,128]{2,1,0:T(8,128)(2,1)}), bf16[8,64,128]{2,1,0:T(8,128)(2,1)S(1)}, u32[]{:S(2)}, u32[]{:S(2)}) async-start(bf16[8,64,128]{2,1,0:T(8,128)(2,1)} %get-tuple-element.20), calls=%async_computation | async-start | bytes 262144 | tf_op jit(solution)/shard_map/all_to_all | solution.py:459
  7.8 2.4 %collective-permute-start = (bf16[2,128,128]{2,1,0:T(8,128)(2,1)}, bf16[2,128,128]{2,1,0:T(8,128)(2,1)S(1)}, u32[]{:S(2)}, u32[]{:S(2)}) collective-permute-start(bf16[2,128,128]{2,1,0:T(8,128)(2,1)} %get-tuple-element.22), channel_id=1, source_target_pairs={{0,4},{4,8},{8,12},{12,16},{16,20},{20,24},{24,28},{1,5},{5,9},{9,... | collective-permute-start | bytes 196616 | tf_op jit(solution)/shard_map/ppermute | solution.py:457
  10.3 1.3 %collective-permute-start.1 = (bf16[2,128,128]{2,1,0:T(8,128)(2,1)}, bf16[2,128,128]{2,1,0:T(8,128)(2,1)S(1)}, u32[]{:S(2)}, u32[]{:S(2)}) collective-permute-start(bf16[2,128,128]{2,1,0:T(8,128)(2,1)} %get-tuple-element.23), channel_id=1, source_target_pairs={{4,0},{8,4},{12,8},{16,12},{20,16},{24,20},{28,24},{5,1},{9,5},{13... | collective-permute-start | bytes 196616 | tf_op jit(solution)/shard_map/ppermute | solution.py:458
  11.6 1.8 %all-to-all-done.returned_ref = bf16[8,64,128]{2,1,0:T(8,128)(2,1)S(1)} async-done(((bf16[8,64,128]{2,1,0:T(8,128)(2,1)}), bf16[8,64,128]{2,1,0:T(8,128)(2,1)S(1)}, u32[]{:S(2)}, u32[]{:S(2)}) %all-to-all-start) | async-done | bytes 131104 | tf_op jit(solution)/shard_map/all_to_all | solution.py:459
  13.4 1.2 %shard_map.95 = (bf16[64,512]{1,0:T(8,128)(2,1)S(1)}, s32[2,8]{1,0:T(2,128)S(1)}) custom-call(s32[1,8]{1,0:T(1,128)S(1)} %bitcast.45, bf16[8,64,128]{2,1,0:T(8,128)(2,1)S(1)} %all-to-all-done.returned_ref), custom_call_target="tpu_custom_call" | custom-call | flops 1724999936 | tf_op jit(solution)/shard_map/pallas_call | solution.py:461
  14.6 3.7 %collective-permute-start.4 = (bf16[64,512]{1,0:T(8,128)(2,1)S(1)}, bf16[64,512]{1,0:T(8,128)(2,1)S(1)}, u32[]{:S(2)}, u32[]{:S(2)}) collective-permute-start(bf16[64,512]{1,0:T(8,128)(2,1)S(1)} %get-tuple-element.25.refs_0_), channel_id=1, source_target_pairs={{0,3},{1,2},{2,1},{3,0},{4,7},{5,6},{6,5},{7,4},{8,11},{9,10},{10,... | collective-permute-start | bytes 196616 | tf_op jit(solution)/shard_map/ppermute | solution.py:419
  18.3 0.8 %collective-permute-start.2 = (bf16[64,512]{1,0:T(8,128)(2,1)S(1)}, bf16[64,512]{1,0:T(8,128)(2,1)S(1)}, u32[]{:S(2)}, u32[]{:S(2)}) collective-permute-start(bf16[64,512]{1,0:T(8,128)(2,1)S(1)} %get-tuple-element.25.refs_0_), channel_id=1, source_target_pairs={{0,1},{1,0},{2,3},{3,2},{4,5},{5,4},{6,7},{7,6},{8,9},{9,8},{10,11... | collective-permute-start | bytes 196616 | tf_op jit(solution)/shard_map/ppermute | solution.py:419
  19.1 8.4 %shard_map.96 = (f32[256,640]{1,0:T(8,128)S(1)}, bf16[256,512]{1,0:T(8,128)(2,1)S(1)}, bf16[7168,384]{1,0:T(8,128)(2,1)S(1)}, bf16[512,640]{1,0:T(8,128)(2,1)S(1)}, bf16[640,1024]{1,0:T(8,128)(2,1)S(1)}) custom-call(bf16[2,128,128]{2,1,0:T(8,128)(2,1)S(1)} %collective-permute-done.prev_ref, bf16[2,128,128]{2,1,0:T(8,128)(2,1)S(1)} %collective-permute-done.1.next_ref, ...), custom_call_target="tpu_custom_call" | custom-call | flops 9200000000 | tf_op jit(solution)/shard_map/pallas_call | solution.py:474
  28.2 3.7 %collective-permute-start.10 = (f32[2,64,128]{2,1,0:T(8,128)S(1)}, f32[2,64,128]{2,1,0:T(8,128)S(1)}, u32[]{:S(2)}, u32[]{:S(2)}) collective-permute-start(f32[2,64,128]{2,1,0:T(8,128)S(1)} %get-tuple-element.47), channel_id=1, source_target_pairs={{0,3},{1,2},{2,1},{3,0},{4,7},{5,6},{6,5},{7,4},{8,11},{9,10},{10,... | collective-permute-start | bytes 196616 | tf_op jit(solution)/shard_map/ppermute | solution.py:419
  32.7 5.8 %shard_map.99 = (f32[432,128]{1,0:T(8,128)S(1)}, f32[432,128]{1,0:T(8,128)S(1)}) custom-call(bf16[256,512]{1,0:T(8,128)(2,1)S(1)} %get-tuple-element.27.dp_ref, bf16[8,256,128]{2,1,0:T(8,128)(2,1)S(1)} %copy-done.1, s32[8,512]{1,0:T(8,128)S(1)} %copy-done.3, f32[256,640]{1,0:T(8,128)S(1)} %get-tuple-element.28.pre_ref, ...), custom_call_target="tpu_custom_call" | custom-call | flops 6899999744 | tf_op jit(solution)/shard_map/pallas_call | solution.py:523
  38.6 1.7 %collective-permute-done.11 = f32[688,128]{1,0:T(8,128)S(1)} collective-permute-done((f32[688,128]{1,0:T(8,128)S(1)}, f32[688,128]{1,0:T(8,128)S(1)}, u32[]{:S(2)}, u32[]{:S(2)}) %collective-permute-start.11) | collective-permute-done | bytes 352288 | tf_op jit(solution)/shard_map/ppermute | solution.py:419
  40.4 1.7 %collective-permute-start.12 = (f32[344,128]{1,0:T(8,128)S(1)}, f32[344,128]{1,0:T(8,128)S(1)}, u32[]{:S(2)}, u32[]{:S(2)}) collective-permute-start(f32[344,128]{1,0:T(8,128)S(1)} %get-tuple-element.43), channel_id=1, source_target_pairs={{0,8},{4,12},{8,0},{12,4},{16,24},{20,28},{24,16},{28,20},{1,9},{5... | collective-permute-start | bytes 528392 | tf_op jit(solution)/shard_map/ppermute | solution.py:419
  42.1 1.5 %collective-permute-start.14 = (f32[344,128]{1,0:T(8,128)S(1)}, f32[344,128]{1,0:T(8,128)S(1)}, u32[]{:S(2)}, u32[]{:S(2)}) collective-permute-start(f32[344,128]{1,0:T(8,128)S(1)} %get-tuple-element.44), channel_id=1, source_target_pairs={{0,16},{4,20},{8,24},{12,28},{16,0},{20,4},{24,8},{28,12},{1,17},{... | collective-permute-start | bytes 528392 | tf_op jit(solution)/shard_map/ppermute | solution.py:419
  43.6 3.7 %collective-permute-start.7 = (f32[64,512]{1,0:T(8,128)S(1)}, f32[64,512]{1,0:T(8,128)S(1)}, u32[]{:S(2)}, u32[]{:S(2)}) collective-permute-start(f32[64,512]{1,0:T(8,128)S(1)} %get-tuple-element.37), channel_id=1, source_target_pairs={{0,3},{1,2},{2,1},{3,0},{4,7},{5,6},{6,5},{7,4},{8,11},{9,10},{10,... | collective-permute-start | bytes 393224 | tf_op jit(solution)/shard_map/ppermute | solution.py:419
  47.3 0.8 %collective-permute-start.5 = (f32[64,512]{1,0:T(8,128)S(1)}, f32[64,512]{1,0:T(8,128)S(1)}, u32[]{:S(2)}, u32[]{:S(2)}) collective-permute-start(f32[64,512]{1,0:T(8,128)S(1)} %get-tuple-element.39), channel_id=1, source_target_pairs={{0,1},{1,0},{2,3},{3,2},{4,5},{5,4},{6,7},{7,6},{8,9},{9,8},{10,11... | collective-permute-start | bytes 393224 | tf_op jit(solution)/shard_map/ppermute | solution.py:419
  48.4 1.8 %collective-permute-start.13 = (f32[344,128]{1,0:T(8,128)S(1)}, f32[344,128]{1,0:T(8,128)S(1)}, u32[]{:S(2)}, u32[]{:S(2)}) collective-permute-start(f32[344,128]{1,0:T(8,128)S(1)} %get-tuple-element.41), channel_id=1, source_target_pairs={{0,16},{4,20},{8,24},{12,28},{16,0},{20,4},{24,8},{28,12},{1,17},{... | collective-permute-start | bytes 528392 | tf_op jit(solution)/shard_map/ppermute | solution.py:419
  50.2 1.7 %collective-permute-start.15 = (f32[344,128]{1,0:T(8,128)S(1)}, f32[344,128]{1,0:T(8,128)S(1)}, u32[]{:S(2)}, u32[]{:S(2)}) collective-permute-start(f32[344,128]{1,0:T(8,128)S(1)} %get-tuple-element.42), channel_id=1, source_target_pairs={{0,8},{4,12},{8,0},{12,4},{16,24},{20,28},{24,16},{28,20},{1,9},{5... | collective-permute-start | bytes 528392 | tf_op jit(solution)/shard_map/ppermute | solution.py:419
  51.9 6.1 %collective-permute-done.6.refs_2_ = f32[64,512]{1,0:T(8,128)S(1)} collective-permute-done((f32[64,512]{1,0:T(8,128)S(1)}, f32[64,512]{1,0:T(8,128)S(1)}, u32[]{:S(2)}, u32[]{:S(2)}) %collective-permute-start.6) | collective-permute-done | bytes 131104 | tf_op jit(solution)/shard_map/ppermute | solution.py:419
  58.0 1.3 %shard_map.98 = bf16[8,64,128]{2,1,0:T(8,128)(2,1)} custom-call(s32[2,8]{1,0:T(2,128)S(1)} %get-tuple-element.21.rank_ref, f32[64,512]{1,0:T(8,128)S(1)} %get-tuple-element.40.refs_0_, f32[64,512]{1,0:T(8,128)S(1)} %collective-permute-done.5.refs_1_, f32[64,512]{1,0:T(8,128)S(1)} %collective-permute-done.6.refs_2_, f32[64,512]{1,0:T(8,128)S(1)} %collective-permute-done.7.refs_3_), custom_call_target="tpu_custom_call" | custom-call | flops 1724999936 | tf_op jit(solution)/shard_map/pallas_call | solution.py:539
  59.4 3.4 %all-to-all-start.1 = ((bf16[8,64,128]{2,1,0:T(8,128)(2,1)}), bf16[8,64,128]{2,1,0:T(8,128)(2,1)S(1)}, u32[]{:S(2)}, u32[]{:S(2)}) async-start(bf16[8,64,128]{2,1,0:T(8,128)(2,1)} %shard_map.98), calls=%async_computation.1 | async-start | bytes 262144 | tf_op jit(solution)/shard_map/all_to_all | solution.py:547
  63.3 4.9 %all-to-all-done.1 = bf16[8,64,128]{2,1,0:T(8,128)(2,1)S(1)} async-done(((bf16[8,64,128]{2,1,0:T(8,128)(2,1)}), bf16[8,64,128]{2,1,0:T(8,128)(2,1)S(1)}, u32[]{:S(2)}, u32[]{:S(2)}) %all-to-all-start.1) | async-done | bytes 131104 | tf_op jit(solution)/shard_map/all_to_all | solution.py:547
  68.3 0.8 %pad_maximum_fusion.1 = bf16[8,128,64]{2,1,0:T(8,128)(2,1)} fusion(bf16[8,64,64]{2,1,0:T(8,128)(2,1)S(1)} %get-tuple-element.51, bf16[8,64,64]{2,1,0:T(8,128)(2,1)S(1)} %get-tuple-element.50), kind=kLoop, calls=%fused_computation.1 | loop fusion | flops 262144 | bytes 262144 | tf_op jit(solution)/shard_map/concatenate
  69.1 1.2 %shard_map.100 = (f32[864,128]{1,0:T(8,128)}, f32[8,64,128]{2,1,0:T(8,128)}) custom-call(f32[688,128]{1,0:T(8,128)S(1)} %pad_maximum_fusion.own_ref, f32[688,128]{1,0:T(8,128)S(1)} %collective-permute-done.16.other_ref), custom_call_target="tpu_custom_call" | custom-call | flops 1724999936 | tf_op jit(solution)/shard_map/pallas_call | solution.py:565
  (48 shorter events, 2.7 us)
Async XLA Ops:
  0.6 18.4 %copy-start.3 = (s32[8,512]{1,0:T(8,128)S(1)}, s32[8,512]{1,0:T(8,128)}, u32[]{:S(2)}) copy-start(s32[8,512]{1,0:T(8,128)} %mask_ref.3) | copy-start | bytes 49156
  0.6 18.4 %copy-start = (bf16[8,128,512]{2,1,0:T(8,128)(2,1)S(1)}, bf16[8,128,512]{2,1,0:T(8,128)(2,1)}, u32[]{:S(2)}) copy-start(bf16[8,128,512]{2,1,0:T(8,128)(2,1)} %feat_hbm.1) | copy-start | bytes 3145732
  0.7 18.4 %copy-start.2 = (bf16[27,32,128]{2,1,0:T(8,128)(2,1)S(1)}, bf16[27,32,128]{2,1,0:T(8,128)(2,1)}, u32[]{:S(2)}) copy-start(bf16[27,32,128]{2,1,0:T(8,128)(2,1)} %wconv_hbm.1) | copy-start | bytes 663556
  0.7 18.4 %copy-start.4 = (s32[8,26]{1,0:T(8,128)S(1)}, s32[8,26]{1,0:T(8,128)}, u32[]{:S(2)}) copy-start(s32[8,26]{1,0:T(8,128)} %nbr_hbm.1) | copy-start | bytes 2500
  2.7 10.7 %all-to-all-start = ((bf16[8,64,128]{2,1,0:T(8,128)(2,1)}), bf16[8,64,128]{2,1,0:T(8,128)(2,1)S(1)}, u32[]{:S(2)}, u32[]{:S(2)}) async-start(bf16[8,64,128]{2,1,0:T(8,128)(2,1)} %get-tuple-element.20), calls=%async_computation | async-start | bytes 262144 | tf_op jit(solution)/shard_map/all_to_all | solution.py:459
  7.8 11.2 %collective-permute-start = (bf16[2,128,128]{2,1,0:T(8,128)(2,1)}, bf16[2,128,128]{2,1,0:T(8,128)(2,1)S(1)}, u32[]{:S(2)}, u32[]{:S(2)}) collective-permute-start(bf16[2,128,128]{2,1,0:T(8,128)(2,1)} %get-tuple-element.22), channel_id=1, source_target_pairs={{0,4},{4,8},{8,12},{12,16},{16,20},{20,24},{24,28},{1,5},{5,9},{9,... | collective-permute-start | bytes 196616 | tf_op jit(solution)/shard_map/ppermute | solution.py:457
  10.3 8.8 %collective-permute-start.1 = (bf16[2,128,128]{2,1,0:T(8,128)(2,1)}, bf16[2,128,128]{2,1,0:T(8,128)(2,1)S(1)}, u32[]{:S(2)}, u32[]{:S(2)}) collective-permute-start(bf16[2,128,128]{2,1,0:T(8,128)(2,1)} %get-tuple-element.23), channel_id=1, source_target_pairs={{4,0},{8,4},{12,8},{16,12},{20,16},{24,20},{28,24},{5,1},{9,5},{13... | collective-permute-start | bytes 196616 | tf_op jit(solution)/shard_map/ppermute | solution.py:458
  14.6 12.9 %copy-start.1 = (bf16[8,256,128]{2,1,0:T(8,128)(2,1)S(1)}, bf16[8,256,128]{2,1,0:T(8,128)(2,1)}, u32[]{:S(2)}) copy-start(bf16[8,256,128]{2,1,0:T(8,128)(2,1)} %wdown_ref.3) | copy-start | bytes 1572868
  14.6 12.9 %collective-permute-start.4 = (bf16[64,512]{1,0:T(8,128)(2,1)S(1)}, bf16[64,512]{1,0:T(8,128)(2,1)S(1)}, u32[]{:S(2)}, u32[]{:S(2)}) collective-permute-start(bf16[64,512]{1,0:T(8,128)(2,1)S(1)} %get-tuple-element.25.refs_0_), channel_id=1, source_target_pairs={{0,3},{1,2},{2,1},{3,0},{4,7},{5,6},{6,5},{7,4},{8,11},{9,10},{10,... | collective-permute-start | bytes 196616 | tf_op jit(solution)/shard_map/ppermute | solution.py:419
  18.3 9.2 %collective-permute-start.3 = (bf16[64,512]{1,0:T(8,128)(2,1)S(1)}, bf16[64,512]{1,0:T(8,128)(2,1)S(1)}, u32[]{:S(2)}, u32[]{:S(2)}) collective-permute-start(bf16[64,512]{1,0:T(8,128)(2,1)S(1)} %get-tuple-element.25.refs_0_), channel_id=1, source_target_pairs={{0,2},{1,3},{2,0},{3,1},{4,6},{5,7},{6,4},{7,5},{8,10},{9,11},{10,... | collective-permute-start | bytes 196616 | tf_op jit(solution)/shard_map/ppermute | solution.py:419
  18.3 9.2 %collective-permute-start.2 = (bf16[64,512]{1,0:T(8,128)(2,1)S(1)}, bf16[64,512]{1,0:T(8,128)(2,1)S(1)}, u32[]{:S(2)}, u32[]{:S(2)}) collective-permute-start(bf16[64,512]{1,0:T(8,128)(2,1)S(1)} %get-tuple-element.25.refs_0_), channel_id=1, source_target_pairs={{0,1},{1,0},{2,3},{3,2},{4,5},{5,4},{6,7},{7,6},{8,9},{9,8},{10,11... | collective-permute-start | bytes 196616 | tf_op jit(solution)/shard_map/ppermute | solution.py:419
  28.2 10.3 %collective-permute-start.10 = (f32[2,64,128]{2,1,0:T(8,128)S(1)}, f32[2,64,128]{2,1,0:T(8,128)S(1)}, u32[]{:S(2)}, u32[]{:S(2)}) collective-permute-start(f32[2,64,128]{2,1,0:T(8,128)S(1)} %get-tuple-element.47), channel_id=1, source_target_pairs={{0,3},{1,2},{2,1},{3,0},{4,7},{5,6},{6,5},{7,4},{8,11},{9,10},{10,... | collective-permute-start | bytes 196616 | tf_op jit(solution)/shard_map/ppermute | solution.py:419
  31.9 6.6 %collective-permute-start.9 = (f32[2,64,128]{2,1,0:T(8,128)S(1)}, f32[2,64,128]{2,1,0:T(8,128)S(1)}, u32[]{:S(2)}, u32[]{:S(2)}) collective-permute-start(f32[2,64,128]{2,1,0:T(8,128)S(1)} %get-tuple-element.48), channel_id=1, source_target_pairs={{0,2},{1,3},{2,0},{3,1},{4,6},{5,7},{6,4},{7,5},{8,10},{9,11},{10,... | collective-permute-start | bytes 196616 | tf_op jit(solution)/shard_map/ppermute | solution.py:419
  31.9 6.6 %collective-permute-start.8 = (f32[2,64,128]{2,1,0:T(8,128)S(1)}, f32[2,64,128]{2,1,0:T(8,128)S(1)}, u32[]{:S(2)}, u32[]{:S(2)}) collective-permute-start(f32[2,64,128]{2,1,0:T(8,128)S(1)} %get-tuple-element.49), channel_id=1, source_target_pairs={{0,1},{1,0},{2,3},{3,2},{4,5},{5,4},{6,7},{7,6},{8,9},{9,8},{10,11... | collective-permute-start | bytes 196616 | tf_op jit(solution)/shard_map/ppermute | solution.py:419
  38.6 1.7 %collective-permute-start.11 = (f32[688,128]{1,0:T(8,128)S(1)}, f32[688,128]{1,0:T(8,128)S(1)}, u32[]{:S(2)}, u32[]{:S(2)}) collective-permute-start(f32[688,128]{1,0:T(8,128)S(1)} %get-tuple-element.52), channel_id=1, source_target_pairs={{0,4},{4,0},{8,12},{12,8},{16,20},{20,16},{24,28},{28,24},{1,5},{5... | collective-permute-start | bytes 1056776 | tf_op jit(solution)/shard_map/ppermute | solution.py:419
  40.4 7.7 %collective-permute-start.12 = (f32[344,128]{1,0:T(8,128)S(1)}, f32[344,128]{1,0:T(8,128)S(1)}, u32[]{:S(2)}, u32[]{:S(2)}) collective-permute-start(f32[344,128]{1,0:T(8,128)S(1)} %get-tuple-element.43), channel_id=1, source_target_pairs={{0,8},{4,12},{8,0},{12,4},{16,24},{20,28},{24,16},{28,20},{1,9},{5... | collective-permute-start | bytes 528392 | tf_op jit(solution)/shard_map/ppermute | solution.py:419
  42.1 6.2 %collective-permute-start.14 = (f32[344,128]{1,0:T(8,128)S(1)}, f32[344,128]{1,0:T(8,128)S(1)}, u32[]{:S(2)}, u32[]{:S(2)}) collective-permute-start(f32[344,128]{1,0:T(8,128)S(1)} %get-tuple-element.44), channel_id=1, source_target_pairs={{0,16},{4,20},{8,24},{12,28},{16,0},{20,4},{24,8},{28,12},{1,17},{... | collective-permute-start | bytes 528392 | tf_op jit(solution)/shard_map/ppermute | solution.py:419
  43.6 8.3 %collective-permute-start.7 = (f32[64,512]{1,0:T(8,128)S(1)}, f32[64,512]{1,0:T(8,128)S(1)}, u32[]{:S(2)}, u32[]{:S(2)}) collective-permute-start(f32[64,512]{1,0:T(8,128)S(1)} %get-tuple-element.37), channel_id=1, source_target_pairs={{0,3},{1,2},{2,1},{3,0},{4,7},{5,6},{6,5},{7,4},{8,11},{9,10},{10,... | collective-permute-start | bytes 393224 | tf_op jit(solution)/shard_map/ppermute | solution.py:419
  47.3 10.8 %collective-permute-start.6 = (f32[64,512]{1,0:T(8,128)S(1)}, f32[64,512]{1,0:T(8,128)S(1)}, u32[]{:S(2)}, u32[]{:S(2)}) collective-permute-start(f32[64,512]{1,0:T(8,128)S(1)} %get-tuple-element.38), channel_id=1, source_target_pairs={{0,2},{1,3},{2,0},{3,1},{4,6},{5,7},{6,4},{7,5},{8,10},{9,11},{10,... | collective-permute-start | bytes 393224 | tf_op jit(solution)/shard_map/ppermute | solution.py:419
  47.3 10.8 %collective-permute-start.5 = (f32[64,512]{1,0:T(8,128)S(1)}, f32[64,512]{1,0:T(8,128)S(1)}, u32[]{:S(2)}, u32[]{:S(2)}) collective-permute-start(f32[64,512]{1,0:T(8,128)S(1)} %get-tuple-element.39), channel_id=1, source_target_pairs={{0,1},{1,0},{2,3},{3,2},{4,5},{5,4},{6,7},{7,6},{8,9},{9,8},{10,11... | collective-permute-start | bytes 393224 | tf_op jit(solution)/shard_map/ppermute | solution.py:419
  48.4 14.4 %collective-permute-start.13 = (f32[344,128]{1,0:T(8,128)S(1)}, f32[344,128]{1,0:T(8,128)S(1)}, u32[]{:S(2)}, u32[]{:S(2)}) collective-permute-start(f32[344,128]{1,0:T(8,128)S(1)} %get-tuple-element.41), channel_id=1, source_target_pairs={{0,16},{4,20},{8,24},{12,28},{16,0},{20,4},{24,8},{28,12},{1,17},{... | collective-permute-start | bytes 528392 | tf_op jit(solution)/shard_map/ppermute | solution.py:419
  50.2 12.6 %collective-permute-start.15 = (f32[344,128]{1,0:T(8,128)S(1)}, f32[344,128]{1,0:T(8,128)S(1)}, u32[]{:S(2)}, u32[]{:S(2)}) collective-permute-start(f32[344,128]{1,0:T(8,128)S(1)} %get-tuple-element.42), channel_id=1, source_target_pairs={{0,8},{4,12},{8,0},{12,4},{16,24},{20,28},{24,16},{28,20},{1,9},{5... | collective-permute-start | bytes 528392 | tf_op jit(solution)/shard_map/ppermute | solution.py:419
  59.4 8.8 %all-to-all-start.1 = ((bf16[8,64,128]{2,1,0:T(8,128)(2,1)}), bf16[8,64,128]{2,1,0:T(8,128)(2,1)S(1)}, u32[]{:S(2)}, u32[]{:S(2)}) async-start(bf16[8,64,128]{2,1,0:T(8,128)(2,1)} %shard_map.98), calls=%async_computation.1 | async-start | bytes 262144 | tf_op jit(solution)/shard_map/all_to_all | solution.py:547
  62.9 6.2 %collective-permute-start.16 = (f32[688,128]{1,0:T(8,128)S(1)}, f32[688,128]{1,0:T(8,128)S(1)}, u32[]{:S(2)}, u32[]{:S(2)}) collective-permute-start(f32[688,128]{1,0:T(8,128)S(1)} %pad_maximum_fusion.own_ref), channel_id=1, source_target_pairs={{0,4},{4,0},{8,12},{12,8},{16,20},{20,16},{24,28},{28,24},{1,5},{5... | collective-permute-start | bytes 1056776 | tf_op jit(solution)/shard_map/ppermute | solution.py:419
  (1 other events, 12.7 us)

commit v4 on v3

--- a/solution.py
+++ b/solution.py
@@ -232,16 +232,21 @@
         two_planes(halo + 2 * pair, prev_ref[pair].astype(F32))
         two_planes(halo + edge + 2 * pair, next_ref[pair].astype(F32))
 
+    same_from[same] = 0
+    same_code[same] = 9
+
     def same_layer(item, carry):
-        code = same_code[item]
-        block = lax.shift_right_logical(code, 4)
-        table = edge_ref[code & 15]
-        cells = planes[pl.ds(same_from[item] * 10 + 1, 8)].reshape(8 * channels, LANES)
-        moved = jnp.dot(cells, table, preferred_element_type=F32).astype(BF16)
-        planes[pl.ds(block * 10 + 1, 8)] += moved.reshape(8, channels, LANES)
+        results = []
+        for extra in range(2):
+            code = same_code[2 * item + extra]
+            cells = planes[pl.ds(same_from[2 * item + extra] * 10 + 1, 8)].reshape(8 * channels, LANES)
+            moved = jnp.dot(cells, edge_ref[code & 15], preferred_element_type=F32).astype(BF16)
+            results.append((lax.shift_right_logical(code, 4), moved.reshape(8, channels, LANES)))
+        for block, moved in results:
+            planes[pl.ds(block * 10 + 1, 8)] += moved
         return carry
 
-    lax.fori_loop(0, same, same_layer, 0)
+    lax.fori_loop(0, lax.shift_right_logical(same + 1, 1), same_layer, 0)
     for extra in range(3):
         side_from[side + extra] = dummy - halo + blocks
         side_code[side + extra] = dummy * 32 + 18
@@ -383,11 +388,11 @@
             moved = pltpu.roll(dpre, (k // 3) * PLANE + (k % 3) * 8, 1) if k else dpre
             d9[k * width : (k + 1) * width, lanes] = moved.astype(BF16)
 
-    for j in range(3):
-        part = jnp.dot(d9[...], patches_ref[:, j * channels : (j + 1) * channels], preferred_element_type=F32)
-        for k in range(9):
-            at = (3 * k + j) * width
-            conv_s[at : at + width] = part[k * width : (k + 1) * width]
+    part = jnp.dot(d9[...], patches_ref[...], preferred_element_type=F32)
+    for k in range(27):
+        conv_s[k * width : (k + 1) * width] = part[
+            k // 3 * width : (k // 3 + 1) * width, k % 3 * channels : (k % 3 + 1) * channels
+        ]
     half = keep_out.shape[0]
     keep_out[...] = conv_s[pl.ds(pl.multiple_of(core * half, 8), half), :]
     give_out[...] = conv_s[pl.ds(pl.multiple_of((1 - core) * half, 8), half), :]
@@ -550,17 +555,10 @@
     keep = jnp.concatenate([conv_keep] + [d[0] for d in downs])
     give = jnp.concatenate([conv_give] + [d[1] for d in downs])
     mine = keep + exchange(give, "space", 1)
-    cut = mine.shape[0] // 2
-    first, second = mine[:cut], mine[cut:]
-    steps = []
     step = 2
     while step < peers:
-        steps.append(step)
+        mine = mine + exchange(mine, "space", step)
         step *= 2
-    for near, far in zip(steps, reversed(steps)):
-        first = first + exchange(first, "space", near)
-        second = second + exchange(second, "space", far)
-    mine = jnp.concatenate([first, second])
     other = exchange(mine, "space", 1)
     conv_sum, down_sum = pl.pallas_call(
         functools.partial(finish_kernel, axes, shards, half),

time: 70.9 us -> 68.6 us (0.968)
  starting transfers between devices: 32.8 us -> 29.9 us
  waiting for transfers between devices: 14.9 us -> 16.7 us
  Pallas kernels: 20.5 us -> 19 us
    ppermute x15 -> x13, starting transfers between devices: 20.5 us -> 17.6 us  [exchange(): return lax.ppermute(values, axis, [(i, i ^ step) for i in range(count)])]
    ppermute x15 -> x13, waiting for transfers between devices: 8.14 us -> 9.9 us  [exchange(): return lax.ppermute(values, axis, [(i, i ^ step) for i in range(count)])]
    pallas_call x1, Pallas kernels: 5.77 us -> 4.38 us  [local(): pl.pallas_call(functools.partial(backward_kernel, axes), out_shape=[jax.S...]
  transfers between devices with their start and end apart: 19 -> 17, of which waited for: 5 -> 6; matrix products, arithmetic and copies ran while one was open for 2% -> 2% of each run, Pallas kernels for 24% -> 22%
where the time goes in v4:
time: 68.6 us; the launch traced here: 67.6 us
  starting transfers between devices  29.9 us (44%)
  Pallas kernels  19 us (28%)
  waiting for transfers between devices  16.7 us (24%)
  other arithmetic  0.9 us (1%)
  between operations  0.88 us (1%)
    ppermute x13, starting transfers between devices, exchange(): return lax.ppermute(values, axis, [(i, i ^ step) for i in range(count)])  17.6 us
    ppermute x13, waiting for transfers between devices, exchange(): return lax.ppermute(values, axis, [(i, i ^ step) for i in range(count)])  9.9 us
    pallas_call x1, Pallas kernels, local(): pl.pallas_call(functools.partial(forward_kernel, 'chan'), out_shape=[jax....  8.26 us
    all_to_all x1, starting transfers between devices, local(): lax.all_to_all(packed, 'space', split_axis=0, concat_axis=0, tiled=True)  5.17 us
    all_to_all x1, waiting for transfers between devices, local(): lax.all_to_all(outgoing, 'space', split_axis=0, concat_axis=0, tiled=True)  4.92 us
    pallas_call x1, Pallas kernels, local(): pl.pallas_call(functools.partial(backward_kernel, axes), out_shape=[jax.S...  4.38 us
    all_to_all x1, starting transfers between devices, local(): lax.all_to_all(outgoing, 'space', split_axis=0, concat_axis=0, tiled=True)  3.37 us
    ppermute x1, starting transfers between devices, local(): before = lax.ppermute(tail, 'space', [(i, i + 1) for i in range(ends)])  2.4 us
  transfers between devices with their start and end apart: 17, of which 6 were waited for; matrix products, arithmetic and copies ran while one was open for 2% of the time, Pallas kernels for 22%

profile of v4, /device:TPU:0, one launch (start us, length us, event | category | flops | bytes accessed | tf_op | source)
XLA Modules:
  0.0 67.6 jit_solution(9504611103037170617)
XLA Ops:
  0.7 2.0 %shard_map.94 = (bf16[2,128,128]{2,1,0:T(8,128)(2,1)}, bf16[2,128,128]{2,1,0:T(8,128)(2,1)}, bf16[8,64,128]{2,1,0:T(8,128)(2,1)}) custom-call(bf16[8,128,512]{2,1,0:T(8,128)(2,1)} %feat_hbm.1, bf16[8,128,512]{2,1,0:T(8,128)(2,1)} %feat_hbm.1, s32[8,512]{1,0:T(8,128)} %mask_ref.3, bf16[16,64,64]{2,1,0:T(8,128)(2,1)} %cot_ref.1), custom_call_target="tpu_custom_call" | custom-call | flops 2300000000 | tf_op jit(solution)/shard_map/pallas_call | solution.py:439
  2.7 5.2 %all-to-all-start = ((bf16[8,64,128]{2,1,0:T(8,128)(2,1)}), bf16[8,64,128]{2,1,0:T(8,128)(2,1)S(1)}, u32[]{:S(2)}, u32[]{:S(2)}) async-start(bf16[8,64,128]{2,1,0:T(8,128)(2,1)} %get-tuple-element.20), calls=%async_computation | async-start | bytes 262144 | tf_op jit(solution)/shard_map/all_to_all | solution.py:464
  7.8 2.4 %collective-permute-start = (bf16[2,128,128]{2,1,0:T(8,128)(2,1)}, bf16[2,128,128]{2,1,0:T(8,128)(2,1)S(1)}, u32[]{:S(2)}, u32[]{:S(2)}) collective-permute-start(bf16[2,128,128]{2,1,0:T(8,128)(2,1)} %get-tuple-element.22), channel_id=1, source_target_pairs={{0,4},{4,8},{8,12},{12,16},{16,20},{20,24},{24,28},{1,5},{5,9},{9,... | collective-permute-start | bytes 196616 | tf_op jit(solution)/shard_map/ppermute | solution.py:462
  10.3 1.3 %collective-permute-start.1 = (bf16[2,128,128]{2,1,0:T(8,128)(2,1)}, bf16[2,128,128]{2,1,0:T(8,128)(2,1)S(1)}, u32[]{:S(2)}, u32[]{:S(2)}) collective-permute-start(bf16[2,128,128]{2,1,0:T(8,128)(2,1)} %get-tuple-element.23), channel_id=1, source_target_pairs={{4,0},{8,4},{12,8},{16,12},{20,16},{24,20},{28,24},{5,1},{9,5},{13... | collective-permute-start | bytes 196616 | tf_op jit(solution)/shard_map/ppermute | solution.py:463
  11.6 1.8 %all-to-all-done.returned_ref = bf16[8,64,128]{2,1,0:T(8,128)(2,1)S(1)} async-done(((bf16[8,64,128]{2,1,0:T(8,128)(2,1)}), bf16[8,64,128]{2,1,0:T(8,128)(2,1)S(1)}, u32[]{:S(2)}, u32[]{:S(2)}) %all-to-all-start) | async-done | bytes 131104 | tf_op jit(solution)/shard_map/all_to_all | solution.py:464
  13.4 1.2 %shard_map.95 = (bf16[64,512]{1,0:T(8,128)(2,1)S(1)}, s32[2,8]{1,0:T(2,128)S(1)}) custom-call(s32[1,8]{1,0:T(1,128)S(1)} %bitcast.45, bf16[8,64,128]{2,1,0:T(8,128)(2,1)S(1)} %all-to-all-done.returned_ref), custom_call_target="tpu_custom_call" | custom-call | flops 1724999936 | tf_op jit(solution)/shard_map/pallas_call | solution.py:466
  14.6 3.7 %collective-permute-start.4 = (bf16[64,512]{1,0:T(8,128)(2,1)S(1)}, bf16[64,512]{1,0:T(8,128)(2,1)S(1)}, u32[]{:S(2)}, u32[]{:S(2)}) collective-permute-start(bf16[64,512]{1,0:T(8,128)(2,1)S(1)} %get-tuple-element.25.refs_0_), channel_id=1, source_target_pairs={{0,3},{1,2},{2,1},{3,0},{4,7},{5,6},{6,5},{7,4},{8,11},{9,10},{10,... | collective-permute-start | bytes 196616 | tf_op jit(solution)/shard_map/ppermute | solution.py:424
  18.3 0.8 %collective-permute-start.2 = (bf16[64,512]{1,0:T(8,128)(2,1)S(1)}, bf16[64,512]{1,0:T(8,128)(2,1)S(1)}, u32[]{:S(2)}, u32[]{:S(2)}) collective-permute-start(bf16[64,512]{1,0:T(8,128)(2,1)S(1)} %get-tuple-element.25.refs_0_), channel_id=1, source_target_pairs={{0,1},{1,0},{2,3},{3,2},{4,5},{5,4},{6,7},{7,6},{8,9},{9,8},{10,11... | collective-permute-start | bytes 196616 | tf_op jit(solution)/shard_map/ppermute | solution.py:424
  19.1 8.3 %shard_map.96 = (f32[256,640]{1,0:T(8,128)S(1)}, bf16[256,512]{1,0:T(8,128)(2,1)S(1)}, bf16[7168,384]{1,0:T(8,128)(2,1)S(1)}, bf16[512,640]{1,0:T(8,128)(2,1)S(1)}, bf16[640,1024]{1,0:T(8,128)(2,1)S(1)}) custom-call(bf16[2,128,128]{2,1,0:T(8,128)(2,1)S(1)} %collective-permute-done.prev_ref, bf16[2,128,128]{2,1,0:T(8,128)(2,1)S(1)} %collective-permute-done.1.next_ref, ...), custom_call_target="tpu_custom_call" | custom-call | flops 9200000000 | tf_op jit(solution)/shard_map/pallas_call | solution.py:479
  28.1 3.7 %collective-permute-start.10 = (f32[2,64,128]{2,1,0:T(8,128)S(1)}, f32[2,64,128]{2,1,0:T(8,128)S(1)}, u32[]{:S(2)}, u32[]{:S(2)}) collective-permute-start(f32[2,64,128]{2,1,0:T(8,128)S(1)} %get-tuple-element.43), channel_id=1, source_target_pairs={{0,3},{1,2},{2,1},{3,0},{4,7},{5,6},{6,5},{7,4},{8,11},{9,10},{10,... | collective-permute-start | bytes 196616 | tf_op jit(solution)/shard_map/ppermute | solution.py:424
  31.8 0.8 %collective-permute-start.8 = (f32[2,64,128]{2,1,0:T(8,128)S(1)}, f32[2,64,128]{2,1,0:T(8,128)S(1)}, u32[]{:S(2)}, u32[]{:S(2)}) collective-permute-start(f32[2,64,128]{2,1,0:T(8,128)S(1)} %get-tuple-element.45), channel_id=1, source_target_pairs={{0,1},{1,0},{2,3},{3,2},{4,5},{5,4},{6,7},{7,6},{8,9},{9,8},{10,11... | collective-permute-start | bytes 196616 | tf_op jit(solution)/shard_map/ppermute | solution.py:424
  32.5 4.4 %shard_map.99 = (f32[432,128]{1,0:T(8,128)S(1)}, f32[432,128]{1,0:T(8,128)S(1)}) custom-call(bf16[256,512]{1,0:T(8,128)(2,1)S(1)} %get-tuple-element.27.dp_ref, bf16[8,256,128]{2,1,0:T(8,128)(2,1)S(1)} %copy-done.1, s32[8,512]{1,0:T(8,128)S(1)} %copy-done.3, f32[256,640]{1,0:T(8,128)S(1)} %get-tuple-element.28.pre_ref, ...), custom_call_target="tpu_custom_call" | custom-call | flops 6899999744 | tf_op jit(solution)/shard_map/pallas_call | solution.py:528
  37.6 1.7 %collective-permute-done.11 = f32[688,128]{1,0:T(8,128)S(1)} collective-permute-done((f32[688,128]{1,0:T(8,128)S(1)}, f32[688,128]{1,0:T(8,128)S(1)}, u32[]{:S(2)}, u32[]{:S(2)}) %collective-permute-start.11) | collective-permute-done | bytes 352288 | tf_op jit(solution)/shard_map/ppermute | solution.py:424
  39.3 1.6 %collective-permute-start.12 = (f32[688,128]{1,0:T(8,128)S(1)}, f32[688,128]{1,0:T(8,128)S(1)}, u32[]{:S(2)}, u32[]{:S(2)}) collective-permute-start(f32[688,128]{1,0:T(8,128)S(1)} %add.9), channel_id=1, source_target_pairs={{0,8},{4,12},{8,0},{12,4},{16,24},{20,28},{24,16},{28,20},{1,9},{5... | collective-permute-start | bytes 1056776 | tf_op jit(solution)/shard_map/ppermute | solution.py:424
  40.9 3.7 %collective-permute-start.7 = (f32[64,512]{1,0:T(8,128)S(1)}, f32[64,512]{1,0:T(8,128)S(1)}, u32[]{:S(2)}, u32[]{:S(2)}) collective-permute-start(f32[64,512]{1,0:T(8,128)S(1)} %get-tuple-element.37), channel_id=1, source_target_pairs={{0,3},{1,2},{2,1},{3,0},{4,7},{5,6},{6,5},{7,4},{8,11},{9,10},{10,... | collective-permute-start | bytes 393224 | tf_op jit(solution)/shard_map/ppermute | solution.py:424
  44.5 0.8 %collective-permute-start.5 = (f32[64,512]{1,0:T(8,128)S(1)}, f32[64,512]{1,0:T(8,128)S(1)}, u32[]{:S(2)}, u32[]{:S(2)}) collective-permute-start(f32[64,512]{1,0:T(8,128)S(1)} %get-tuple-element.39), channel_id=1, source_target_pairs={{0,1},{1,0},{2,3},{3,2},{4,5},{5,4},{6,7},{7,6},{8,9},{9,8},{10,11... | collective-permute-start | bytes 393224 | tf_op jit(solution)/shard_map/ppermute | solution.py:424
  45.3 4.3 %collective-permute-done.12 = f32[688,128]{1,0:T(8,128)S(1)} collective-permute-done((f32[688,128]{1,0:T(8,128)S(1)}, f32[688,128]{1,0:T(8,128)S(1)}, u32[]{:S(2)}, u32[]{:S(2)}) %collective-permute-start.12) | collective-permute-done | bytes 352288 | tf_op jit(solution)/shard_map/ppermute | solution.py:424
  49.7 2.1 %collective-permute-start.13 = (f32[688,128]{1,0:T(8,128)S(1)}, f32[688,128]{1,0:T(8,128)S(1)}, u32[]{:S(2)}, u32[]{:S(2)}) collective-permute-start(f32[688,128]{1,0:T(8,128)S(1)} %add.10), channel_id=1, source_target_pairs={{0,16},{4,20},{8,24},{12,28},{16,0},{20,4},{24,8},{28,12},{1,17},{... | collective-permute-start | bytes 1056776 | tf_op jit(solution)/shard_map/ppermute | solution.py:424
  51.8 3.5 %collective-permute-done.6.refs_2_ = f32[64,512]{1,0:T(8,128)S(1)} collective-permute-done((f32[64,512]{1,0:T(8,128)S(1)}, f32[64,512]{1,0:T(8,128)S(1)}, u32[]{:S(2)}, u32[]{:S(2)}) %collective-permute-start.6) | collective-permute-done | bytes 131104 | tf_op jit(solution)/shard_map/ppermute | solution.py:424
  55.3 1.3 %shard_map.98 = bf16[8,64,128]{2,1,0:T(8,128)(2,1)} custom-call(s32[2,8]{1,0:T(2,128)S(1)} %get-tuple-element.21.rank_ref, f32[64,512]{1,0:T(8,128)S(1)} %get-tuple-element.40.refs_0_, f32[64,512]{1,0:T(8,128)S(1)} %collective-permute-done.5.refs_1_, f32[64,512]{1,0:T(8,128)S(1)} %collective-permute-done.6.refs_2_, f32[64,512]{1,0:T(8,128)S(1)} %collective-permute-done.7.refs_3_), custom_call_target="tpu_custom_call" | custom-call | flops 1724999936 | tf_op jit(solution)/shard_map/pallas_call | solution.py:544
  56.7 3.4 %all-to-all-start.1 = ((bf16[8,64,128]{2,1,0:T(8,128)(2,1)}), bf16[8,64,128]{2,1,0:T(8,128)(2,1)S(1)}, u32[]{:S(2)}, u32[]{:S(2)}) async-start(bf16[8,64,128]{2,1,0:T(8,128)(2,1)} %shard_map.98), calls=%async_computation.1 | async-start | bytes 262144 | tf_op jit(solution)/shard_map/all_to_all | solution.py:552
  60.6 4.9 %all-to-all-done.1 = bf16[8,64,128]{2,1,0:T(8,128)(2,1)S(1)} async-done(((bf16[8,64,128]{2,1,0:T(8,128)(2,1)}), bf16[8,64,128]{2,1,0:T(8,128)(2,1)S(1)}, u32[]{:S(2)}, u32[]{:S(2)}) %all-to-all-start.1) | async-done | bytes 131104 | tf_op jit(solution)/shard_map/all_to_all | solution.py:552
  65.6 0.8 %pad_maximum_fusion = bf16[8,128,64]{2,1,0:T(8,128)(2,1)} fusion(bf16[8,64,64]{2,1,0:T(8,128)(2,1)S(1)} %get-tuple-element.47, bf16[8,64,64]{2,1,0:T(8,128)(2,1)S(1)} %get-tuple-element.46), kind=kLoop, calls=%fused_computation | loop fusion | flops 262144 | bytes 262144 | tf_op jit(solution)/shard_map/concatenate
  66.4 1.2 %shard_map.100 = (f32[864,128]{1,0:T(8,128)}, f32[8,64,128]{2,1,0:T(8,128)}) custom-call(f32[688,128]{1,0:T(8,128)S(1)} %add.11.own_ref, f32[688,128]{1,0:T(8,128)S(1)} %collective-permute-done.14.other_ref), custom_call_target="tpu_custom_call" | custom-call | flops 1724999936 | tf_op jit(solution)/shard_map/pallas_call | solution.py:563
  (41 shorter events, 2.1 us)
Async XLA Ops:
  0.6 18.4 %copy-start.3 = (s32[8,512]{1,0:T(8,128)S(1)}, s32[8,512]{1,0:T(8,128)}, u32[]{:S(2)}) copy-start(s32[8,512]{1,0:T(8,128)} %mask_ref.3) | copy-start | bytes 49156
  0.6 18.4 %copy-start = (bf16[8,128,512]{2,1,0:T(8,128)(2,1)S(1)}, bf16[8,128,512]{2,1,0:T(8,128)(2,1)}, u32[]{:S(2)}) copy-start(bf16[8,128,512]{2,1,0:T(8,128)(2,1)} %feat_hbm.1) | copy-start | bytes 3145732
  0.7 12.7 %copy-start.5 = (s32[8,1]{0,1:T(1,128)S(1)}, s32[8,1]{0,1:T(1,128)}, u32[]{:S(2)}) copy-start(s32[8,1]{0,1:T(1,128)} %param.12) | copy-start | bytes 100
  0.7 18.4 %copy-start.2 = (bf16[27,32,128]{2,1,0:T(8,128)(2,1)S(1)}, bf16[27,32,128]{2,1,0:T(8,128)(2,1)}, u32[]{:S(2)}) copy-start(bf16[27,32,128]{2,1,0:T(8,128)(2,1)} %wconv_hbm.1) | copy-start | bytes 663556
  0.7 18.4 %copy-start.4 = (s32[8,26]{1,0:T(8,128)S(1)}, s32[8,26]{1,0:T(8,128)}, u32[]{:S(2)}) copy-start(s32[8,26]{1,0:T(8,128)} %nbr_hbm.1) | copy-start | bytes 2500
  2.7 10.7 %all-to-all-start = ((bf16[8,64,128]{2,1,0:T(8,128)(2,1)}), bf16[8,64,128]{2,1,0:T(8,128)(2,1)S(1)}, u32[]{:S(2)}, u32[]{:S(2)}) async-start(bf16[8,64,128]{2,1,0:T(8,128)(2,1)} %get-tuple-element.20), calls=%async_computation | async-start | bytes 262144 | tf_op jit(solution)/shard_map/all_to_all | solution.py:464
  7.8 11.2 %collective-permute-start = (bf16[2,128,128]{2,1,0:T(8,128)(2,1)}, bf16[2,128,128]{2,1,0:T(8,128)(2,1)S(1)}, u32[]{:S(2)}, u32[]{:S(2)}) collective-permute-start(bf16[2,128,128]{2,1,0:T(8,128)(2,1)} %get-tuple-element.22), channel_id=1, source_target_pairs={{0,4},{4,8},{8,12},{12,16},{16,20},{20,24},{24,28},{1,5},{5,9},{9,... | collective-permute-start | bytes 196616 | tf_op jit(solution)/shard_map/ppermute | solution.py:462
  10.3 8.8 %collective-permute-start.1 = (bf16[2,128,128]{2,1,0:T(8,128)(2,1)}, bf16[2,128,128]{2,1,0:T(8,128)(2,1)S(1)}, u32[]{:S(2)}, u32[]{:S(2)}) collective-permute-start(bf16[2,128,128]{2,1,0:T(8,128)(2,1)} %get-tuple-element.23), channel_id=1, source_target_pairs={{4,0},{8,4},{12,8},{16,12},{20,16},{24,20},{28,24},{5,1},{9,5},{13... | collective-permute-start | bytes 196616 | tf_op jit(solution)/shard_map/ppermute | solution.py:463
  14.6 12.8 %copy-start.1 = (bf16[8,256,128]{2,1,0:T(8,128)(2,1)S(1)}, bf16[8,256,128]{2,1,0:T(8,128)(2,1)}, u32[]{:S(2)}) copy-start(bf16[8,256,128]{2,1,0:T(8,128)(2,1)} %wdown_ref.3) | copy-start | bytes 1572868
  14.6 12.8 %collective-permute-start.4 = (bf16[64,512]{1,0:T(8,128)(2,1)S(1)}, bf16[64,512]{1,0:T(8,128)(2,1)S(1)}, u32[]{:S(2)}, u32[]{:S(2)}) collective-permute-start(bf16[64,512]{1,0:T(8,128)(2,1)S(1)} %get-tuple-element.25.refs_0_), channel_id=1, source_target_pairs={{0,3},{1,2},{2,1},{3,0},{4,7},{5,6},{6,5},{7,4},{8,11},{9,10},{10,... | collective-permute-start | bytes 196616 | tf_op jit(solution)/shard_map/ppermute | solution.py:424
  18.3 9.1 %collective-permute-start.3 = (bf16[64,512]{1,0:T(8,128)(2,1)S(1)}, bf16[64,512]{1,0:T(8,128)(2,1)S(1)}, u32[]{:S(2)}, u32[]{:S(2)}) collective-permute-start(bf16[64,512]{1,0:T(8,128)(2,1)S(1)} %get-tuple-element.25.refs_0_), channel_id=1, source_target_pairs={{0,2},{1,3},{2,0},{3,1},{4,6},{5,7},{6,4},{7,5},{8,10},{9,11},{10,... | collective-permute-start | bytes 196616 | tf_op jit(solution)/shard_map/ppermute | solution.py:424
  18.3 9.1 %collective-permute-start.2 = (bf16[64,512]{1,0:T(8,128)(2,1)S(1)}, bf16[64,512]{1,0:T(8,128)(2,1)S(1)}, u32[]{:S(2)}, u32[]{:S(2)}) collective-permute-start(bf16[64,512]{1,0:T(8,128)(2,1)S(1)} %get-tuple-element.25.refs_0_), channel_id=1, source_target_pairs={{0,1},{1,0},{2,3},{3,2},{4,5},{5,4},{6,7},{7,6},{8,9},{9,8},{10,11... | collective-permute-start | bytes 196616 | tf_op jit(solution)/shard_map/ppermute | solution.py:424
  28.1 9.4 %collective-permute-start.10 = (f32[2,64,128]{2,1,0:T(8,128)S(1)}, f32[2,64,128]{2,1,0:T(8,128)S(1)}, u32[]{:S(2)}, u32[]{:S(2)}) collective-permute-start(f32[2,64,128]{2,1,0:T(8,128)S(1)} %get-tuple-element.43), channel_id=1, source_target_pairs={{0,3},{1,2},{2,1},{3,0},{4,7},{5,6},{6,5},{7,4},{8,11},{9,10},{10,... | collective-permute-start | bytes 196616 | tf_op jit(solution)/shard_map/ppermute | solution.py:424
  31.8 5.7 %collective-permute-start.9 = (f32[2,64,128]{2,1,0:T(8,128)S(1)}, f32[2,64,128]{2,1,0:T(8,128)S(1)}, u32[]{:S(2)}, u32[]{:S(2)}) collective-permute-start(f32[2,64,128]{2,1,0:T(8,128)S(1)} %get-tuple-element.44), channel_id=1, source_target_pairs={{0,2},{1,3},{2,0},{3,1},{4,6},{5,7},{6,4},{7,5},{8,10},{9,11},{10,... | collective-permute-start | bytes 196616 | tf_op jit(solution)/shard_map/ppermute | solution.py:424
  31.8 5.7 %collective-permute-start.8 = (f32[2,64,128]{2,1,0:T(8,128)S(1)}, f32[2,64,128]{2,1,0:T(8,128)S(1)}, u32[]{:S(2)}, u32[]{:S(2)}) collective-permute-start(f32[2,64,128]{2,1,0:T(8,128)S(1)} %get-tuple-element.45), channel_id=1, source_target_pairs={{0,1},{1,0},{2,3},{3,2},{4,5},{5,4},{6,7},{7,6},{8,9},{9,8},{10,11... | collective-permute-start | bytes 196616 | tf_op jit(solution)/shard_map/ppermute | solution.py:424
  37.5 1.7 %collective-permute-start.11 = (f32[688,128]{1,0:T(8,128)S(1)}, f32[688,128]{1,0:T(8,128)S(1)}, u32[]{:S(2)}, u32[]{:S(2)}) collective-permute-start(f32[688,128]{1,0:T(8,128)S(1)} %get-tuple-element.48), channel_id=1, source_target_pairs={{0,4},{4,0},{8,12},{12,8},{16,20},{20,16},{24,28},{28,24},{1,5},{5... | collective-permute-start | bytes 1056776 | tf_op jit(solution)/shard_map/ppermute | solution.py:424
  39.3 10.3 %collective-permute-start.12 = (f32[688,128]{1,0:T(8,128)S(1)}, f32[688,128]{1,0:T(8,128)S(1)}, u32[]{:S(2)}, u32[]{:S(2)}) collective-permute-start(f32[688,128]{1,0:T(8,128)S(1)} %add.9), channel_id=1, source_target_pairs={{0,8},{4,12},{8,0},{12,4},{16,24},{20,28},{24,16},{28,20},{1,9},{5... | collective-permute-start | bytes 1056776 | tf_op jit(solution)/shard_map/ppermute | solution.py:424
  40.9 10.9 %collective-permute-start.7 = (f32[64,512]{1,0:T(8,128)S(1)}, f32[64,512]{1,0:T(8,128)S(1)}, u32[]{:S(2)}, u32[]{:S(2)}) collective-permute-start(f32[64,512]{1,0:T(8,128)S(1)} %get-tuple-element.37), channel_id=1, source_target_pairs={{0,3},{1,2},{2,1},{3,0},{4,7},{5,6},{6,5},{7,4},{8,11},{9,10},{10,... | collective-permute-start | bytes 393224 | tf_op jit(solution)/shard_map/ppermute | solution.py:424
  44.5 10.8 %collective-permute-start.6 = (f32[64,512]{1,0:T(8,128)S(1)}, f32[64,512]{1,0:T(8,128)S(1)}, u32[]{:S(2)}, u32[]{:S(2)}) collective-permute-start(f32[64,512]{1,0:T(8,128)S(1)} %get-tuple-element.38), channel_id=1, source_target_pairs={{0,2},{1,3},{2,0},{3,1},{4,6},{5,7},{6,4},{7,5},{8,10},{9,11},{10,... | collective-permute-start | bytes 393224 | tf_op jit(solution)/shard_map/ppermute | solution.py:424
  44.5 10.8 %collective-permute-start.5 = (f32[64,512]{1,0:T(8,128)S(1)}, f32[64,512]{1,0:T(8,128)S(1)}, u32[]{:S(2)}, u32[]{:S(2)}) collective-permute-start(f32[64,512]{1,0:T(8,128)S(1)} %get-tuple-element.39), channel_id=1, source_target_pairs={{0,1},{1,0},{2,3},{3,2},{4,5},{5,4},{6,7},{7,6},{8,9},{9,8},{10,11... | collective-permute-start | bytes 393224 | tf_op jit(solution)/shard_map/ppermute | solution.py:424
  49.7 10.4 %collective-permute-start.13 = (f32[688,128]{1,0:T(8,128)S(1)}, f32[688,128]{1,0:T(8,128)S(1)}, u32[]{:S(2)}, u32[]{:S(2)}) collective-permute-start(f32[688,128]{1,0:T(8,128)S(1)} %add.10), channel_id=1, source_target_pairs={{0,16},{4,20},{8,24},{12,28},{16,0},{20,4},{24,8},{28,12},{1,17},{... | collective-permute-start | bytes 1056776 | tf_op jit(solution)/shard_map/ppermute | solution.py:424
  56.7 8.8 %all-to-all-start.1 = ((bf16[8,64,128]{2,1,0:T(8,128)(2,1)}), bf16[8,64,128]{2,1,0:T(8,128)(2,1)S(1)}, u32[]{:S(2)}, u32[]{:S(2)}) async-start(bf16[8,64,128]{2,1,0:T(8,128)(2,1)} %shard_map.98), calls=%async_computation.1 | async-start | bytes 262144 | tf_op jit(solution)/shard_map/all_to_all | solution.py:552
  60.1 6.3 %collective-permute-start.14 = (f32[688,128]{1,0:T(8,128)S(1)}, f32[688,128]{1,0:T(8,128)S(1)}, u32[]{:S(2)}, u32[]{:S(2)}) collective-permute-start(f32[688,128]{1,0:T(8,128)S(1)} %add.11.own_ref), channel_id=1, source_target_pairs={{0,4},{4,0},{8,12},{12,8},{16,20},{20,16},{24,28},{28,24},{1,5},{5... | collective-permute-start | bytes 1056776 | tf_op jit(solution)/shard_map/ppermute | solution.py:424

commit v5 on v4

--- a/solution.py
+++ b/solution.py
@@ -23,10 +23,6 @@
     return pl.BlockSpec(memory_space=pltpu.VMEM)
 
 
-def smem():
-    return pl.BlockSpec(memory_space=pltpu.SMEM)
-
-
 def cost(microseconds):
     return pl.CostEstimate(flops=int(microseconds * 1.15e9), bytes_accessed=0, transcendentals=0)
 
@@ -75,8 +71,7 @@
     cell = column(PLANE)
     octant = 4 * (plane % 2) + 2 * ((cell >> 3) & 1) + (cell & 1)
     place = 16 * (plane // 2) + 4 * ((cell >> 4) & 3) + ((cell >> 1) & 3)
-    lane = row(8 * LANES)
-    return equal(jnp.where(cell < 64, octant * 64 + place, -1), (lane >> 7) * 64 + (lane & 63))
+    return equal(jnp.where(cell < 64, octant * 64 + place, -1), row(8 * 64))
 
 
 def low_half(rows):
@@ -103,37 +98,48 @@
         cot_out[peer] = jnp.concatenate(pair, axis=1).astype(BF16)
 
 
-def pick_kernel(owner_ref, returned_ref, out_ref, rank_ref):
+def pick_kernel(owner_ref, returned_ref, out_ref, slot_ref):
     blocks = owner_ref.shape[1]
-    low = low_half(out_ref.shape[0])
+    share = out_ref.shape[0]
+    low = low_half(share)
+    owners = owner_ref[...].astype(F32)
+    block = lax.broadcasted_iota(jnp.int32, (blocks, blocks), 0)
+    other = lax.broadcasted_iota(jnp.int32, (blocks, blocks), 1)
+    owner = jnp.sum(jnp.where(block == other, owners, 0.0), axis=1, keepdims=True)
+    rank = jnp.sum(jnp.where((owner == owners) & (other < block), 1.0, 0.0), axis=1, keepdims=True)
+    slots = jnp.broadcast_to((2.0 * owner + rank).astype(jnp.int32), (blocks, LANES))
+    slot_ref[...] = slots
+    sources = [returned_ref[peer].astype(F32) for peer in range(returned_ref.shape[0])]
     for pair in range(blocks // 2):
-        rows = []
+        tiles = []
         for side in range(2):
-            block = 2 * pair + side
-            owner = owner_ref[0, block]
-            rank = jnp.int32(0)
-            for earlier in range(block):
-                rank = rank + (owner_ref[0, earlier] == owner).astype(jnp.int32)
-            rank_ref[0, block] = owner
-            rank_ref[1, block] = rank
-            tile = returned_ref[owner].astype(F32)
-            rows.append(jnp.where(rank == side, tile, swap_halves(tile)))
-        out_ref[:, pair * LANES : (pair + 1) * LANES] = jnp.where(low, rows[0], rows[1]).astype(BF16)
-
-
-def route_kernel(rank_ref, *refs):
+            slot = jnp.broadcast_to(slots[2 * pair + side : 2 * pair + side + 1], (share, LANES))
+            tile = sources[0]
+            for peer in range(1, len(sources)):
+                tile = jnp.where((slot >> 1) == peer, sources[peer], tile)
+            tiles.append(jnp.where((slot & 1) == side, tile, swap_halves(tile)))
+        out_ref[:, pair * LANES : (pair + 1) * LANES] = jnp.where(low, tiles[0], tiles[1]).astype(BF16)
+
+
+def route_kernel(slot_ref, *refs):
     out_ref = refs[-1]
-    blocks = rank_ref.shape[1]
-    half = lax.broadcasted_iota(jnp.int32, (out_ref.shape[1], LANES), 1) // 64
-    out_ref[...] = jnp.zeros_like(out_ref)
+    blocks, share = slot_ref.shape[0], out_ref.shape[1]
+    half = lax.broadcasted_iota(jnp.int32, (share, LANES), 1) // 64
+    pieces = []
     for block in range(blocks):
         lanes = slice(block // 2 * LANES, (block // 2 + 1) * LANES)
         total = refs[0][:, lanes]
         for ref in refs[1:-1]:
             total = total + ref[:, lanes]
-        owner, rank = rank_ref[0, block], rank_ref[1, block]
+        slot = jnp.broadcast_to(slot_ref[block : block + 1, :], (share, LANES))
+        rank = slot & 1
         tile = jnp.where(rank == block % 2, total, swap_halves(total))
-        out_ref[owner] += jnp.where(half == rank, tile, 0.0).astype(BF16)
+        pieces.append((jnp.where(half == rank, slot >> 1, -1), tile))
+    for peer in range(out_ref.shape[0]):
+        tile = jnp.zeros((share, LANES), F32)
+        for owner, piece in pieces:
+            tile = jnp.where(owner == peer, piece, tile)
+        out_ref[peer] = tile.astype(BF16)
 
 
 def forward_kernel(
@@ -309,14 +315,16 @@
 
     split_up = jnp.dot(hidden_s[...], octant_ref[...], preferred_element_type=F32)
     low = low_half(width)
-    for octant in range(8):
-        lanes = slice(octant * LANES, (octant + 1) * LANES)
+    for octant in range(0, 8, 2):
+        lanes = slice(octant * 64, octant * 64 + LANES)
         for pair in range(blocks // 2):
             even = split_up[2 * pair * width : (2 * pair + 1) * width, lanes]
             odd = split_up[(2 * pair + 1) * width : (2 * pair + 2) * width, lanes]
-            octs_out[octant * width : (octant + 1) * width, pair * LANES : (pair + 1) * LANES] = jnp.where(
-                low, even, odd
-            ).astype(BF16)
+            at = slice(pair * LANES, (pair + 1) * LANES)
+            first = jnp.where(low, even, swap_halves(odd)).astype(BF16)
+            second = jnp.where(low, swap_halves(even), odd).astype(BF16)
+            octs_out[octant * width : (octant + 1) * width, at] = first
+            octs_out[(octant + 1) * width : (octant + 2) * width, at] = second
 
 
 def down_kernel(axes, shards, octs_ref, wdown_ref, *refs):
@@ -360,18 +368,19 @@
 
     for octant in range(8):
         dh_s[octant] = lax.dot_general(wdown_ref[octant], dp_ref[...], TN, preferred_element_type=F32)
-    for octant in range(8):
-        lanes = slice(octant * LANES, (octant + 1) * LANES)
+    for octant in range(0, 8, 2):
+        lanes = slice(octant * 64, octant * 64 + LANES)
         for pair in range(blocks // 2):
-            tile = dh_s[octant, own_rows, pair * LANES : (pair + 1) * LANES]
-            high = tile.astype(BF16).astype(F32)
-            rest = tile - high
-            even = slice(2 * pair * width, (2 * pair + 1) * width)
-            odd = slice((2 * pair + 1) * width, (2 * pair + 2) * width)
-            dhi[even, lanes] = jnp.where(low, high, 0.0).astype(BF16)
-            dhi[odd, lanes] = jnp.where(low, 0.0, high).astype(BF16)
-            dlo[even, lanes] = jnp.where(low, rest, 0.0).astype(BF16)
-            dlo[odd, lanes] = jnp.where(low, 0.0, rest).astype(BF16)
+            at = slice(pair * LANES, (pair + 1) * LANES)
+            first, second = dh_s[octant, own_rows, at], dh_s[octant + 1, own_rows, at]
+            for block, tile in (
+                (2 * pair, jnp.where(low, first, swap_halves(second))),
+                (2 * pair + 1, jnp.where(low, swap_halves(first), second)),
+            ):
+                rows = slice(block * width, (block + 1) * width)
+                high = tile.astype(BF16)
+                dhi[rows, lanes] = high
+                dlo[rows, lanes] = (tile - high.astype(F32)).astype(BF16)
     dhidden = lax.dot_general(dhi[...], octant_ref[...], NT, preferred_element_type=F32)
     dhidden = dhidden + lax.dot_general(dlo[...], octant_ref[...], NT, preferred_element_type=F32)
     keeps = jnp.dot(mask_ref[...].astype(F32).astype(BF16), spread_ref[...], preferred_element_type=F32)
@@ -467,10 +476,10 @@
         pick_kernel,
         out_shape=[
             jax.ShapeDtypeStruct((share, lanes), BF16),
-            jax.ShapeDtypeStruct((2, blocks), jnp.int32),
-        ],
-        in_specs=[smem(), vmem()],
-        out_specs=[vmem(), smem()],
+            jax.ShapeDtypeStruct((blocks, LANES), jnp.int32),
+        ],
+        in_specs=[vmem()] * 2,
+        out_specs=[vmem()] * 2,
         cost_estimate=cost(1.5),
         compiler_params=pltpu.CompilerParams(vmem_limit_bytes=8 * MIB),
     )(coarse_owner.reshape(1, blocks), returned)
@@ -483,7 +492,7 @@
             jax.ShapeDtypeStruct((8 * width, lanes), BF16),
             jax.ShapeDtypeStruct((blocks * STRIDE, 3 * channels), BF16),
             jax.ShapeDtypeStruct((512, SPAN), BF16),
-            jax.ShapeDtypeStruct((SPAN, 8 * LANES), BF16),
+            jax.ShapeDtypeStruct((SPAN, 8 * 64), BF16),
         ],
         in_specs=[vmem()] * 2 + [pl.BlockSpec(memory_space=pltpu.HBM)] * 4,
         out_specs=[vmem()] * 5,
@@ -532,8 +541,8 @@
         out_specs=[vmem()] * 2,
         scratch_shapes=[
             pltpu.VMEM((8, channels, lanes), F32),
-            pltpu.VMEM((blocks * width, 8 * LANES), BF16),
-            pltpu.VMEM((blocks * width, 8 * LANES), BF16),
+            pltpu.VMEM((blocks * width, 8 * 64), BF16),
+            pltpu.VMEM((blocks * width, 8 * 64), BF16),
             pltpu.VMEM((9 * width, blocks * STRIDE), BF16),
             pltpu.VMEM((27 * width, channels), F32),
         ],
@@ -544,7 +553,7 @@
     outgoing = pl.pallas_call(
         route_kernel,
         out_shape=jax.ShapeDtypeStruct((peers, share, capacity * 64), BF16),
-        in_specs=[smem()] + [vmem()] * shards,
+        in_specs=[vmem()] * (1 + shards),
         out_specs=vmem(),
         cost_estimate=cost(1.5),
         compiler_params=pltpu.CompilerParams(vmem_limit_bytes=8 * MIB),

time: 68.6 us -> 66.9 us (0.975)
  Pallas kernels: 19 us -> 16.6 us
  starting transfers between devices: 29.9 us -> 31.1 us
    ppermute x13, starting transfers between devices: 17.6 us -> 18.8 us  [exchange(): return lax.ppermute(values, axis, [(i, i ^ step) for i in range(count)])]
    pallas_call x1, Pallas kernels: 1.18 us -> 0.32 us  [local(): pl.pallas_call(pick_kernel, out_shape=[jax.ShapeDtypeStruct((share, lanes...]
  transfers between devices with their start and end apart: 17 -> 17, of which waited for: 6 -> 7; matrix products, arithmetic and copies ran while one was open for 2% -> 2% of each run, Pallas kernels for 22% -> 19%
where the time goes in v5:
time: 66.9 us; the launch traced here: 66.5 us
  starting transfers between devices  31.1 us (46%)
  waiting for transfers between devices  16.8 us (25%)
  Pallas kernels  16.6 us (25%)
  other arithmetic  0.9 us (1%)
  between operations  0.86 us (1%)
    ppermute x13, starting transfers between devices, exchange(): return lax.ppermute(values, axis, [(i, i ^ step) for i in range(count)])  18.8 us
    ppermute x13, waiting for transfers between devices, exchange(): return lax.ppermute(values, axis, [(i, i ^ step) for i in range(count)])  10.1 us
    pallas_call x1, Pallas kernels, local(): pl.pallas_call(functools.partial(forward_kernel, 'chan'), out_shape=[jax....  7.69 us
    all_to_all x1, starting transfers between devices, local(): lax.all_to_all(packed, 'space', split_axis=0, concat_axis=0, tiled=True)  5.17 us
    all_to_all x1, waiting for transfers between devices, local(): lax.all_to_all(outgoing, 'space', split_axis=0, concat_axis=0, tiled=True)  4.94 us
    pallas_call x1, Pallas kernels, local(): pl.pallas_call(functools.partial(backward_kernel, axes), out_shape=[jax.S...  3.87 us
    all_to_all x1, starting transfers between devices, local(): lax.all_to_all(outgoing, 'space', split_axis=0, concat_axis=0, tiled=True)  3.37 us
    ppermute x1, starting transfers between devices, local(): before = lax.ppermute(tail, 'space', [(i, i + 1) for i in range(ends)])  2.4 us
  transfers between devices with their start and end apart: 17, of which 7 were waited for; matrix products, arithmetic and copies ran while one was open for 2% of the time, Pallas kernels for 19%

profile of v5, /device:TPU:0, one launch (start us, length us, event | category | flops | bytes accessed | tf_op | source)
XLA Modules:
  0.0 66.5 jit_solution(9898792102007349269)
XLA Ops:
  0.7 2.0 %shard_map.94 = (bf16[2,128,128]{2,1,0:T(8,128)(2,1)}, bf16[2,128,128]{2,1,0:T(8,128)(2,1)}, bf16[8,64,128]{2,1,0:T(8,128)(2,1)}) custom-call(bf16[8,128,512]{2,1,0:T(8,128)(2,1)} %feat_hbm.1, bf16[8,128,512]{2,1,0:T(8,128)(2,1)} %feat_hbm.1, s32[8,512]{1,0:T(8,128)} %mask_ref.3, bf16[16,64,64]{2,1,0:T(8,128)(2,1)} %cot_ref.1), custom_call_target="tpu_custom_call" | custom-call | flops 2300000000 | tf_op jit(solution)/shard_map/pallas_call | solution.py:448
  2.7 5.2 %all-to-all-start = ((bf16[8,64,128]{2,1,0:T(8,128)(2,1)}), bf16[8,64,128]{2,1,0:T(8,128)(2,1)S(1)}, u32[]{:S(2)}, u32[]{:S(2)}) async-start(bf16[8,64,128]{2,1,0:T(8,128)(2,1)} %get-tuple-element.20), calls=%async_computation | async-start | bytes 262144 | tf_op jit(solution)/shard_map/all_to_all | solution.py:473
  7.8 2.4 %collective-permute-start = (bf16[2,128,128]{2,1,0:T(8,128)(2,1)}, bf16[2,128,128]{2,1,0:T(8,128)(2,1)S(1)}, u32[]{:S(2)}, u32[]{:S(2)}) collective-permute-start(bf16[2,128,128]{2,1,0:T(8,128)(2,1)} %get-tuple-element.22), channel_id=1, source_target_pairs={{0,4},{4,8},{8,12},{12,16},{16,20},{20,24},{24,28},{1,5},{5,9},{9,... | collective-permute-start | bytes 196616 | tf_op jit(solution)/shard_map/ppermute | solution.py:471
  10.3 1.3 %collective-permute-start.1 = (bf16[2,128,128]{2,1,0:T(8,128)(2,1)}, bf16[2,128,128]{2,1,0:T(8,128)(2,1)S(1)}, u32[]{:S(2)}, u32[]{:S(2)}) collective-permute-start(bf16[2,128,128]{2,1,0:T(8,128)(2,1)} %get-tuple-element.23), channel_id=1, source_target_pairs={{4,0},{8,4},{12,8},{16,12},{20,16},{24,20},{28,24},{5,1},{9,5},{13... | collective-permute-start | bytes 196616 | tf_op jit(solution)/shard_map/ppermute | solution.py:472
  11.6 1.8 %all-to-all-done.returned_ref = bf16[8,64,128]{2,1,0:T(8,128)(2,1)S(1)} async-done(((bf16[8,64,128]{2,1,0:T(8,128)(2,1)}), bf16[8,64,128]{2,1,0:T(8,128)(2,1)S(1)}, u32[]{:S(2)}, u32[]{:S(2)}) %all-to-all-start) | async-done | bytes 131104 | tf_op jit(solution)/shard_map/all_to_all | solution.py:473
  13.7 3.7 %collective-permute-start.4 = (bf16[64,512]{1,0:T(8,128)(2,1)S(1)}, bf16[64,512]{1,0:T(8,128)(2,1)S(1)}, u32[]{:S(2)}, u32[]{:S(2)}) collective-permute-start(bf16[64,512]{1,0:T(8,128)(2,1)S(1)} %get-tuple-element.25.refs_0_), channel_id=1, source_target_pairs={{0,3},{1,2},{2,1},{3,0},{4,7},{5,6},{6,5},{7,4},{8,11},{9,10},{10,... | collective-permute-start | bytes 196616 | tf_op jit(solution)/shard_map/ppermute | solution.py:433
  17.4 0.8 %collective-permute-start.2 = (bf16[64,512]{1,0:T(8,128)(2,1)S(1)}, bf16[64,512]{1,0:T(8,128)(2,1)S(1)}, u32[]{:S(2)}, u32[]{:S(2)}) collective-permute-start(bf16[64,512]{1,0:T(8,128)(2,1)S(1)} %get-tuple-element.25.refs_0_), channel_id=1, source_target_pairs={{0,1},{1,0},{2,3},{3,2},{4,5},{5,4},{6,7},{7,6},{8,9},{9,8},{10,11... | collective-permute-start | bytes 196616 | tf_op jit(solution)/shard_map/ppermute | solution.py:433
  18.2 7.7 %shard_map.96 = (f32[256,640]{1,0:T(8,128)S(1)}, bf16[256,512]{1,0:T(8,128)(2,1)S(1)}, bf16[7168,384]{1,0:T(8,128)(2,1)S(1)}, bf16[512,640]{1,0:T(8,128)(2,1)S(1)}, bf16[640,512]{1,0:T(8,128)(2,1)S(1)}) custom-call(bf16[2,128,128]{2,1,0:T(8,128)(2,1)S(1)} %collective-permute-done.prev_ref, bf16[2,128,128]{2,1,0:T(8,128)(2,1)S(1)} %collective-permute-done.1.next_ref, ...), custom_call_target="tpu_custom_call" | custom-call | flops 9200000000 | tf_op jit(solution)/shard_map/pallas_call | solution.py:488
  26.6 3.7 %collective-permute-start.10 = (f32[2,64,128]{2,1,0:T(8,128)S(1)}, f32[2,64,128]{2,1,0:T(8,128)S(1)}, u32[]{:S(2)}, u32[]{:S(2)}) collective-permute-start(f32[2,64,128]{2,1,0:T(8,128)S(1)} %get-tuple-element.43), channel_id=1, source_target_pairs={{0,3},{1,2},{2,1},{3,0},{4,7},{5,6},{6,5},{7,4},{8,11},{9,10},{10,... | collective-permute-start | bytes 196616 | tf_op jit(solution)/shard_map/ppermute | solution.py:433
  30.3 0.8 %collective-permute-start.8 = (f32[2,64,128]{2,1,0:T(8,128)S(1)}, f32[2,64,128]{2,1,0:T(8,128)S(1)}, u32[]{:S(2)}, u32[]{:S(2)}) collective-permute-start(f32[2,64,128]{2,1,0:T(8,128)S(1)} %get-tuple-element.45), channel_id=1, source_target_pairs={{0,1},{1,0},{2,3},{3,2},{4,5},{5,4},{6,7},{7,6},{8,9},{9,8},{10,11... | collective-permute-start | bytes 196616 | tf_op jit(solution)/shard_map/ppermute | solution.py:433
  31.1 3.9 %shard_map.99 = (f32[432,128]{1,0:T(8,128)S(1)}, f32[432,128]{1,0:T(8,128)S(1)}) custom-call(bf16[256,512]{1,0:T(8,128)(2,1)S(1)} %get-tuple-element.27.dp_ref, bf16[8,256,128]{2,1,0:T(8,128)(2,1)S(1)} %copy-done.1, s32[8,512]{1,0:T(8,128)S(1)} %copy-done.3, f32[256,640]{1,0:T(8,128)S(1)} %get-tuple-element.28.pre_ref, ...), custom_call_target="tpu_custom_call" | custom-call | flops 6899999744 | tf_op jit(solution)/shard_map/pallas_call | solution.py:537
  35.0 0.9 %collective-permute-done.8 = f32[2,64,128]{2,1,0:T(8,128)S(1)} collective-permute-done((f32[2,64,128]{2,1,0:T(8,128)S(1)}, f32[2,64,128]{2,1,0:T(8,128)S(1)}, u32[]{:S(2)}, u32[]{:S(2)}) %collective-permute-start.8) | collective-permute-done | bytes 65568 | tf_op jit(solution)/shard_map/ppermute | solution.py:433
  36.0 1.7 %collective-permute-done.11 = f32[688,128]{1,0:T(8,128)S(1)} collective-permute-done((f32[688,128]{1,0:T(8,128)S(1)}, f32[688,128]{1,0:T(8,128)S(1)}, u32[]{:S(2)}, u32[]{:S(2)}) %collective-permute-start.11) | collective-permute-done | bytes 352288 | tf_op jit(solution)/shard_map/ppermute | solution.py:433
  37.7 2.9 %collective-permute-start.12 = (f32[688,128]{1,0:T(8,128)S(1)}, f32[688,128]{1,0:T(8,128)S(1)}, u32[]{:S(2)}, u32[]{:S(2)}) collective-permute-start(f32[688,128]{1,0:T(8,128)S(1)} %add.9), channel_id=1, source_target_pairs={{0,8},{4,12},{8,0},{12,4},{16,24},{20,28},{24,16},{28,20},{1,9},{5... | collective-permute-start | bytes 1056776 | tf_op jit(solution)/shard_map/ppermute | solution.py:433
  40.7 3.3 %collective-permute-start.7 = (f32[64,512]{1,0:T(8,128)S(1)}, f32[64,512]{1,0:T(8,128)S(1)}, u32[]{:S(2)}, u32[]{:S(2)}) collective-permute-start(f32[64,512]{1,0:T(8,128)S(1)} %get-tuple-element.37), channel_id=1, source_target_pairs={{0,3},{1,2},{2,1},{3,0},{4,7},{5,6},{6,5},{7,4},{8,11},{9,10},{10,... | collective-permute-start | bytes 393224 | tf_op jit(solution)/shard_map/ppermute | solution.py:433
  43.9 1.2 %collective-permute-start.5 = (f32[64,512]{1,0:T(8,128)S(1)}, f32[64,512]{1,0:T(8,128)S(1)}, u32[]{:S(2)}, u32[]{:S(2)}) collective-permute-start(f32[64,512]{1,0:T(8,128)S(1)} %get-tuple-element.39), channel_id=1, source_target_pairs={{0,1},{1,0},{2,3},{3,2},{4,5},{5,4},{6,7},{7,6},{8,9},{9,8},{10,11... | collective-permute-start | bytes 393224 | tf_op jit(solution)/shard_map/ppermute | solution.py:433
  45.1 4.0 %collective-permute-done.12 = f32[688,128]{1,0:T(8,128)S(1)} collective-permute-done((f32[688,128]{1,0:T(8,128)S(1)}, f32[688,128]{1,0:T(8,128)S(1)}, u32[]{:S(2)}, u32[]{:S(2)}) %collective-permute-start.12) | collective-permute-done | bytes 352288 | tf_op jit(solution)/shard_map/ppermute | solution.py:433
  49.2 2.2 %collective-permute-start.13 = (f32[688,128]{1,0:T(8,128)S(1)}, f32[688,128]{1,0:T(8,128)S(1)}, u32[]{:S(2)}, u32[]{:S(2)}) collective-permute-start(f32[688,128]{1,0:T(8,128)S(1)} %add.10), channel_id=1, source_target_pairs={{0,16},{4,20},{8,24},{12,28},{16,0},{20,4},{24,8},{28,12},{1,17},{... | collective-permute-start | bytes 1056776 | tf_op jit(solution)/shard_map/ppermute | solution.py:433
  51.4 3.3 %collective-permute-done.6.refs_2_ = f32[64,512]{1,0:T(8,128)S(1)} collective-permute-done((f32[64,512]{1,0:T(8,128)S(1)}, f32[64,512]{1,0:T(8,128)S(1)}, u32[]{:S(2)}, u32[]{:S(2)}) %collective-permute-start.6) | collective-permute-done | bytes 131104 | tf_op jit(solution)/shard_map/ppermute | solution.py:433
  54.7 0.8 %shard_map.98 = bf16[8,64,128]{2,1,0:T(8,128)(2,1)} custom-call(s32[8,128]{1,0:T(8,128)S(1)} %get-tuple-element.21.slot_ref, f32[64,512]{1,0:T(8,128)S(1)} %get-tuple-element.40.refs_0_, f32[64,512]{1,0:T(8,128)S(1)} %collective-permute-done.5.refs_1_, f32[64,512]{1,0:T(8,128)S(1)} %collective-permute-done.6.refs_2_, ...), custom_call_target="tpu_custom_call" | custom-call | flops 1724999936 | tf_op jit(solution)/shard_map/pallas_call | solution.py:553
  55.6 3.4 %all-to-all-start.1 = ((bf16[8,64,128]{2,1,0:T(8,128)(2,1)}), bf16[8,64,128]{2,1,0:T(8,128)(2,1)S(1)}, u32[]{:S(2)}, u32[]{:S(2)}) async-start(bf16[8,64,128]{2,1,0:T(8,128)(2,1)} %shard_map.98), calls=%async_computation.1 | async-start | bytes 262144 | tf_op jit(solution)/shard_map/all_to_all | solution.py:561
  59.5 4.9 %all-to-all-done.1 = bf16[8,64,128]{2,1,0:T(8,128)(2,1)S(1)} async-done(((bf16[8,64,128]{2,1,0:T(8,128)(2,1)}), bf16[8,64,128]{2,1,0:T(8,128)(2,1)S(1)}, u32[]{:S(2)}, u32[]{:S(2)}) %all-to-all-start.1) | async-done | bytes 131104 | tf_op jit(solution)/shard_map/all_to_all | solution.py:561
  64.5 0.8 %pad_maximum_fusion = bf16[8,128,64]{2,1,0:T(8,128)(2,1)} fusion(bf16[8,64,64]{2,1,0:T(8,128)(2,1)S(1)} %get-tuple-element.47, bf16[8,64,64]{2,1,0:T(8,128)(2,1)S(1)} %get-tuple-element.46), kind=kLoop, calls=%fused_computation | loop fusion | flops 262144 | bytes 262144 | tf_op jit(solution)/shard_map/concatenate
  65.3 1.2 %shard_map.100 = (f32[864,128]{1,0:T(8,128)}, f32[8,64,128]{2,1,0:T(8,128)}) custom-call(f32[688,128]{1,0:T(8,128)S(1)} %add.11.own_ref, f32[688,128]{1,0:T(8,128)S(1)} %collective-permute-done.14.other_ref), custom_call_target="tpu_custom_call" | custom-call | flops 1724999936 | tf_op jit(solution)/shard_map/pallas_call | solution.py:572
  (41 shorter events, 1.9 us)
Async XLA Ops:
  0.6 17.5 %copy-start.3 = (s32[8,512]{1,0:T(8,128)S(1)}, s32[8,512]{1,0:T(8,128)}, u32[]{:S(2)}) copy-start(s32[8,512]{1,0:T(8,128)} %mask_ref.3) | copy-start | bytes 49156
  0.6 17.5 %copy-start = (bf16[8,128,512]{2,1,0:T(8,128)(2,1)S(1)}, bf16[8,128,512]{2,1,0:T(8,128)(2,1)}, u32[]{:S(2)}) copy-start(bf16[8,128,512]{2,1,0:T(8,128)(2,1)} %feat_hbm.1) | copy-start | bytes 3145732
  0.7 12.7 %copy-start.5 = (s32[8,1]{0,1:T(1,128)S(1)}, s32[8,1]{0,1:T(1,128)}, u32[]{:S(2)}) copy-start(s32[8,1]{0,1:T(1,128)} %param.12) | copy-start | bytes 100
  0.7 17.5 %copy-start.2 = (bf16[27,32,128]{2,1,0:T(8,128)(2,1)S(1)}, bf16[27,32,128]{2,1,0:T(8,128)(2,1)}, u32[]{:S(2)}) copy-start(bf16[27,32,128]{2,1,0:T(8,128)(2,1)} %wconv_hbm.1) | copy-start | bytes 663556
  0.7 17.5 %copy-start.4 = (s32[8,26]{1,0:T(8,128)S(1)}, s32[8,26]{1,0:T(8,128)}, u32[]{:S(2)}) copy-start(s32[8,26]{1,0:T(8,128)} %nbr_hbm.1) | copy-start | bytes 2500
  2.7 10.7 %all-to-all-start = ((bf16[8,64,128]{2,1,0:T(8,128)(2,1)}), bf16[8,64,128]{2,1,0:T(8,128)(2,1)S(1)}, u32[]{:S(2)}, u32[]{:S(2)}) async-start(bf16[8,64,128]{2,1,0:T(8,128)(2,1)} %get-tuple-element.20), calls=%async_computation | async-start | bytes 262144 | tf_op jit(solution)/shard_map/all_to_all | solution.py:473
  7.8 10.3 %collective-permute-start = (bf16[2,128,128]{2,1,0:T(8,128)(2,1)}, bf16[2,128,128]{2,1,0:T(8,128)(2,1)S(1)}, u32[]{:S(2)}, u32[]{:S(2)}) collective-permute-start(bf16[2,128,128]{2,1,0:T(8,128)(2,1)} %get-tuple-element.22), channel_id=1, source_target_pairs={{0,4},{4,8},{8,12},{12,16},{16,20},{20,24},{24,28},{1,5},{5,9},{9,... | collective-permute-start | bytes 196616 | tf_op jit(solution)/shard_map/ppermute | solution.py:471
  10.3 7.9 %collective-permute-start.1 = (bf16[2,128,128]{2,1,0:T(8,128)(2,1)}, bf16[2,128,128]{2,1,0:T(8,128)(2,1)S(1)}, u32[]{:S(2)}, u32[]{:S(2)}) collective-permute-start(bf16[2,128,128]{2,1,0:T(8,128)(2,1)} %get-tuple-element.23), channel_id=1, source_target_pairs={{4,0},{8,4},{12,8},{16,12},{20,16},{24,20},{28,24},{5,1},{9,5},{13... | collective-permute-start | bytes 196616 | tf_op jit(solution)/shard_map/ppermute | solution.py:472
  13.7 12.2 %copy-start.1 = (bf16[8,256,128]{2,1,0:T(8,128)(2,1)S(1)}, bf16[8,256,128]{2,1,0:T(8,128)(2,1)}, u32[]{:S(2)}) copy-start(bf16[8,256,128]{2,1,0:T(8,128)(2,1)} %wdown_ref.3) | copy-start | bytes 1572868
  13.7 12.2 %collective-permute-start.4 = (bf16[64,512]{1,0:T(8,128)(2,1)S(1)}, bf16[64,512]{1,0:T(8,128)(2,1)S(1)}, u32[]{:S(2)}, u32[]{:S(2)}) collective-permute-start(bf16[64,512]{1,0:T(8,128)(2,1)S(1)} %get-tuple-element.25.refs_0_), channel_id=1, source_target_pairs={{0,3},{1,2},{2,1},{3,0},{4,7},{5,6},{6,5},{7,4},{8,11},{9,10},{10,... | collective-permute-start | bytes 196616 | tf_op jit(solution)/shard_map/ppermute | solution.py:433
  17.4 8.5 %collective-permute-start.3 = (bf16[64,512]{1,0:T(8,128)(2,1)S(1)}, bf16[64,512]{1,0:T(8,128)(2,1)S(1)}, u32[]{:S(2)}, u32[]{:S(2)}) collective-permute-start(bf16[64,512]{1,0:T(8,128)(2,1)S(1)} %get-tuple-element.25.refs_0_), channel_id=1, source_target_pairs={{0,2},{1,3},{2,0},{3,1},{4,6},{5,7},{6,4},{7,5},{8,10},{9,11},{10,... | collective-permute-start | bytes 196616 | tf_op jit(solution)/shard_map/ppermute | solution.py:433
  17.4 8.6 %collective-permute-start.2 = (bf16[64,512]{1,0:T(8,128)(2,1)S(1)}, bf16[64,512]{1,0:T(8,128)(2,1)S(1)}, u32[]{:S(2)}, u32[]{:S(2)}) collective-permute-start(bf16[64,512]{1,0:T(8,128)(2,1)S(1)} %get-tuple-element.25.refs_0_), channel_id=1, source_target_pairs={{0,1},{1,0},{2,3},{3,2},{4,5},{5,4},{6,7},{7,6},{8,9},{9,8},{10,11... | collective-permute-start | bytes 196616 | tf_op jit(solution)/shard_map/ppermute | solution.py:433
  26.6 9.3 %collective-permute-start.10 = (f32[2,64,128]{2,1,0:T(8,128)S(1)}, f32[2,64,128]{2,1,0:T(8,128)S(1)}, u32[]{:S(2)}, u32[]{:S(2)}) collective-permute-start(f32[2,64,128]{2,1,0:T(8,128)S(1)} %get-tuple-element.43), channel_id=1, source_target_pairs={{0,3},{1,2},{2,1},{3,0},{4,7},{5,6},{6,5},{7,4},{8,11},{9,10},{10,... | collective-permute-start | bytes 196616 | tf_op jit(solution)/shard_map/ppermute | solution.py:433
  30.3 5.6 %collective-permute-start.9 = (f32[2,64,128]{2,1,0:T(8,128)S(1)}, f32[2,64,128]{2,1,0:T(8,128)S(1)}, u32[]{:S(2)}, u32[]{:S(2)}) collective-permute-start(f32[2,64,128]{2,1,0:T(8,128)S(1)} %get-tuple-element.44), channel_id=1, source_target_pairs={{0,2},{1,3},{2,0},{3,1},{4,6},{5,7},{6,4},{7,5},{8,10},{9,11},{10,... | collective-permute-start | bytes 196616 | tf_op jit(solution)/shard_map/ppermute | solution.py:433
  30.3 5.6 %collective-permute-start.8 = (f32[2,64,128]{2,1,0:T(8,128)S(1)}, f32[2,64,128]{2,1,0:T(8,128)S(1)}, u32[]{:S(2)}, u32[]{:S(2)}) collective-permute-start(f32[2,64,128]{2,1,0:T(8,128)S(1)} %get-tuple-element.45), channel_id=1, source_target_pairs={{0,1},{1,0},{2,3},{3,2},{4,5},{5,4},{6,7},{7,6},{8,9},{9,8},{10,11... | collective-permute-start | bytes 196616 | tf_op jit(solution)/shard_map/ppermute | solution.py:433
  35.9 1.7 %collective-permute-start.11 = (f32[688,128]{1,0:T(8,128)S(1)}, f32[688,128]{1,0:T(8,128)S(1)}, u32[]{:S(2)}, u32[]{:S(2)}) collective-permute-start(f32[688,128]{1,0:T(8,128)S(1)} %get-tuple-element.48), channel_id=1, source_target_pairs={{0,4},{4,0},{8,12},{12,8},{16,20},{20,16},{24,28},{28,24},{1,5},{5... | collective-permute-start | bytes 1056776 | tf_op jit(solution)/shard_map/ppermute | solution.py:433
  37.7 11.4 %collective-permute-start.12 = (f32[688,128]{1,0:T(8,128)S(1)}, f32[688,128]{1,0:T(8,128)S(1)}, u32[]{:S(2)}, u32[]{:S(2)}) collective-permute-start(f32[688,128]{1,0:T(8,128)S(1)} %add.9), channel_id=1, source_target_pairs={{0,8},{4,12},{8,0},{12,4},{16,24},{20,28},{24,16},{28,20},{1,9},{5... | collective-permute-start | bytes 1056776 | tf_op jit(solution)/shard_map/ppermute | solution.py:433
  40.7 10.8 %collective-permute-start.7 = (f32[64,512]{1,0:T(8,128)S(1)}, f32[64,512]{1,0:T(8,128)S(1)}, u32[]{:S(2)}, u32[]{:S(2)}) collective-permute-start(f32[64,512]{1,0:T(8,128)S(1)} %get-tuple-element.37), channel_id=1, source_target_pairs={{0,3},{1,2},{2,1},{3,0},{4,7},{5,6},{6,5},{7,4},{8,11},{9,10},{10,... | collective-permute-start | bytes 393224 | tf_op jit(solution)/shard_map/ppermute | solution.py:433
  43.9 10.8 %collective-permute-start.6 = (f32[64,512]{1,0:T(8,128)S(1)}, f32[64,512]{1,0:T(8,128)S(1)}, u32[]{:S(2)}, u32[]{:S(2)}) collective-permute-start(f32[64,512]{1,0:T(8,128)S(1)} %get-tuple-element.38), channel_id=1, source_target_pairs={{0,2},{1,3},{2,0},{3,1},{4,6},{5,7},{6,4},{7,5},{8,10},{9,11},{10,... | collective-permute-start | bytes 393224 | tf_op jit(solution)/shard_map/ppermute | solution.py:433
  43.9 10.8 %collective-permute-start.5 = (f32[64,512]{1,0:T(8,128)S(1)}, f32[64,512]{1,0:T(8,128)S(1)}, u32[]{:S(2)}, u32[]{:S(2)}) collective-permute-start(f32[64,512]{1,0:T(8,128)S(1)} %get-tuple-element.39), channel_id=1, source_target_pairs={{0,1},{1,0},{2,3},{3,2},{4,5},{5,4},{6,7},{7,6},{8,9},{9,8},{10,11... | collective-permute-start | bytes 393224 | tf_op jit(solution)/shard_map/ppermute | solution.py:433
  49.2 9.9 %collective-permute-start.13 = (f32[688,128]{1,0:T(8,128)S(1)}, f32[688,128]{1,0:T(8,128)S(1)}, u32[]{:S(2)}, u32[]{:S(2)}) collective-permute-start(f32[688,128]{1,0:T(8,128)S(1)} %add.10), channel_id=1, source_target_pairs={{0,16},{4,20},{8,24},{12,28},{16,0},{20,4},{24,8},{28,12},{1,17},{... | collective-permute-start | bytes 1056776 | tf_op jit(solution)/shard_map/ppermute | solution.py:433
  55.6 8.8 %all-to-all-start.1 = ((bf16[8,64,128]{2,1,0:T(8,128)(2,1)}), bf16[8,64,128]{2,1,0:T(8,128)(2,1)S(1)}, u32[]{:S(2)}, u32[]{:S(2)}) async-start(bf16[8,64,128]{2,1,0:T(8,128)(2,1)} %shard_map.98), calls=%async_computation.1 | async-start | bytes 262144 | tf_op jit(solution)/shard_map/all_to_all | solution.py:561
  59.2 6.1 %collective-permute-start.14 = (f32[688,128]{1,0:T(8,128)S(1)}, f32[688,128]{1,0:T(8,128)S(1)}, u32[]{:S(2)}, u32[]{:S(2)}) collective-permute-start(f32[688,128]{1,0:T(8,128)S(1)} %add.11.own_ref), channel_id=1, source_target_pairs={{0,4},{4,0},{8,12},{12,8},{16,20},{20,16},{24,28},{28,24},{1,5},{5... | collective-permute-start | bytes 1056776 | tf_op jit(solution)/shard_map/ppermute | solution.py:433

commit v6 on v5

--- a/solution.py
+++ b/solution.py
@@ -159,10 +159,8 @@
     weights,
     own_s,
     hidden_s,
-    same_from,
-    same_code,
-    side_from,
-    side_code,
+    same_list,
+    side_list,
     nbr_ref,
     feat_ref,
     mask_ref,
@@ -211,12 +209,10 @@
             there = (source >= 0).astype(jnp.int32)
             step, table = position // 9, position % 9
             if step == 1:
-                same_from[same] = source
-                same_code[same] = block * 16 + table
+                same_list[same] = source * 256 + (block * 16 + table)
                 same = same + there
             else:
-                side_from[side] = source
-                side_code[side] = (block * 10 + (9 if step else 0)) * 32 + table * 2 + step // 2
+                side_list[side] = source * 4096 + ((block * 10 + (9 if step else 0)) * 32 + table * 2 + step // 2)
                 side = side + there
 
     loads[1].wait()
@@ -238,14 +234,14 @@
         two_planes(halo + 2 * pair, prev_ref[pair].astype(F32))
         two_planes(halo + edge + 2 * pair, next_ref[pair].astype(F32))
 
-    same_from[same] = 0
-    same_code[same] = 9
+    same_list[same] = 9
 
     def same_layer(item, carry):
         results = []
         for extra in range(2):
-            code = same_code[2 * item + extra]
-            cells = planes[pl.ds(same_from[2 * item + extra] * 10 + 1, 8)].reshape(8 * channels, LANES)
+            entry = same_list[2 * item + extra]
+            source, code = entry >> 8, entry & 255
+            cells = planes[pl.ds(source * 10 + 1, 8)].reshape(8 * channels, LANES)
             moved = jnp.dot(cells, edge_ref[code & 15], preferred_element_type=F32).astype(BF16)
             results.append((lax.shift_right_logical(code, 4), moved.reshape(8, channels, LANES)))
         for block, moved in results:
@@ -254,13 +250,13 @@
 
     lax.fori_loop(0, lax.shift_right_logical(same + 1, 1), same_layer, 0)
     for extra in range(3):
-        side_from[side + extra] = dummy - halo + blocks
-        side_code[side + extra] = dummy * 32 + 18
+        side_list[side + extra] = (dummy - halo + blocks) * 4096 + dummy * 32 + 18
 
     def side_layer(item, carry):
         results = []
         for extra in range(4):
-            source, code = side_from[4 * item + extra], side_code[4 * item + extra]
+            entry = side_list[4 * item + extra]
+            source, code = entry >> 12, entry & 4095
             own = source * 10 + jnp.where(code & 1 == 1, 1, 8)
             cells = planes[jnp.where(source < blocks, own, halo + source - blocks)]
             table = edge_ref[lax.shift_right_logical(code, 1) & 15]
@@ -391,11 +387,11 @@
         pre = pre_ref[rows, :]
         gate = 1.0 / (1.0 + jnp.exp(-pre))
         dpre = dhidden[rows] * keeps[block : block + 1] * gate * (1.0 + pre * (1.0 - gate))
-        dpre = jnp.concatenate([dpre, blank], axis=1)
+        dpre = jnp.concatenate([dpre, blank], axis=1).astype(BF16)
         lanes = slice(block * STRIDE, (block + 1) * STRIDE)
         for k in range(9):
             moved = pltpu.roll(dpre, (k // 3) * PLANE + (k % 3) * 8, 1) if k else dpre
-            d9[k * width : (k + 1) * width, lanes] = moved.astype(BF16)
+            d9[k * width : (k + 1) * width, lanes] = moved
 
     part = jnp.dot(d9[...], patches_ref[...], preferred_element_type=F32)
     for k in range(27):
@@ -502,8 +498,6 @@
             pltpu.VMEM((blocks * width, 512), BF16),
             pltpu.VMEM((blocks * width, SPAN), BF16),
             pltpu.SMEM((8 * blocks + 8,), jnp.int32),
-            pltpu.SMEM((8 * blocks + 8,), jnp.int32),
-            pltpu.SMEM((18 * blocks + 8,), jnp.int32),
             pltpu.SMEM((18 * blocks + 8,), jnp.int32),
             pltpu.SMEM(neighbors.shape, jnp.int32),
             pltpu.VMEM(features.shape, BF16),

time: 66.9 us -> 66.4 us (level)
  starting transfers between devices: 31.1 us -> 28.8 us
  waiting for transfers between devices: 16.8 us -> 17.8 us
  Pallas kernels: 16.6 us -> 17.4 us
    ppermute x13, starting transfers between devices: 18.8 us -> 16.6 us  [exchange(): return lax.ppermute(values, axis, [(i, i ^ step) for i in range(count)])]
    ppermute x13, waiting for transfers between devices: 10.1 us -> 11.1 us  [exchange(): return lax.ppermute(values, axis, [(i, i ^ step) for i in range(count)])]
    pallas_call x1, Pallas kernels: 7.69 us -> 8.63 us  [local(): pl.pallas_call(functools.partial(forward_kernel, 'chan'), out_shape=[jax....]
  transfers between devices with their start and end apart: 17 -> 17, of which waited for: 7 -> 7; matrix products, arithmetic and copies ran while one was open for 2% -> 2% of each run, Pallas kernels for 19% -> 21%
where the time goes in v6:
time: 66.4 us; the launch traced here: 66 us
  starting transfers between devices  28.8 us (43%)
  waiting for transfers between devices  17.8 us (27%)
  Pallas kernels  17.4 us (26%)
  other arithmetic  0.9 us (1%)
  between operations  0.86 us (1%)
    ppermute x13, starting transfers between devices, exchange(): return lax.ppermute(values, axis, [(i, i ^ step) for i in range(count)])  16.6 us
    ppermute x13, waiting for transfers between devices, exchange(): return lax.ppermute(values, axis, [(i, i ^ step) for i in range(count)])  11.1 us
    pallas_call x1, Pallas kernels, local(): pl.pallas_call(functools.partial(forward_kernel, 'chan'), out_shape=[jax....  8.63 us
    all_to_all x1, starting transfers between devices, local(): lax.all_to_all(packed, 'space', split_axis=0, concat_axis=0, tiled=True)  5.17 us
    all_to_all x1, waiting for transfers between devices, local(): lax.all_to_all(outgoing, 'space', split_axis=0, concat_axis=0, tiled=True)  4.92 us
    pallas_call x1, Pallas kernels, local(): pl.pallas_call(functools.partial(backward_kernel, axes), out_shape=[jax.S...  3.75 us
    all_to_all x1, starting transfers between devices, local(): lax.all_to_all(outgoing, 'space', split_axis=0, concat_axis=0, tiled=True)  3.37 us
    ppermute x1, starting transfers between devices, local(): before = lax.ppermute(tail, 'space', [(i, i + 1) for i in range(ends)])  2.4 us
  transfers between devices with their start and end apart: 17, of which 7 were waited for; matrix products, arithmetic and copies ran while one was open for 2% of the time, Pallas kernels for 21%

profile of v6, /device:TPU:0, one launch (start us, length us, event | category | flops | bytes accessed | tf_op | source)
XLA Modules:
  0.0 66.0 jit_solution(13949229999857805837)
XLA Ops:
  0.7 2.0 %shard_map.94 = (bf16[2,128,128]{2,1,0:T(8,128)(2,1)}, bf16[2,128,128]{2,1,0:T(8,128)(2,1)}, bf16[8,64,128]{2,1,0:T(8,128)(2,1)}) custom-call(bf16[8,128,512]{2,1,0:T(8,128)(2,1)} %feat_hbm.1, bf16[8,128,512]{2,1,0:T(8,128)(2,1)} %feat_hbm.1, s32[8,512]{1,0:T(8,128)} %mask_ref.3, bf16[16,64,64]{2,1,0:T(8,128)(2,1)} %cot_ref.1), custom_call_target="tpu_custom_call" | custom-call | flops 2300000000 | tf_op jit(solution)/shard_map/pallas_call | solution.py:444
  2.7 5.2 %all-to-all-start = ((bf16[8,64,128]{2,1,0:T(8,128)(2,1)}), bf16[8,64,128]{2,1,0:T(8,128)(2,1)S(1)}, u32[]{:S(2)}, u32[]{:S(2)}) async-start(bf16[8,64,128]{2,1,0:T(8,128)(2,1)} %get-tuple-element.20), calls=%async_computation | async-start | bytes 262144 | tf_op jit(solution)/shard_map/all_to_all | solution.py:469
  7.8 2.4 %collective-permute-start = (bf16[2,128,128]{2,1,0:T(8,128)(2,1)}, bf16[2,128,128]{2,1,0:T(8,128)(2,1)S(1)}, u32[]{:S(2)}, u32[]{:S(2)}) collective-permute-start(bf16[2,128,128]{2,1,0:T(8,128)(2,1)} %get-tuple-element.22), channel_id=1, source_target_pairs={{0,4},{4,8},{8,12},{12,16},{16,20},{20,24},{24,28},{1,5},{5,9},{9,... | collective-permute-start | bytes 196616 | tf_op jit(solution)/shard_map/ppermute | solution.py:467
  10.3 1.3 %collective-permute-start.1 = (bf16[2,128,128]{2,1,0:T(8,128)(2,1)}, bf16[2,128,128]{2,1,0:T(8,128)(2,1)S(1)}, u32[]{:S(2)}, u32[]{:S(2)}) collective-permute-start(bf16[2,128,128]{2,1,0:T(8,128)(2,1)} %get-tuple-element.23), channel_id=1, source_target_pairs={{4,0},{8,4},{12,8},{16,12},{20,16},{24,20},{28,24},{5,1},{9,5},{13... | collective-permute-start | bytes 196616 | tf_op jit(solution)/shard_map/ppermute | solution.py:468
  11.6 1.8 %all-to-all-done.returned_ref = bf16[8,64,128]{2,1,0:T(8,128)(2,1)S(1)} async-done(((bf16[8,64,128]{2,1,0:T(8,128)(2,1)}), bf16[8,64,128]{2,1,0:T(8,128)(2,1)S(1)}, u32[]{:S(2)}, u32[]{:S(2)}) %all-to-all-start) | async-done | bytes 131104 | tf_op jit(solution)/shard_map/all_to_all | solution.py:469
  13.7 3.7 %collective-permute-start.4 = (bf16[64,512]{1,0:T(8,128)(2,1)S(1)}, bf16[64,512]{1,0:T(8,128)(2,1)S(1)}, u32[]{:S(2)}, u32[]{:S(2)}) collective-permute-start(bf16[64,512]{1,0:T(8,128)(2,1)S(1)} %get-tuple-element.25.refs_0_), channel_id=1, source_target_pairs={{0,3},{1,2},{2,1},{3,0},{4,7},{5,6},{6,5},{7,4},{8,11},{9,10},{10,... | collective-permute-start | bytes 196616 | tf_op jit(solution)/shard_map/ppermute | solution.py:429
  17.4 0.8 %collective-permute-start.2 = (bf16[64,512]{1,0:T(8,128)(2,1)S(1)}, bf16[64,512]{1,0:T(8,128)(2,1)S(1)}, u32[]{:S(2)}, u32[]{:S(2)}) collective-permute-start(bf16[64,512]{1,0:T(8,128)(2,1)S(1)} %get-tuple-element.25.refs_0_), channel_id=1, source_target_pairs={{0,1},{1,0},{2,3},{3,2},{4,5},{5,4},{6,7},{7,6},{8,9},{9,8},{10,11... | collective-permute-start | bytes 196616 | tf_op jit(solution)/shard_map/ppermute | solution.py:429
  18.2 8.6 %shard_map.96 = (f32[256,640]{1,0:T(8,128)S(1)}, bf16[256,512]{1,0:T(8,128)(2,1)S(1)}, bf16[7168,384]{1,0:T(8,128)(2,1)S(1)}, bf16[512,640]{1,0:T(8,128)(2,1)S(1)}, bf16[640,512]{1,0:T(8,128)(2,1)S(1)}) custom-call(bf16[2,128,128]{2,1,0:T(8,128)(2,1)S(1)} %collective-permute-done.prev_ref, bf16[2,128,128]{2,1,0:T(8,128)(2,1)S(1)} %collective-permute-done.1.next_ref, ...), custom_call_target="tpu_custom_call" | custom-call | flops 9200000000 | tf_op jit(solution)/shard_map/pallas_call | solution.py:484
  27.6 3.7 %collective-permute-start.10 = (f32[2,64,128]{2,1,0:T(8,128)S(1)}, f32[2,64,128]{2,1,0:T(8,128)S(1)}, u32[]{:S(2)}, u32[]{:S(2)}) collective-permute-start(f32[2,64,128]{2,1,0:T(8,128)S(1)} %get-tuple-element.43), channel_id=1, source_target_pairs={{0,3},{1,2},{2,1},{3,0},{4,7},{5,6},{6,5},{7,4},{8,11},{9,10},{10,... | collective-permute-start | bytes 196616 | tf_op jit(solution)/shard_map/ppermute | solution.py:429
  31.3 0.8 %collective-permute-start.8 = (f32[2,64,128]{2,1,0:T(8,128)S(1)}, f32[2,64,128]{2,1,0:T(8,128)S(1)}, u32[]{:S(2)}, u32[]{:S(2)}) collective-permute-start(f32[2,64,128]{2,1,0:T(8,128)S(1)} %get-tuple-element.45), channel_id=1, source_target_pairs={{0,1},{1,0},{2,3},{3,2},{4,5},{5,4},{6,7},{7,6},{8,9},{9,8},{10,11... | collective-permute-start | bytes 196616 | tf_op jit(solution)/shard_map/ppermute | solution.py:429
  32.0 3.8 %shard_map.99 = (f32[432,128]{1,0:T(8,128)S(1)}, f32[432,128]{1,0:T(8,128)S(1)}) custom-call(bf16[256,512]{1,0:T(8,128)(2,1)S(1)} %get-tuple-element.27.dp_ref, bf16[8,256,128]{2,1,0:T(8,128)(2,1)S(1)} %copy-done.1, s32[8,512]{1,0:T(8,128)S(1)} %copy-done.3, f32[256,640]{1,0:T(8,128)S(1)} %get-tuple-element.28.pre_ref, ...), custom_call_target="tpu_custom_call" | custom-call | flops 6899999744 | tf_op jit(solution)/shard_map/pallas_call | solution.py:531
  35.9 1.3 %collective-permute-done.9 = f32[2,64,128]{2,1,0:T(8,128)S(1)} collective-permute-done((f32[2,64,128]{2,1,0:T(8,128)S(1)}, f32[2,64,128]{2,1,0:T(8,128)S(1)}, u32[]{:S(2)}, u32[]{:S(2)}) %collective-permute-start.9) | collective-permute-done | bytes 65568 | tf_op jit(solution)/shard_map/ppermute | solution.py:429
  37.3 1.7 %collective-permute-done.11 = f32[688,128]{1,0:T(8,128)S(1)} collective-permute-done((f32[688,128]{1,0:T(8,128)S(1)}, f32[688,128]{1,0:T(8,128)S(1)}, u32[]{:S(2)}, u32[]{:S(2)}) %collective-permute-start.11) | collective-permute-done | bytes 352288 | tf_op jit(solution)/shard_map/ppermute | solution.py:429
  39.0 1.2 %collective-permute-start.12 = (f32[688,128]{1,0:T(8,128)S(1)}, f32[688,128]{1,0:T(8,128)S(1)}, u32[]{:S(2)}, u32[]{:S(2)}) collective-permute-start(f32[688,128]{1,0:T(8,128)S(1)} %add.9), channel_id=1, source_target_pairs={{0,8},{4,12},{8,0},{12,4},{16,24},{20,28},{24,16},{28,20},{1,9},{5... | collective-permute-start | bytes 1056776 | tf_op jit(solution)/shard_map/ppermute | solution.py:429
  40.2 3.1 %collective-permute-start.7 = (f32[64,512]{1,0:T(8,128)S(1)}, f32[64,512]{1,0:T(8,128)S(1)}, u32[]{:S(2)}, u32[]{:S(2)}) collective-permute-start(f32[64,512]{1,0:T(8,128)S(1)} %get-tuple-element.37), channel_id=1, source_target_pairs={{0,3},{1,2},{2,1},{3,0},{4,7},{5,6},{6,5},{7,4},{8,11},{9,10},{10,... | collective-permute-start | bytes 393224 | tf_op jit(solution)/shard_map/ppermute | solution.py:429
  43.4 1.3 %collective-permute-start.5 = (f32[64,512]{1,0:T(8,128)S(1)}, f32[64,512]{1,0:T(8,128)S(1)}, u32[]{:S(2)}, u32[]{:S(2)}) collective-permute-start(f32[64,512]{1,0:T(8,128)S(1)} %get-tuple-element.39), channel_id=1, source_target_pairs={{0,1},{1,0},{2,3},{3,2},{4,5},{5,4},{6,7},{7,6},{8,9},{9,8},{10,11... | collective-permute-start | bytes 393224 | tf_op jit(solution)/shard_map/ppermute | solution.py:429
  44.7 4.6 %collective-permute-done.12 = f32[688,128]{1,0:T(8,128)S(1)} collective-permute-done((f32[688,128]{1,0:T(8,128)S(1)}, f32[688,128]{1,0:T(8,128)S(1)}, u32[]{:S(2)}, u32[]{:S(2)}) %collective-permute-start.12) | collective-permute-done | bytes 352288 | tf_op jit(solution)/shard_map/ppermute | solution.py:429
  49.3 1.8 %collective-permute-start.13 = (f32[688,128]{1,0:T(8,128)S(1)}, f32[688,128]{1,0:T(8,128)S(1)}, u32[]{:S(2)}, u32[]{:S(2)}) collective-permute-start(f32[688,128]{1,0:T(8,128)S(1)} %add.10), channel_id=1, source_target_pairs={{0,16},{4,20},{8,24},{12,28},{16,0},{20,4},{24,8},{28,12},{1,17},{... | collective-permute-start | bytes 1056776 | tf_op jit(solution)/shard_map/ppermute | solution.py:429
  51.1 3.1 %collective-permute-done.6.refs_2_ = f32[64,512]{1,0:T(8,128)S(1)} collective-permute-done((f32[64,512]{1,0:T(8,128)S(1)}, f32[64,512]{1,0:T(8,128)S(1)}, u32[]{:S(2)}, u32[]{:S(2)}) %collective-permute-start.6) | collective-permute-done | bytes 131104 | tf_op jit(solution)/shard_map/ppermute | solution.py:429
  54.3 0.8 %shard_map.98 = bf16[8,64,128]{2,1,0:T(8,128)(2,1)} custom-call(s32[8,128]{1,0:T(8,128)S(1)} %get-tuple-element.21.slot_ref, f32[64,512]{1,0:T(8,128)S(1)} %get-tuple-element.40.refs_0_, f32[64,512]{1,0:T(8,128)S(1)} %collective-permute-done.5.refs_1_, f32[64,512]{1,0:T(8,128)S(1)} %collective-permute-done.6.refs_2_, ...), custom_call_target="tpu_custom_call" | custom-call | flops 1724999936 | tf_op jit(solution)/shard_map/pallas_call | solution.py:547
  55.1 3.4 %all-to-all-start.1 = ((bf16[8,64,128]{2,1,0:T(8,128)(2,1)}), bf16[8,64,128]{2,1,0:T(8,128)(2,1)S(1)}, u32[]{:S(2)}, u32[]{:S(2)}) async-start(bf16[8,64,128]{2,1,0:T(8,128)(2,1)} %shard_map.98), calls=%async_computation.1 | async-start | bytes 262144 | tf_op jit(solution)/shard_map/all_to_all | solution.py:555
  59.0 4.9 %all-to-all-done.1 = bf16[8,64,128]{2,1,0:T(8,128)(2,1)S(1)} async-done(((bf16[8,64,128]{2,1,0:T(8,128)(2,1)}), bf16[8,64,128]{2,1,0:T(8,128)(2,1)S(1)}, u32[]{:S(2)}, u32[]{:S(2)}) %all-to-all-start.1) | async-done | bytes 131104 | tf_op jit(solution)/shard_map/all_to_all | solution.py:555
  64.1 0.8 %pad_maximum_fusion = bf16[8,128,64]{2,1,0:T(8,128)(2,1)} fusion(bf16[8,64,64]{2,1,0:T(8,128)(2,1)S(1)} %get-tuple-element.47, bf16[8,64,64]{2,1,0:T(8,128)(2,1)S(1)} %get-tuple-element.46), kind=kLoop, calls=%fused_computation | loop fusion | flops 262144 | bytes 262144 | tf_op jit(solution)/shard_map/concatenate
  64.8 1.2 %shard_map.100 = (f32[864,128]{1,0:T(8,128)}, f32[8,64,128]{2,1,0:T(8,128)}) custom-call(f32[688,128]{1,0:T(8,128)S(1)} %add.11.own_ref, f32[688,128]{1,0:T(8,128)S(1)} %collective-permute-done.14.other_ref), custom_call_target="tpu_custom_call" | custom-call | flops 1724999936 | tf_op jit(solution)/shard_map/pallas_call | solution.py:566
  (41 shorter events, 2.0 us)
Async XLA Ops:
  0.6 17.5 %copy-start.3 = (s32[8,512]{1,0:T(8,128)S(1)}, s32[8,512]{1,0:T(8,128)}, u32[]{:S(2)}) copy-start(s32[8,512]{1,0:T(8,128)} %mask_ref.3) | copy-start | bytes 49156
  0.6 17.5 %copy-start = (bf16[8,128,512]{2,1,0:T(8,128)(2,1)S(1)}, bf16[8,128,512]{2,1,0:T(8,128)(2,1)}, u32[]{:S(2)}) copy-start(bf16[8,128,512]{2,1,0:T(8,128)(2,1)} %feat_hbm.1) | copy-start | bytes 3145732
  0.7 12.7 %copy-start.5 = (s32[8,1]{0,1:T(1,128)S(1)}, s32[8,1]{0,1:T(1,128)}, u32[]{:S(2)}) copy-start(s32[8,1]{0,1:T(1,128)} %param.12) | copy-start | bytes 100
  0.7 17.5 %copy-start.2 = (bf16[27,32,128]{2,1,0:T(8,128)(2,1)S(1)}, bf16[27,32,128]{2,1,0:T(8,128)(2,1)}, u32[]{:S(2)}) copy-start(bf16[27,32,128]{2,1,0:T(8,128)(2,1)} %wconv_hbm.1) | copy-start | bytes 663556
  0.7 17.5 %copy-start.4 = (s32[8,26]{1,0:T(8,128)S(1)}, s32[8,26]{1,0:T(8,128)}, u32[]{:S(2)}) copy-start(s32[8,26]{1,0:T(8,128)} %nbr_hbm.1) | copy-start | bytes 2500
  2.7 10.7 %all-to-all-start = ((bf16[8,64,128]{2,1,0:T(8,128)(2,1)}), bf16[8,64,128]{2,1,0:T(8,128)(2,1)S(1)}, u32[]{:S(2)}, u32[]{:S(2)}) async-start(bf16[8,64,128]{2,1,0:T(8,128)(2,1)} %get-tuple-element.20), calls=%async_computation | async-start | bytes 262144 | tf_op jit(solution)/shard_map/all_to_all | solution.py:469
  7.8 10.3 %collective-permute-start = (bf16[2,128,128]{2,1,0:T(8,128)(2,1)}, bf16[2,128,128]{2,1,0:T(8,128)(2,1)S(1)}, u32[]{:S(2)}, u32[]{:S(2)}) collective-permute-start(bf16[2,128,128]{2,1,0:T(8,128)(2,1)} %get-tuple-element.22), channel_id=1, source_target_pairs={{0,4},{4,8},{8,12},{12,16},{16,20},{20,24},{24,28},{1,5},{5,9},{9,... | collective-permute-start | bytes 196616 | tf_op jit(solution)/shard_map/ppermute | solution.py:467
  10.3 7.9 %collective-permute-start.1 = (bf16[2,128,128]{2,1,0:T(8,128)(2,1)}, bf16[2,128,128]{2,1,0:T(8,128)(2,1)S(1)}, u32[]{:S(2)}, u32[]{:S(2)}) collective-permute-start(bf16[2,128,128]{2,1,0:T(8,128)(2,1)} %get-tuple-element.23), channel_id=1, source_target_pairs={{4,0},{8,4},{12,8},{16,12},{20,16},{24,20},{28,24},{5,1},{9,5},{13... | collective-permute-start | bytes 196616 | tf_op jit(solution)/shard_map/ppermute | solution.py:468
  13.7 13.2 %copy-start.1 = (bf16[8,256,128]{2,1,0:T(8,128)(2,1)S(1)}, bf16[8,256,128]{2,1,0:T(8,128)(2,1)}, u32[]{:S(2)}) copy-start(bf16[8,256,128]{2,1,0:T(8,128)(2,1)} %wdown_ref.3) | copy-start | bytes 1572868
  13.7 13.1 %collective-permute-start.4 = (bf16[64,512]{1,0:T(8,128)(2,1)S(1)}, bf16[64,512]{1,0:T(8,128)(2,1)S(1)}, u32[]{:S(2)}, u32[]{:S(2)}) collective-permute-start(bf16[64,512]{1,0:T(8,128)(2,1)S(1)} %get-tuple-element.25.refs_0_), channel_id=1, source_target_pairs={{0,3},{1,2},{2,1},{3,0},{4,7},{5,6},{6,5},{7,4},{8,11},{9,10},{10,... | collective-permute-start | bytes 196616 | tf_op jit(solution)/shard_map/ppermute | solution.py:429
  17.4 9.5 %collective-permute-start.3 = (bf16[64,512]{1,0:T(8,128)(2,1)S(1)}, bf16[64,512]{1,0:T(8,128)(2,1)S(1)}, u32[]{:S(2)}, u32[]{:S(2)}) collective-permute-start(bf16[64,512]{1,0:T(8,128)(2,1)S(1)} %get-tuple-element.25.refs_0_), channel_id=1, source_target_pairs={{0,2},{1,3},{2,0},{3,1},{4,6},{5,7},{6,4},{7,5},{8,10},{9,11},{10,... | collective-permute-start | bytes 196616 | tf_op jit(solution)/shard_map/ppermute | solution.py:429
  17.4 9.5 %collective-permute-start.2 = (bf16[64,512]{1,0:T(8,128)(2,1)S(1)}, bf16[64,512]{1,0:T(8,128)(2,1)S(1)}, u32[]{:S(2)}, u32[]{:S(2)}) collective-permute-start(bf16[64,512]{1,0:T(8,128)(2,1)S(1)} %get-tuple-element.25.refs_0_), channel_id=1, source_target_pairs={{0,1},{1,0},{2,3},{3,2},{4,5},{5,4},{6,7},{7,6},{8,9},{9,8},{10,11... | collective-permute-start | bytes 196616 | tf_op jit(solution)/shard_map/ppermute | solution.py:429
  27.6 9.6 %collective-permute-start.10 = (f32[2,64,128]{2,1,0:T(8,128)S(1)}, f32[2,64,128]{2,1,0:T(8,128)S(1)}, u32[]{:S(2)}, u32[]{:S(2)}) collective-permute-start(f32[2,64,128]{2,1,0:T(8,128)S(1)} %get-tuple-element.43), channel_id=1, source_target_pairs={{0,3},{1,2},{2,1},{3,0},{4,7},{5,6},{6,5},{7,4},{8,11},{9,10},{10,... | collective-permute-start | bytes 196616 | tf_op jit(solution)/shard_map/ppermute | solution.py:429
  31.3 5.9 %collective-permute-start.9 = (f32[2,64,128]{2,1,0:T(8,128)S(1)}, f32[2,64,128]{2,1,0:T(8,128)S(1)}, u32[]{:S(2)}, u32[]{:S(2)}) collective-permute-start(f32[2,64,128]{2,1,0:T(8,128)S(1)} %get-tuple-element.44), channel_id=1, source_target_pairs={{0,2},{1,3},{2,0},{3,1},{4,6},{5,7},{6,4},{7,5},{8,10},{9,11},{10,... | collective-permute-start | bytes 196616 | tf_op jit(solution)/shard_map/ppermute | solution.py:429
  31.3 4.6 %collective-permute-start.8 = (f32[2,64,128]{2,1,0:T(8,128)S(1)}, f32[2,64,128]{2,1,0:T(8,128)S(1)}, u32[]{:S(2)}, u32[]{:S(2)}) collective-permute-start(f32[2,64,128]{2,1,0:T(8,128)S(1)} %get-tuple-element.45), channel_id=1, source_target_pairs={{0,1},{1,0},{2,3},{3,2},{4,5},{5,4},{6,7},{7,6},{8,9},{9,8},{10,11... | collective-permute-start | bytes 196616 | tf_op jit(solution)/shard_map/ppermute | solution.py:429
  37.2 1.7 %collective-permute-start.11 = (f32[688,128]{1,0:T(8,128)S(1)}, f32[688,128]{1,0:T(8,128)S(1)}, u32[]{:S(2)}, u32[]{:S(2)}) collective-permute-start(f32[688,128]{1,0:T(8,128)S(1)} %get-tuple-element.48), channel_id=1, source_target_pairs={{0,4},{4,0},{8,12},{12,8},{16,20},{20,16},{24,28},{28,24},{1,5},{5... | collective-permute-start | bytes 1056776 | tf_op jit(solution)/shard_map/ppermute | solution.py:429
  39.0 10.3 %collective-permute-start.12 = (f32[688,128]{1,0:T(8,128)S(1)}, f32[688,128]{1,0:T(8,128)S(1)}, u32[]{:S(2)}, u32[]{:S(2)}) collective-permute-start(f32[688,128]{1,0:T(8,128)S(1)} %add.9), channel_id=1, source_target_pairs={{0,8},{4,12},{8,0},{12,4},{16,24},{20,28},{24,16},{28,20},{1,9},{5... | collective-permute-start | bytes 1056776 | tf_op jit(solution)/shard_map/ppermute | solution.py:429
  40.2 10.9 %collective-permute-start.7 = (f32[64,512]{1,0:T(8,128)S(1)}, f32[64,512]{1,0:T(8,128)S(1)}, u32[]{:S(2)}, u32[]{:S(2)}) collective-permute-start(f32[64,512]{1,0:T(8,128)S(1)} %get-tuple-element.37), channel_id=1, source_target_pairs={{0,3},{1,2},{2,1},{3,0},{4,7},{5,6},{6,5},{7,4},{8,11},{9,10},{10,... | collective-permute-start | bytes 393224 | tf_op jit(solution)/shard_map/ppermute | solution.py:429
  43.3 10.9 %collective-permute-start.6 = (f32[64,512]{1,0:T(8,128)S(1)}, f32[64,512]{1,0:T(8,128)S(1)}, u32[]{:S(2)}, u32[]{:S(2)}) collective-permute-start(f32[64,512]{1,0:T(8,128)S(1)} %get-tuple-element.38), channel_id=1, source_target_pairs={{0,2},{1,3},{2,0},{3,1},{4,6},{5,7},{6,4},{7,5},{8,10},{9,11},{10,... | collective-permute-start | bytes 393224 | tf_op jit(solution)/shard_map/ppermute | solution.py:429
  43.4 10.9 %collective-permute-start.5 = (f32[64,512]{1,0:T(8,128)S(1)}, f32[64,512]{1,0:T(8,128)S(1)}, u32[]{:S(2)}, u32[]{:S(2)}) collective-permute-start(f32[64,512]{1,0:T(8,128)S(1)} %get-tuple-element.39), channel_id=1, source_target_pairs={{0,1},{1,0},{2,3},{3,2},{4,5},{5,4},{6,7},{7,6},{8,9},{9,8},{10,11... | collective-permute-start | bytes 393224 | tf_op jit(solution)/shard_map/ppermute | solution.py:429
  49.3 9.5 %collective-permute-start.13 = (f32[688,128]{1,0:T(8,128)S(1)}, f32[688,128]{1,0:T(8,128)S(1)}, u32[]{:S(2)}, u32[]{:S(2)}) collective-permute-start(f32[688,128]{1,0:T(8,128)S(1)} %add.10), channel_id=1, source_target_pairs={{0,16},{4,20},{8,24},{12,28},{16,0},{20,4},{24,8},{28,12},{1,17},{... | collective-permute-start | bytes 1056776 | tf_op jit(solution)/shard_map/ppermute | solution.py:429
  55.1 8.8 %all-to-all-start.1 = ((bf16[8,64,128]{2,1,0:T(8,128)(2,1)}), bf16[8,64,128]{2,1,0:T(8,128)(2,1)S(1)}, u32[]{:S(2)}, u32[]{:S(2)}) async-start(bf16[8,64,128]{2,1,0:T(8,128)(2,1)} %shard_map.98), calls=%async_computation.1 | async-start | bytes 262144 | tf_op jit(solution)/shard_map/all_to_all | solution.py:555
  58.9 5.9 %collective-permute-start.14 = (f32[688,128]{1,0:T(8,128)S(1)}, f32[688,128]{1,0:T(8,128)S(1)}, u32[]{:S(2)}, u32[]{:S(2)}) collective-permute-start(f32[688,128]{1,0:T(8,128)S(1)} %add.11.own_ref), channel_id=1, source_target_pairs={{0,4},{4,0},{8,12},{12,8},{16,20},{20,16},{24,28},{28,24},{1,5},{5... | collective-permute-start | bytes 1056776 | tf_op jit(solution)/shard_map/ppermute | solution.py:429
